TPU v7x, 512 devices: a whole 4x8x8 slice. The times are simulated.
512 devices in a mesh: clip: 2 (over core), seq: 16 (over z_hi, x), mp: 16 (over z_lo, y).
Axes of the slice: x: 4, y: 8, z: 8 (z_hi: 4, z_lo: 2; z = z_hi * 2 + z_lo), core: 2. Of those that a mesh axis runs over, the one named last changes fastest.
Arguments:
- frames_in: bfloat16 [32, 256, 2048], P(('clip', 'seq'), None, 'mp'), parts along dimension 0, may hold values from -6 to 6
- norm_gain: bfloat16 [2048], replicated, may hold values from 0.5 to 1.5
- w_qkv: bfloat16 [2048, 6144], P(None, 'mp'), may hold values from -4 to 4
- w_out: bfloat16 [2048, 2048], P('mp'), may hold values from -0.125 to 0.125
- cotangent: bfloat16 [32, 256, 2048], P(('clip', 'seq'), None, 'mp'), parts along dimension 0, may hold values from -6 to 6
Outputs:
- layer_out: bfloat16 [32, 256, 2048], P(('clip', 'seq'), None, 'mp'), parts along dimension 0
- input_grad: bfloat16 [32, 256, 2048], P(('clip', 'seq'), None, 'mp'), parts along dimension 0
- qkv_weight_grad: bfloat16 [4096, 6144], P('clip', 'mp'), parts along dimension 0
- out_weight_grad: bfloat16 [4096, 2048], P(('clip', 'mp'), 'seq'), parts along dimension 0
There are 2 independent parts, one for each index of `clip`. A program takes and returns all parts, laid end to end along the dimension named above; an argument that names none is the same for every part. Nothing has to cross between parts.
All inputs are finite; a program needn't handle non-finite values.
Results may differ from a plain program's by a relative error of at most 0.028.
The roundings to bfloat16 on the way count: a program that leaves them out, or rounds other values in their place, can miss the bound.
Values may be sent and summed in bfloat16 or wider, within the bound.
A program may use at most 64 MiB of HBM per device.

v0:
```python
import jax
import jax.numpy as jnp
from jax import lax
from jax.sharding import PartitionSpec as P

HEAD = 128


EPS = 1e-05


def attend(queries, keys, values):
    scale = queries.shape[-1] ** (-0.5)
    scores = (
        jnp.einsum("fphe,gphe->phfg", queries, keys, preferred_element_type=jnp.float32) * scale
    )
    count = queries.shape[0]
    causal = jnp.arange(count)[:, None] >= jnp.arange(count)[None, :]
    scores = jnp.where(causal, scores, -1e30)
    peak = jnp.max(scores, axis=-1, keepdims=True)
    expo = jnp.exp(scores - peak)
    probs = (expo / jnp.sum(expo, axis=-1, keepdims=True)).astype(jnp.bfloat16)
    return jnp.einsum("phfg,gphe->fphe", probs, values, preferred_element_type=jnp.float32)


def shards(frames_in, norm_gain, w_qkv, w_out, cotangent):
    feat_local = frames_in.shape[2]
    width = norm_gain.shape[0]
    head_cols = w_out.shape[0]
    heads_here = head_cols // HEAD
    gathered = lax.all_gather(frames_in, "mp", axis=2, tiled=True)
    inputs_f32 = gathered.astype(jnp.float32)
    gain = norm_gain.astype(jnp.float32)
    inv_rms = lax.rsqrt(jnp.mean(inputs_f32 * inputs_f32, axis=-1, keepdims=True) + EPS)
    normed = (inputs_f32 * inv_rms * gain).astype(jnp.bfloat16)
    projected = jnp.einsum("abd,dc->abc", normed, w_qkv, preferred_element_type=jnp.float32).astype(
        jnp.bfloat16
    )
    projected = lax.all_to_all(projected, "seq", split_axis=1, concat_axis=0, tiled=True)
    frame_count, patch_count = (projected.shape[0], projected.shape[1])
    split = projected.reshape(frame_count, patch_count, heads_here, 3, HEAD)
    queries = split[:, :, :, 0]
    keys = split[:, :, :, 1]
    values = split[:, :, :, 2]
    attended = (
        attend(queries, keys, values)
        .astype(jnp.bfloat16)
        .reshape(frame_count, patch_count, head_cols)
    )
    attended_local = lax.all_to_all(attended, "seq", split_axis=0, concat_axis=1, tiled=True)
    term = jnp.einsum("abc,cd->abd", attended_local, w_out, preferred_element_type=jnp.float32)
    summed = lax.psum_scatter(
        term.astype(jnp.bfloat16), "mp", scatter_dimension=2, tiled=True
    ).astype(jnp.float32)
    local_f32 = frames_in.astype(jnp.float32)
    layer_out = (local_f32 + summed).astype(jnp.bfloat16)
    grad_whole = lax.all_gather(cotangent, "mp", axis=2, tiled=True)
    grad_heads = jnp.einsum(
        "abd,cd->abc", grad_whole, w_out, preferred_element_type=jnp.float32
    ).astype(jnp.bfloat16)
    out_weight_part = jnp.einsum(
        "abc,abd->cd", attended_local, grad_whole, preferred_element_type=jnp.float32
    )
    grad_heads = lax.all_to_all(grad_heads, "seq", split_axis=1, concat_axis=0, tiled=True)
    _, pull = jax.vjp(attend, queries, keys, values)
    grad_q, grad_k, grad_v = pull(
        grad_heads.reshape(frame_count, patch_count, heads_here, HEAD).astype(jnp.float32)
    )
    grad_proj = jnp.stack([grad_q, grad_k, grad_v], axis=3).reshape(
        frame_count, patch_count, 3 * head_cols
    )
    grad_proj = lax.all_to_all(grad_proj, "seq", split_axis=0, concat_axis=1, tiled=True)
    qkv_weight_part = jnp.einsum(
        "abd,abc->dc", normed, grad_proj, preferred_element_type=jnp.float32
    )
    normed_term = jnp.einsum("abc,dc->abd", grad_proj, w_qkv, preferred_element_type=jnp.float32)
    normed_grad = lax.psum_scatter(
        normed_term.astype(jnp.bfloat16), "mp", scatter_dimension=2, tiled=True
    ).astype(jnp.float32)
    gain_local = lax.dynamic_slice_in_dim(gain, lax.axis_index("mp") * feat_local, feat_local)
    row = lax.psum(jnp.sum(gain_local * normed_grad * local_f32, axis=-1, keepdims=True), "mp")
    input_grad = (
        cotangent.astype(jnp.float32)
        + inv_rms * gain_local * normed_grad
        - local_f32 * inv_rms**3 * row / width
    )
    input_grad = input_grad.astype(jnp.bfloat16)
    out_weight_grad = lax.psum_scatter(
        out_weight_part.astype(jnp.bfloat16), "seq", scatter_dimension=1, tiled=True
    )
    qkv_weight_grad = lax.psum(qkv_weight_part.astype(jnp.bfloat16), "seq")
    return (layer_out, input_grad, qkv_weight_grad, out_weight_grad)


def solution(mesh):
    return jax.shard_map(
        shards,
        mesh=mesh,
        in_specs=(
            P(("clip", "seq"), None, "mp"),
            P(),
            P(None, "mp"),
            P("mp", None),
            P(("clip", "seq"), None, "mp"),
        ),
        out_specs=(
            P(("clip", "seq"), None, "mp"),
            P(("clip", "seq"), None, "mp"),
            P("clip", "mp"),
            P(("clip", "mp"), "seq"),
        ),
        check_vma=False,
    )
```

profile of v0, /device:TPU:8, one launch (start us, length us, event | category | flops | bytes accessed | tf_op | source)
XLA Modules:
  0.0 584.8 jit_solution(3831165757135717225)
XLA Ops:
  7.2 0.7 all-gather.3.cloned.1.call-update
  8.0 0.7 all-gather.5.cloned.1.call-update
  8.7 0.7 convert_element_type.113
  9.4 72.5 %all-gather.3.cloned.1.call-done = bf16[1,256,2048]{2,1,0:T(8,128)(2,1)} async-done(((bf16[1,256,128]{2,1,0:T(8,128)(2,1)}), bf16[1,256,2048]{2,1,0:T(8,128)(2,1)}) %all-gather.3.cloned.1.call-update) | async-done | bytes 1048592 | tf_op jit(solution)/shard_map/all_gather | solution.py:31
  81.8 1.5 fusion.2
  83.4 0.5 multiply_multiply_fusion
  83.9 2.0 fusion.5
  85.9 0.3 copy.87
  86.2 0.5 broadcast.117
  86.7 1.7 reduce.15
  88.5 0.7 reshape.269
  89.2 9.8 %all-to-all-start = ((bf16[16,2,3072]{2,1,0:T(2,128)(2,1)}), bf16[16,2,3072]{2,1,0:T(2,128)(2,1)S(1)}, u32[]{:S(2)}, u32[]{:S(2)}) async-start(bf16[16,2,3072]{2,1,0:T(2,128)(2,1)} %reshape.269), calls=%async_computation | async-start | bytes 393216 | tf_op jit(solution)/shard_map/all_to_all | solution.py:39
  99.0 10.8 %all-to-all-done = bf16[16,2,3072]{2,1,0:T(2,128)(2,1)S(1)} async-done(((bf16[16,2,3072]{2,1,0:T(2,128)(2,1)}), bf16[16,2,3072]{2,1,0:T(2,128)(2,1)S(1)}, u32[]{:S(2)}, u32[]{:S(2)}) %all-to-all-start) | async-done | bytes 196640 | tf_op jit(solution)/shard_map/all_to_all | solution.py:39
  110.0 1.1 bitcast_reduce_fusion
  111.2 0.3 fusion.43
  111.5 0.2 fusion.44
  111.7 0.4 copy-done.6
  112.1 0.2 fusion.9
  112.4 0.7 copy.37
  113.0 3.8 all-to-all-start.1
  116.9 34.2 %all-gather.5.cloned.1.call-done = bf16[1,256,2048]{2,1,0:T(8,128)(2,1)} async-done(((bf16[1,256,128]{2,1,0:T(8,128)(2,1)}), bf16[1,256,2048]{2,1,0:T(8,128)(2,1)}) %all-gather.5.cloned.1.call-update) | async-done | bytes 1048592 | tf_op jit(solution)/shard_map/all_gather | solution.py:57
  151.1 2.4 convolution_convert_fusion.3
  153.6 2.1 copy.48
  155.7 0.4 fusion.8
  156.3 0.9 reduce.14
  157.2 0.7 reshape.271
  157.8 9.9 %all-to-all-start.2 = ((bf16[16,2,1024]{2,1,0:T(2,128)(2,1)}), bf16[16,2,1024]{2,1,0:T(2,128)(2,1)S(1)}, u32[]{:S(2)}, u32[]{:S(2)}) async-start(bf16[16,2,1024]{2,1,0:T(2,128)(2,1)} %reshape.271), calls=%async_computation.2 | async-start | bytes 131072 | tf_op jit(solution)/shard_map/all_to_all | solution.py:64
  167.8 0.4 fusion
  168.2 3.7 copy.44
  172.0 2.8 copy.86
  174.8 3.0 all-to-all-done.2
  178.2 0.2 fusion.10
  179.2 17.3 %all_to_all.16 = bf16[16,16,384]{2,1,0:T(8,128)(2,1)S(1)} all-to-all(bf16[16,16,384]{2,1,0:T(8,128)(2,1)S(1)} %reshape.257), channel_id=1, replica_groups=mesh['clip'=2,'seq'=16,'mp'=16] {'seq'}, dimensions={0} | all-to-all | bytes 393216 | tf_op jit(solution)/shard_map/all_to_all | solution.py:72
  196.5 0.7 fusion.1
  197.3 3.7 copy.46
  201.0 2.8 copy.85
  204.0 2.0 convolution_convert_fusion
  206.0 0.8 dynamic_slice.3
  206.8 41.1 %reduce-scatter.14.cloned.1.call-done = bf16[128,128]{1,0:T(8,128)(2,1)} async-done(((bf16[2048,128]{1,0:T(8,128)(2,1)}), bf16[128,128]{1,0:T(8,128)(2,1)}) %reduce-scatter.14.cloned.1.call-update) | async-done | bytes 32784
  247.9 1.5 copy.49
  249.3 70.5 %reduce-scatter.10.cloned.1.call-done = bf16[128,256]{1,0:T(8,128)(2,1)} async-done(((bf16[2048,256]{1,0:T(8,128)(2,1)}), bf16[128,256]{1,0:T(8,128)(2,1)}) %reduce-scatter.10.cloned.1.call-update) | async-done | bytes 65552
  319.8 0.9 reshape_bitcast_fusion.1
  320.9 71.9 %reduce-scatter.12.cloned.1.call-done = bf16[128,256]{1,0:T(8,128)(2,1)} async-done(((bf16[2048,256]{1,0:T(8,128)(2,1)}), bf16[128,256]{1,0:T(8,128)(2,1)}) %reduce-scatter.12.cloned.1.call-update) | async-done | bytes 65552
  392.7 0.9 reshape_bitcast_fusion
  393.9 33.4 %psum.14 = f32[256]{0:T(256)S(1)} all-reduce(f32[256]{0:T(256)S(1)} %fusion.24), channel_id=1, replica_groups=mesh['clip'=2,'seq'=16,'mp'=16] {'mp'}, use_global_device_ids=true, to_apply=%region_9.10 | all-reduce | flops 256 | bytes 2048 | tf_op jit(solution)/shard_map/psum | solution.py:81
  427.3 0.8 fusion.20
  428.2 147.1 %all-reduce.2.cloned.1.call-done = bf16[2048,384]{1,0:T(8,128)(2,1)} async-done(((bf16[2048,384]{1,0:T(8,128)(2,1)}), bf16[2048,384]{1,0:T(8,128)(2,1)}) %all-reduce.2.cloned.1.call-update) | async-done | bytes 1572880 | tf_op jit(solution)/shard_map/psum | solution.py:91
  575.3 2.7 copy.90
  (64 shorter events, 2.2 us)
Async XLA Ops:
  7.2 76.7 %copy-start = (bf16[2048,384]{1,0:T(8,128)(2,1)S(1)}, bf16[2048,384]{1,0:T(8,128)(2,1)}, u32[]{:S(2)}) copy-start(bf16[2048,384]{1,0:T(8,128)(2,1)} %param.7) | copy-start | bytes 4718596
  7.2 74.7 %all-gather.3.cloned.1.call-start = ((), (), s32[]{:S(2)}) async-start(), calls=%async_computation.7 | async-start | bytes 1114112 | tf_op jit(solution)/shard_map/all_gather | solution.py:31
  7.9 143.2 %all-gather.5.cloned.1.call-start = ((), (), s32[]{:S(2)}) async-start(), calls=%async_computation.8 | async-start | bytes 1114112 | tf_op jit(solution)/shard_map/all_gather | solution.py:57
  9.4 74.5 %copy-start.10 = (f32[2048]{0:T(1024)}, f32[2048]{0:T(1024)S(1)}, u32[]{:S(2)}) copy-start(f32[2048]{0:T(1024)S(1)} %convert_element_type.113) | copy-start | bytes 24580
  83.9 2.3 copy-start.13
  89.2 20.6 %all-to-all-start = ((bf16[16,2,3072]{2,1,0:T(2,128)(2,1)}), bf16[16,2,3072]{2,1,0:T(2,128)(2,1)S(1)}, u32[]{:S(2)}, u32[]{:S(2)}) async-start(bf16[16,2,3072]{2,1,0:T(2,128)(2,1)} %reshape.269), calls=%async_computation | async-start | bytes 393216 | tf_op jit(solution)/shard_map/all_to_all | solution.py:39
  99.0 12.7 %copy-start.15 = (pred[16,16]{0,1:T(8,128)(4,1)}, pred[16,16]{0,1:T(8,128)(4,1)S(1)}, u32[]{:S(2)}) copy-start(pred[16,16]{0,1:T(8,128)(4,1)S(1)} %iota_compare_fusion) | copy-start | bytes 772
  111.4 0.6 copy-start.6
  111.4 5.5 copy-start.8
  112.1 43.6 %copy-start.2 = (bf16[128,2048]{1,0:T(8,128)(2,1)S(1)}, bf16[128,2048]{1,0:T(8,128)(2,1)}, u32[]{:S(2)}) copy-start(bf16[128,2048]{1,0:T(8,128)(2,1)} %param.8) | copy-start | bytes 1572868
  113.0 38.1 %all-to-all-start.1 = ((bf16[16,16,128]{2,1,0:T(8,128)(2,1)}), bf16[16,16,128]{2,1,0:T(8,128)(2,1)S(1)}, u32[]{:S(2)}, u32[]{:S(2)}) async-start(bf16[16,16,128]{2,1,0:T(8,128)(2,1)} %copy.37), calls=%async_computation.1 | async-start | bytes 131072 | tf_op jit(solution)/shard_map/all_to_all | solution.py:50
  116.9 131.0 %reduce-scatter.14.cloned.1.call-start = ((), (), s32[]{:S(2)}) async-start(), calls=%async_computation.12 | async-start | bytes 557056
  151.1 4.6 copy-start.1
  157.8 20.0 %all-to-all-start.2 = ((bf16[16,2,1024]{2,1,0:T(2,128)(2,1)}), bf16[16,2,1024]{2,1,0:T(2,128)(2,1)S(1)}, u32[]{:S(2)}, u32[]{:S(2)}) async-start(bf16[16,2,1024]{2,1,0:T(2,128)(2,1)} %reshape.271), calls=%async_computation.2 | async-start | bytes 131072 | tf_op jit(solution)/shard_map/all_to_all | solution.py:64
  167.7 152.1 %reduce-scatter.10.cloned.1.call-start = ((), (), s32[]{:S(2)}) async-start(), calls=%async_computation.10 | async-start | bytes 1114112
  172.0 6.0 %copy-start.9 = (bf16[16,16,1,1,128]{4,3,1,0,2:T(2,128)(2,1)S(1)}, bf16[16,16,1,1,128]{4,3,1,0,2:T(2,128)(2,1)}, u32[]{:S(2)}) copy-start(bf16[16,16,1,1,128]{4,3,1,0,2:T(2,128)(2,1)} %copy-done.8) | copy-start | bytes 196612
  172.0 6.3 %copy-start.7 = (bf16[16,16,1,1,128]{4,3,1,0,2:T(2,128)(2,1)S(1)}, bf16[16,16,1,1,128]{4,3,1,0,2:T(2,128)(2,1)}, u32[]{:S(2)}) copy-start(bf16[16,16,1,1,128]{4,3,1,0,2:T(2,128)(2,1)} %copy-done.6) | copy-start | bytes 196612
  172.0 6.3 %copy-start.16 = (pred[16,16]{0,1:T(8,128)(4,1)S(1)}, pred[16,16]{0,1:T(8,128)(4,1)}, u32[]{:S(2)}) copy-start(pred[16,16]{0,1:T(8,128)(4,1)} %copy-done.15) | copy-start | bytes 772
  174.8 218.0 %reduce-scatter.12.cloned.1.call-start = ((), (), s32[]{:S(2)}) async-start(), calls=%async_computation.11 | async-start | bytes 1114112
  201.0 2.9 copy-start.3
  201.0 2.9 copy-start.11
  201.0 3.0 copy-start.14
  203.9 189.9 %copy-start.4 = (bf16[1,256,128]{2,1,0:T(8,128)(2,1)S(1)}, bf16[1,256,128]{2,1,0:T(8,128)(2,1)}, u32[]{:S(2)}) copy-start(bf16[1,256,128]{2,1,0:T(8,128)(2,1)} %param.5) | copy-start | bytes 196612
  203.9 371.4 %all-reduce.2.cloned.1.call-start = ((), (), s32[]{:S(2)}) async-start(), calls=%async_computation.9 | async-start | bytes 3145728 | tf_op jit(solution)/shard_map/psum | solution.py:91
  206.0 221.4 %copy-start.5 = (bf16[1,256,128]{2,1,0:T(8,128)(2,1)S(1)}, bf16[1,256,128]{2,1,0:T(8,128)(2,1)}, u32[]{:S(2)}) copy-start(bf16[1,256,128]{2,1,0:T(8,128)(2,1)} %param.9) | copy-start | bytes 196612
  206.0 221.4 %copy-start.12 = (f32[256]{0:T(256)S(1)}, f32[256]{0:T(256)}, u32[]{:S(2)}) copy-start(f32[256]{0:T(256)} %get-tuple-element.14) | copy-start | bytes 3076
Sparse Core Ops, SparseCore 0:
  10.0 71.7 all-gather.2
  83.8 67.2 all-gather.4
  155.8 92.0 reduce-scatter.13
  250.8 69.0 reduce-scatter.9
  322.5 70.2 reduce-scatter.11
  396.4 178.8 all-reduce.1
where the time goes:
time: 586 us; the launch traced here: 585 us
  waiting for transfers between devices  453 us (77%)
  blocking collectives  50.7 us (9%)
  local copies, waits for them, and re-layouts  27.6 us (5%)
  starting transfers between devices  23.8 us (4%)
  between operations  14.5 us (2%)
  matrix products  9.21 us (2%)
  other arithmetic  6.47 us (1%)
    unnamed x9, waiting for transfers between devices  185 us
    psum x1, waiting for transfers between devices, shards(): qkv_weight_grad = lax.psum(qkv_weight_part.astype(jnp.bfloat16), 'seq')  147 us
    all_gather x1, waiting for transfers between devices, shards(): gathered = lax.all_gather(frames_in, 'mp', axis=2, tiled=True)  72.5 us
    all_gather x1, waiting for transfers between devices, shards(): grad_whole = lax.all_gather(cotangent, 'mp', axis=2, tiled=True)  34.2 us
    psum x1, blocking collectives, shards(): lax.psum(jnp.sum(gain_local * normed_grad * local_f32, axis=-1, keepdims=...  33.4 us
    unnamed x51, local copies, waits for them, and re-layouts  24 us
    all_to_all x1, blocking collectives, shards(): lax.all_to_all(grad_proj, 'seq', split_axis=0, concat_axis=1, tiled=True)  17.3 us
  transfers between devices with their start and end apart: 9, of which 8 were waited for; matrix products, arithmetic and copies ran while one was open for 6% of the time, Pallas kernels for 0%

commit v1 on v0

v1 whole, which is shorter than its diff:
```python
import jax
import jax.numpy as jnp
from jax import lax
from jax.experimental import pallas as pl
from jax.experimental.pallas import tpu as pltpu
from jax.sharding import PartitionSpec as P

HEAD = 128
EPS = 1e-05
BF = jnp.bfloat16
F32 = jnp.float32
MESH = pl.DeviceIdType.MESH
COPIES = 200
NT = (((1,), (1,)), ((), ()))


def mm(a, b):
    return jnp.dot(a, b, preferred_element_type=F32)


def mm_nt(a, b):
    return lax.dot_general(a, b, NT, preferred_element_type=F32)


def flat(block):
    return block.reshape(256, HEAD)


def kernel(
    x_hbm, gain_hbm, wqkv_hbm, wout_hbm, g_hbm,
    lo_hbm, ig_hbm, dwqkv_hbm, dwo_hbm,
    x_ref, g_ref, gain_ref, a1x, a1g, xb, gb, wqkv, wout, gain, inv, norm, norm_t, qkv, att, att_t,
    probs, probs_t, gheads, dqkv, term1, term2, rb1, rb2, zs1, zb1, zs2, zb2, rowb,
    wg, tx, px, mx, sx, rz, res, dwo, los, igs, b1l, b1i, lod, igd,
    ssem, rsem, lsem,
):
    clip, seq, mp = lax.axis_index("clip"), lax.axis_index("seq"), lax.axis_index("mp")
    zh, x = lax.div(seq, 4), lax.rem(seq, 4)
    zl, y = lax.div(mp, 8), lax.rem(mp, 8)
    e = 1 - 2 * clip
    zp = 1 - zl

    def x_at(step):
        return lax.rem(x + step + 4, 4)

    def z_at(step):
        return lax.rem(zh + step + 4, 4)

    def y_at(step):
        return lax.rem(y + step + 8, 8)

    def dev_x(to):
        return (clip, zh * 4 + to, mp)

    def dev_z(to):
        return (clip, to * 4 + x, mp)

    def dev_y(to):
        return (clip, seq, zl * 8 + to)

    dev_pair = (clip, seq, zp * 8 + y)

    loads = [
        pltpu.make_async_copy(src, dst, lsem.at[at])
        for at, (src, dst) in enumerate(
            [(x_hbm, x_ref), (g_hbm, g_ref), (gain_hbm, gain_ref), (wqkv_hbm, wqkv), (wout_hbm, wout)]
        )
    ]
    for load in loads:
        load.start()

    barrier = pltpu.get_barrier_semaphore()
    peers = [dev_x(x_at(s)) for s in (1, 2, 3)] + [dev_z(z_at(s)) for s in (1, 2, 3)]
    peers += [dev_y(y_at(1)), dev_y(y_at(-1)), dev_pair]
    for peer in peers:
        pl.semaphore_signal(barrier, inc=1, device_id=peer, device_id_type=MESH)
    pl.semaphore_wait(barrier, len(peers))

    started = []

    def send(src, dst, device):
        at = len(started)
        copy = pltpu.make_async_remote_copy(
            src_ref=src,
            dst_ref=dst,
            send_sem=ssem.at[at],
            recv_sem=rsem.at[at],
            device_id=device,
            device_id_type=MESH,
        )
        copy.start()
        started.append(copy)
        return copy

    stores = []

    def store(src, dst):
        stores.append(pltpu.make_async_copy(src, dst, lsem.at[len(loads) + len(stores)]))
        stores[-1].start()

    def frames_to_patches(src, mid, dst):
        sent = [send(src.at[:, x_at(s)], mid.at[x], dev_x(x_at(s))) for s in (1, 3, 2)]
        mid[x] = src[:, x]
        yield 2.0
        for copy in sent:
            copy.wait_recv()
        sent = [send(mid.at[:, z_at(s)], dst.at[mp, zh], dev_z(z_at(s))) for s in (1, 3, 2)]
        dst[mp, zh] = mid[:, zh]
        yield 2.0
        for copy in sent:
            copy.wait_recv()

    def patches_to_frames(src, mid, dst):
        sent = [send(src.at[z_at(s)], mid.at[zh], dev_z(z_at(s))) for s in (1, 3, 2)]
        mid[zh] = src[zh]
        yield 2.0
        for copy in sent:
            copy.wait_recv()
        sent = [send(mid.at[:, x_at(s)], dst.at[:, x], dev_x(x_at(s))) for s in (1, 3, 2)]
        dst[:, x] = mid[:, x]
        yield 2.0
        for copy in sent:
            copy.wait_recv()

    def gather(buf):
        def pass_on(block, device):
            return send(buf.at[block], buf.at[block], device)

        ahead, back = dev_y(y_at(e)), dev_y(y_at(-e))

        def own(step):
            return zl * 8 + y_at(step)

        def other(step):
            return zp * 8 + y_at(step)

        a = pass_on(mp, ahead)
        b = pass_on(mp, back)
        pair = [pass_on(mp, dev_pair)]
        yield 2.0
        a.wait_recv()
        a = pass_on(own(-e), ahead)
        yield 0.1
        b.wait_recv()
        b = pass_on(own(e), back)
        yield 0.5
        pair[0].wait_recv()
        c = pass_on(other(0), ahead)
        d = pass_on(other(0), back)
        yield 1.0
        a.wait_recv()
        a = pass_on(own(-2 * e), ahead)
        yield 0.1
        b.wait_recv()
        b = pass_on(own(2 * e), back)
        pair.append(pass_on(own(2 * e), dev_pair))
        yield 1.0
        c.wait_recv()
        c = pass_on(other(-e), ahead)
        yield 0.1
        d.wait_recv()
        yield 1.0
        a.wait_recv()
        a = pass_on(own(-3 * e), ahead)
        pair.append(pass_on(own(-3 * e), dev_pair))
        yield 0.1
        b.wait_recv()
        pair.append(pass_on(own(3 * e), dev_pair))
        yield 0.5
        c.wait_recv()
        yield 1.0
        a.wait_recv()
        pair.append(pass_on(own(-4 * e), dev_pair))
        for copy in pair[1:]:
            yield 0.5
            copy.wait_recv()

    def scatter_sum(term, rb, zs, zb):
        def slot(i, j, k):
            return i * 7 + j * 4 + k - 1

        planes = (zp, zl)
        ways = ((e, 4), (-e, 3))
        order = [(i, j) for i in (0, 1) for j in (0, 1)]
        sent = {}
        for i, j in order:
            way, steps = ways[j]
            dest = planes[i] * 8 + y_at(steps * way)
            sent[i, j] = send(term.at[dest], rb.at[slot(i, j, 1)], dev_y(y_at(way)))
        last = None
        for k in (1, 2, 3, 4):
            for i, j in order:
                way, steps = ways[j]
                if k > steps:
                    continue
                yield 2.2 if (i, j) == (0, 0) else 0.5
                sent[i, j].wait_recv()
                if k < steps:
                    dest = planes[i] * 8 + y_at((steps - k) * way)
                    here = rb.at[slot(i, j, k)]
                    here[...] = (here[...].astype(F32) + term[dest].astype(F32)).astype(BF)
                    sent[i, j] = send(here, rb.at[slot(i, j, k + 1)], dev_y(y_at(way)))
                elif k == 4 and i == 0:
                    zs[...] = (
                        term[zp * 8 + y].astype(F32)
                        + rb[slot(0, 0, 4)].astype(F32)
                        + rb[slot(0, 1, 3)].astype(F32)
                    ).astype(BF)
                    last = send(zs, zb, dev_pair)
        yield 2.0
        last.wait_recv()

    def summed(term, rb, zb):
        return (
            term[mp].astype(F32)
            + rb[7 + 3].astype(F32)
            + rb[7 + 4 + 2].astype(F32)
            + zb[...].astype(F32)
        )

    def weight_sum(c, gathered):
        xp, xm = x_at(e), x_at(-e)
        ahead, back = dev_x(xp), dev_x(xm)
        order = (2, 1, 3, 0)
        far = {}
        for r in order:
            far[r] = send(wg.at[c, z_at(r), x_at(2)], tx.at[c, z_at(r)], ahead)
        plain = send(wg.at[c, :, xm], px.at[c], back)
        near = {}
        for r in order:
            yield 3.0 if r == 2 else 0.7
            q = z_at(r)
            far[r].wait_recv()
            tx[c, q] = (tx[c, q].astype(F32) + wg[c, q, xp].astype(F32)).astype(BF)
            near[r] = send(tx.at[c, q], mx.at[c, q], ahead)
        across = []
        yield 1.0
        plain.wait_recv()
        for r in order[:3]:
            yield 0.7
            q = z_at(r)
            near[r].wait_recv()
            sx[c, q] = (
                wg[c, q, x].astype(F32) + px[c, q].astype(F32) + mx[c, q].astype(F32)
            ).astype(BF)
            across.append(send(sx.at[c, q], rz.at[c, r - 1], dev_z(q)))
        yield 0.7
        near[0].wait_recv()
        total = wg[c, zh, x].astype(F32) + px[c, zh].astype(F32) + mx[c, zh].astype(F32)
        yield 2.0
        for copy in across:
            copy.wait_recv()
        for r in range(3):
            total += rz[c, r].astype(F32)
        if not gathered:
            dwo[...] = total.astype(BF)
            store(dwo, dwo_hbm)
            return
        res[c, zh, x] = total.astype(BF)

        def pass_on(q, column, device):
            return send(res.at[c, q, column], res.at[c, q, column], device)

        zm = z_at(-e)
        up = pass_on(zh, x, dev_z(z_at(e)))
        down = pass_on(zh, x, dev_z(zm))
        first, second = [pass_on(zh, x, ahead)], [pass_on(zh, x, back)]
        third = []
        yield 2.5
        up.wait_recv()
        up = pass_on(zm, x, dev_z(z_at(e)))
        first.append(pass_on(zm, x, ahead))
        second.append(pass_on(zm, x, back))
        yield 0.2
        down.wait_recv()
        first.append(pass_on(z_at(e), x, ahead))
        second.append(pass_on(z_at(e), x, back))
        yield 0.3
        first[0].wait_recv()
        third.append(pass_on(zh, xm, ahead))
        yield 2.0
        up.wait_recv()
        first.append(pass_on(z_at(2), x, ahead))
        second.append(pass_on(z_at(2), x, back))
        for at, q in ((1, zm), (2, z_at(e)), (3, z_at(2))):
            yield 0.7
            first[at].wait_recv()
            third.append(pass_on(q, xm, ahead))
        yield 2.5
        for copy in second + third:
            copy.wait_recv()
        store(res.at[c], dwqkv_hbm.at[:, :, :, pl.ds(c * 128, 128)])

    flows = []
    clock = [0.0]

    def start(flow):
        flows.append([clock[0] + next(flow), flow])
        return flow

    def step(item):
        clock[0] = max(clock[0], item[0])
        wait = next(item[1], None)
        if wait is None:
            flows.remove(item)
        else:
            item[0] = clock[0] + wait

    def finish(flow):
        while any(item[1] is flow for item in flows):
            step(min(flows, key=lambda item: item[0]))

    def passed(time):
        target = clock[0] + time
        while flows and min(item[0] for item in flows) <= target:
            step(min(flows, key=lambda item: item[0]))
        clock[0] = target

    loads[0].wait()
    flow_x = start(frames_to_patches(x_ref, a1x, xb))
    loads[1].wait()
    flow_g = start(frames_to_patches(g_ref, a1g, gb))
    loads[2].wait()
    gain[...] = gain_ref[...].astype(F32)
    finish(flow_x)
    gather_x = start(gather(xb))
    finish(flow_g)
    gather_g = start(gather(gb))
    finish(gather_x)

    def square(m, total):
        block = flat(xb[m]).astype(F32)
        return total + block * block

    squares = lax.fori_loop(0, 16, square, jnp.zeros((256, HEAD), F32))
    mean = jnp.sum(squares, axis=-1, keepdims=True) * (1.0 / 2048)
    inv[...] = jnp.broadcast_to(lax.rsqrt(mean + EPS), (256, HEAD))

    def normalise(m, carry):
        block = flat(xb[m]).astype(F32) * inv[...] * gain[pl.ds(m, 1), :]
        norm[:, pl.ds(pl.multiple_of(m * 128, 128), 128)] = block.astype(BF)
        return carry

    lax.fori_loop(0, 16, normalise, 0, unroll=2)
    passed(1.5)
    for load in loads[3:]:
        load.wait()
    qkv[...] = mm(norm[...], wqkv[...]).astype(BF)
    passed(1.0)

    scale = HEAD ** (-0.5)
    rows = lax.broadcasted_iota(jnp.int32, (256, 256), 0)
    cols = lax.broadcasted_iota(jnp.int32, (256, 256), 1)
    keep = (((rows - cols) & 15) == 0) & (cols <= rows)
    queries, keys, values = (qkv[:, pl.ds(i * 128, 128)] for i in range(3))
    scores = jnp.where(keep, mm_nt(queries, keys) * scale, -1e30)
    expo = jnp.exp(scores - jnp.max(scores, axis=-1, keepdims=True))
    soft = expo / jnp.sum(expo, axis=-1, keepdims=True)
    probs[...] = soft
    attended = mm(soft.astype(BF), values)
    att[...] = attended.astype(BF)
    passed(1.5)

    def out_term(i, carry):
        wide = mm(att[...], wout[:, pl.ds(pl.multiple_of(i * 256, 256), 256)]).astype(BF)
        term1[2 * i] = wide[:, :128]
        term1[2 * i + 1] = wide[:, 128:]
        return carry

    lax.fori_loop(0, 8, out_term, 0, unroll=4)
    passed(1.0)

    def layer_flow():
        yield from scatter_sum(term1, rb1, zs1, zb1)
        los[...] = (flat(xb[mp]).astype(F32) + summed(term1, rb1, zb1)).astype(BF).reshape(
            4, 4, 16, HEAD
        )
        yield 0.1
        yield from patches_to_frames(los, b1l, lod)
        store(lod, lo_hbm)

    start(layer_flow())
    att_t[...] = jnp.transpose(attended).astype(BF)
    probs_t[...] = jnp.transpose(soft).astype(BF)

    def turn(m, carry):
        at = pl.multiple_of(m * 128, 128)
        block = norm[:, pl.ds(at, 128)].astype(F32)
        norm_t[pl.ds(at, 128), :] = jnp.transpose(block).astype(BF)
        return carry

    lax.fori_loop(0, 16, turn, 0, unroll=2)
    finish(gather_g)

    def pair_of(i):
        return jnp.concatenate([flat(gb[2 * i]), flat(gb[2 * i + 1])], axis=1)

    total = jnp.zeros((256, HEAD), F32)
    for i in range(8):
        total += mm_nt(pair_of(i), wout[:, pl.ds(i * 256, 256)])
    gheads[...] = total.astype(BF)

    def out_weight(i, carry):
        wide = mm(att_t[...], pair_of(i)).astype(BF)
        wg[3, lax.div(i, 2), 2 * lax.rem(i, 2)] = wide[:, :128]
        wg[3, lax.div(i, 2), 2 * lax.rem(i, 2) + 1] = wide[:, 128:]
        return carry

    def in_weight(c):
        grad = dqkv[:, pl.ds(c * 128, 128)]

        def body(i, carry):
            tall = mm(norm_t[pl.ds(pl.multiple_of(i * 256, 256), 256), :], grad).astype(BF)
            wg[c, lax.div(i, 2), 2 * lax.rem(i, 2)] = tall[:128]
            wg[c, lax.div(i, 2), 2 * lax.rem(i, 2) + 1] = tall[128:]
            return carry

        lax.fori_loop(0, 8, body, 0, unroll=4)
        start(weight_sum(c, True))
        passed(1.5)

    dqkv[:, pl.ds(256, 128)] = mm(probs_t[...], gheads[...]).astype(BF)
    in_weight(2)
    dprobs = mm_nt(gheads[...], qkv[:, pl.ds(256, 128)]).astype(BF).astype(F32)
    soft = probs[...]
    delta = jnp.sum(soft * dprobs, axis=-1, keepdims=True)
    dscores = soft * (dprobs - delta) * scale
    high = dscores.astype(BF)
    low = (dscores - high.astype(F32)).astype(BF)
    keys = qkv[:, pl.ds(128, 128)]
    dqkv[:, pl.ds(0, 128)] = (mm(high, keys) + mm(low, keys)).astype(BF)
    in_weight(0)
    turned = jnp.transpose(dscores)
    high = turned.astype(BF)
    low = (turned - high.astype(F32)).astype(BF)
    queries = qkv[:, pl.ds(0, 128)]
    dqkv[:, pl.ds(128, 128)] = (mm(high, queries) + mm(low, queries)).astype(BF)
    in_weight(1)
    lax.fori_loop(0, 8, out_weight, 0, unroll=4)
    start(weight_sum(3, False))
    passed(1.5)

    def norm_term(i, total):
        tall = wqkv[pl.ds(pl.multiple_of(i * 256, 256), 256), :]
        wide = mm_nt(dqkv[...], tall).astype(BF)
        for half in (0, 1):
            part = wide[:, half * 128 : half * 128 + 128]
            term2[2 * i + half] = part
            total += gain[pl.ds(2 * i + half, 1), :] * part.astype(F32) * flat(
                xb[2 * i + half]
            ).astype(F32)
        return total

    inner = lax.fori_loop(0, 8, norm_term, jnp.zeros((256, HEAD), F32), unroll=2)
    rowb[mp] = jnp.broadcast_to(jnp.sum(jnp.transpose(inner), axis=0, keepdims=True), (8, 256))
    rows_flow = gather(rowb)

    def input_flow():
        yield from scatter_sum(term2, rb2, zs2, zb2)
        yield from rows_flow
        row = jnp.sum(rowb[...].reshape(16, 8, 256), axis=0)[:1]
        row = jnp.transpose(jnp.broadcast_to(row, (HEAD, 256)))
        grad = summed(term2, rb2, zb2)
        scale_own = inv[...]
        out = (
            flat(gb[mp]).astype(F32)
            + scale_own * gain[pl.ds(mp, 1), :] * grad
            - flat(xb[mp]).astype(F32) * (scale_own * scale_own * scale_own) * row * (1.0 / 2048)
        )
        igs[...] = out.astype(BF).reshape(4, 4, 16, HEAD)
        yield 0.1
        yield from patches_to_frames(igs, b1i, igd)
        store(igd, ig_hbm)

    start(input_flow())
    while flows:
        step(min(flows, key=lambda item: item[0]))

    for copy in started:
        copy.wait_send()
    for copy in stores:
        copy.wait()


def shards(frames_in, norm_gain, w_qkv, w_out, cotangent):
    hbm = pl.BlockSpec(memory_space=pltpu.HBM)

    def bf(*shape):
        return pltpu.VMEM(shape, BF)

    def f32(*shape):
        return pltpu.VMEM(shape, F32)

    scratch = [
        bf(4, 4, 16, HEAD), bf(4, 4, 16, HEAD), bf(16, HEAD),
        bf(4, 4, 16, HEAD), bf(4, 4, 16, HEAD),
        bf(16, 4, 4, 16, HEAD), bf(16, 4, 4, 16, HEAD),
        bf(2048, 384), bf(HEAD, 2048),
        f32(16, HEAD), f32(256, HEAD),
        bf(256, 2048), bf(2048, 256),
        bf(256, 384), bf(256, HEAD), bf(HEAD, 256),
        f32(256, 256), bf(256, 256),
        bf(256, HEAD), bf(256, 384),
        bf(16, 256, HEAD), bf(16, 256, HEAD),
        bf(14, 256, HEAD), bf(14, 256, HEAD),
        bf(256, HEAD), bf(256, HEAD), bf(256, HEAD), bf(256, HEAD),
        f32(16, 8, 256),
        bf(4, 4, 4, HEAD, HEAD),
        bf(4, 4, HEAD, HEAD), bf(4, 4, HEAD, HEAD),
        bf(4, 4, HEAD, HEAD), bf(4, 4, HEAD, HEAD),
        bf(4, 3, HEAD, HEAD),
        bf(3, 4, 4, HEAD, HEAD), bf(HEAD, HEAD),
        bf(4, 4, 16, HEAD), bf(4, 4, 16, HEAD), bf(4, 4, 16, HEAD),
        bf(4, 4, 16, HEAD), bf(4, 4, 16, HEAD), bf(4, 4, 16, HEAD),
        pltpu.SemaphoreType.DMA((COPIES,)),
        pltpu.SemaphoreType.DMA((COPIES,)),
        pltpu.SemaphoreType.DMA((11,)),
    ]
    layer_out, input_grad, qkv_weight_grad, out_weight_grad = pl.pallas_call(
        kernel,
        out_shape=(
            jax.ShapeDtypeStruct((4, 4, 16, HEAD), BF),
            jax.ShapeDtypeStruct((4, 4, 16, HEAD), BF),
            jax.ShapeDtypeStruct((4, 4, HEAD, 384), BF),
            jax.ShapeDtypeStruct((HEAD, HEAD), BF),
        ),
        in_specs=[hbm] * 5,
        out_specs=(hbm, hbm, hbm, hbm),
        scratch_shapes=scratch,
        compiler_params=pltpu.CompilerParams(
            collective_id=0, has_side_effects=True, vmem_limit_bytes=60 * 1024 * 1024
        ),
        name="sublayer",
    )(
        frames_in.reshape(4, 4, 16, HEAD),
        norm_gain.reshape(16, HEAD),
        w_qkv,
        w_out,
        cotangent.reshape(4, 4, 16, HEAD),
    )
    return (
        layer_out.reshape(1, 256, HEAD),
        input_grad.reshape(1, 256, HEAD),
        qkv_weight_grad.reshape(2048, 384),
        out_weight_grad,
    )


def solution(mesh):
    return jax.shard_map(
        shards,
        mesh=mesh,
        in_specs=(
            P(("clip", "seq"), None, "mp"),
            P(),
            P(None, "mp"),
            P("mp", None),
            P(("clip", "seq"), None, "mp"),
        ),
        out_specs=(
            P(("clip", "seq"), None, "mp"),
            P(("clip", "seq"), None, "mp"),
            P("clip", "mp"),
            P(("clip", "mp"), "seq"),
        ),
        check_vma=False,
    )
```

time: 586 us -> 120 us (0.20)
  waiting for transfers between devices: 453 us -> 0 us
  Pallas kernels: 0 us -> 113 us
  blocking collectives: 50.7 us -> 0 us
  starting transfers between devices: 23.8 us -> 0 us
  local copies, waits for them, and re-layouts: 27.6 us -> 6.28 us
  between operations: 14.5 us -> 0.64 us
  matrix products: 9.21 us -> 0 us
  other arithmetic: 6.47 us -> 0 us
    unnamed x9 -> x0, waiting for transfers between devices: 185 us -> none
    psum x1 -> x0, waiting for transfers between devices: 147 us -> none  [shards(): qkv_weight_grad = lax.psum(qkv_weight_part.astype(jnp.bfloat16), 'seq')]
    pallas_call x0 -> x1, Pallas kernels: none -> 113 us  [shards(): pl.pallas_call(kernel, out_shape=(jax.ShapeDtypeStruct((4, 4, 16, HEAD),...]
    all_gather x2 -> x0, waiting for transfers between devices: 107 us -> none  [the longest x1 72.5 us: shards(): gathered = lax.all_gather(frames_in, 'mp', axis=2, tiled=True)]
    psum x1 -> x0, blocking collectives: 33.4 us -> none  [shards(): lax.psum(jnp.sum(gain_local * normed_grad * local_f32, axis=-1, keepdims=...]
    all_to_all x3 -> x0, starting transfers between devices: 23.5 us -> none  [the longest x1 9.88 us: shards(): lax.all_to_all(grad_heads, 'seq', split_axis=1, concat_axis=0, tiled=True)]
    unnamed x51 -> x6, local copies, waits for them, and re-layouts: 24 us -> 6.28 us
    all_to_all x1 -> x0, blocking collectives: 17.3 us -> none  [shards(): lax.all_to_all(grad_proj, 'seq', split_axis=0, concat_axis=1, tiled=True)]
  transfers between devices with their start and end apart: 9 -> 0, of which waited for: 8 -> 0; matrix products, arithmetic and copies ran while one was open for 6% -> 0% of each run, Pallas kernels for 0% -> 0%
where the time goes in v1:
time: 120 us
  Pallas kernels  113 us (94%)
  local copies, waits for them, and re-layouts  6.28 us (5%)
    pallas_call x1, Pallas kernels, shards(): pl.pallas_call(kernel, out_shape=(jax.ShapeDtypeStruct((4, 4, 16, HEAD),...  113 us
    unnamed x6, local copies, waits for them, and re-layouts  6.28 us

profile of v1, /device:TPU:8, one launch (start us, length us, event | category | flops | bytes accessed | tf_op | source)
XLA Modules:
  0.0 119.6 jit_solution(17412363701761699348)
XLA Ops:
  0.6 112.7 %sublayer.1 = (bf16[4,4,16,128]{3,2,1,0:T(8,128)(2,1)}, bf16[4,4,16,128]{3,2,1,0:T(8,128)(2,1)}, bf16[4,4,128,384]{3,2,1,0:T(8,128)(2,1)}, bf16[128,128]{1,0:T(8,128)(2,1)}) custom-call(bf16[4,4,16,128]{3,2,1,0:T(8,128)(2,1)} %bitcast.7, bf16[16,128]{1,0:T(8,128)(2,1)} %bitcast.11, bf16[2048,384]{1,0:T(8,128)(2,1)} %wqkv_hbm.1, bf16[128,2048]{1,0:T(8,128)(2,1)} %wout_hbm.1, ...), custom_call_target="tpu_custom_call" | custom-call | tf_op jit(solution)/shard_map/sublayer/pallas_call | solution.py:519
  113.3 1.5 %copy.13 = bf16[1,256,128]{2,1,0:T(8,128)(2,1)} copy(bf16[1,256,128]{2,1,0:T(8,128)(2,1)} %bitcast.10) | data formatting | bytes 131072
  114.8 1.5 %copy.14 = bf16[1,256,128]{2,1,0:T(8,128)(2,1)} copy(bf16[1,256,128]{2,1,0:T(8,128)(2,1)} %bitcast.9) | data formatting | bytes 131072
  116.3 0.0 copy-start
  116.3 2.7 %copy.15 = bf16[2048,384]{1,0:T(8,128)(2,1)} copy(bf16[2048,384]{1,0:T(8,128)(2,1)} %bitcast.6) | data formatting | bytes 3145728
  119.0 0.0 copy-done
  119.0 0.6 copy.16
Async XLA Ops:
  116.3 2.7 %copy-start = (bf16[128,128]{1,0:T(8,128)(2,1)S(1)}, bf16[128,128]{1,0:T(8,128)(2,1)}, u32[]{:S(2)}) copy-start(bf16[128,128]{1,0:T(8,128)(2,1)} %get-tuple-element.19) | copy-start | bytes 98308

commit v2 on v1

--- a/solution.py
+++ b/solution.py
@@ -10,7 +10,8 @@
 BF = jnp.bfloat16
 F32 = jnp.float32
 MESH = pl.DeviceIdType.MESH
-COPIES = 200
+COPIES = 232
+CUT = 96
 NT = (((1,), (1,)), ((), ()))
 
 
@@ -28,26 +29,26 @@
 
 def kernel(
     x_hbm, gain_hbm, wqkv_hbm, wout_hbm, g_hbm,
-    lo_hbm, ig_hbm, dwqkv_hbm, dwo_hbm,
+    lo_out, ig_out, dwqkv_out, dwo_out,
     x_ref, g_ref, gain_ref, a1x, a1g, xb, gb, wqkv, wout, gain, inv, norm, norm_t, qkv, att, att_t,
     probs, probs_t, gheads, dqkv, term1, term2, rb1, rb2, zs1, zb1, zs2, zb2, rowb,
-    wg, tx, px, mx, sx, rz, res, dwo, los, igs, b1l, b1i, lod, igd,
+    wg, tx, px, mx, sx, tz, pz, mz, tzz, pzz, mzz, szz, rxx, res, dwo, los, igs, b1l, b1i, lod, igd,
     ssem, rsem, lsem,
 ):
     clip, seq, mp = lax.axis_index("clip"), lax.axis_index("seq"), lax.axis_index("mp")
-    zh, x = lax.div(seq, 4), lax.rem(seq, 4)
-    zl, y = lax.div(mp, 8), lax.rem(mp, 8)
+    zh, x = seq // 4, seq & 3
+    zl, y = mp // 8, mp & 7
     e = 1 - 2 * clip
     zp = 1 - zl
 
     def x_at(step):
-        return lax.rem(x + step + 4, 4)
+        return (x + step) & 3
 
     def z_at(step):
-        return lax.rem(zh + step + 4, 4)
+        return (zh + step) & 3
 
     def y_at(step):
-        return lax.rem(y + step + 8, 8)
+        return (y + step) & 7
 
     def dev_x(to):
         return (clip, zh * 4 + to, mp)
@@ -218,78 +219,121 @@
             + zb[...].astype(F32)
         )
 
-    def weight_sum(c, gathered):
-        xp, xm = x_at(e), x_at(-e)
-        ahead, back = dev_x(xp), dev_x(xm)
-        order = (2, 1, 3, 0)
-        far = {}
-        for r in order:
-            far[r] = send(wg.at[c, z_at(r), x_at(2)], tx.at[c, z_at(r)], ahead)
-        plain = send(wg.at[c, :, xm], px.at[c], back)
-        near = {}
-        for r in order:
-            yield 3.0 if r == 2 else 0.7
-            q = z_at(r)
-            far[r].wait_recv()
-            tx[c, q] = (tx[c, q].astype(F32) + wg[c, q, xp].astype(F32)).astype(BF)
-            near[r] = send(tx.at[c, q], mx.at[c, q], ahead)
-        across = []
+    def weight_sum(c, rows, gathered):
+        r = pl.ds(0, rows)
+        xp, xm, zm = x_at(e), x_at(-e), z_at(-e)
+        ahead, back, z_ahead, z_back = dev_x(xp), dev_x(xm), dev_z(z_at(e)), dev_z(zm)
+        q = (z_at(2), z_at(e), zm, zh)
+        far = [send(wg.at[c, q[i], x_at(2), r], tx.at[c, i, r], ahead) for i in range(4)]
+        plain = send(wg.at[c, :, xm, r], px.at[c, :, r], back)
+        near = []
+
+        def here(i):
+            return (
+                wg[c, q[i], x, r].astype(F32) + px[c, q[i], r].astype(F32) + mx[c, i, r].astype(F32)
+            )
+
+        for i in range(4):
+            yield 4.0 if i == 0 else 1.0
+            far[i].wait_recv()
+            tx[c, i, r] = (tx[c, i, r].astype(F32) + wg[c, q[i], xp, r].astype(F32)).astype(BF)
+            near.append(send(tx.at[c, i, r], mx.at[c, i, r], ahead))
         yield 1.0
         plain.wait_recv()
-        for r in order[:3]:
-            yield 0.7
-            q = z_at(r)
-            near[r].wait_recv()
-            sx[c, q] = (
-                wg[c, q, x].astype(F32) + px[c, q].astype(F32) + mx[c, q].astype(F32)
-            ).astype(BF)
-            across.append(send(sx.at[c, q], rz.at[c, r - 1], dev_z(q)))
-        yield 0.7
         near[0].wait_recv()
-        total = wg[c, zh, x].astype(F32) + px[c, zh].astype(F32) + mx[c, zh].astype(F32)
-        yield 2.0
-        for copy in across:
-            copy.wait_recv()
-        for r in range(3):
-            total += rz[c, r].astype(F32)
+        sx[c, 0, r] = here(0).astype(BF)
+        z_far = send(sx.at[c, 0, r], tz.at[c, r], z_ahead)
+        yield 1.5
+        near[1].wait_recv()
+        near[2].wait_recv()
+        sx[c, 1, r] = here(2).astype(BF)
+        z_plain = send(sx.at[c, 1, r], pz.at[c, r], z_back)
+        yield 1.5
+        z_far.wait_recv()
+        tz[c, r] = (tz[c, r].astype(F32) + here(1)).astype(BF)
+        z_near = send(tz.at[c, r], mz.at[c, r], z_ahead)
+        yield 3.0
+        near[3].wait_recv()
+        z_plain.wait_recv()
+        z_near.wait_recv()
+        total = (here(3) + pz[c, r].astype(F32) + mz[c, r].astype(F32)).astype(BF)
         if not gathered:
-            dwo[...] = total.astype(BF)
-            store(dwo, dwo_hbm)
+            dwo[...] = total
+            store(dwo, dwo_out)
             return
-        res[c, zh, x] = total.astype(BF)
-
-        def pass_on(q, column, device):
-            return send(res.at[c, q, column], res.at[c, q, column], device)
-
-        zm = z_at(-e)
-        up = pass_on(zh, x, dev_z(z_at(e)))
-        down = pass_on(zh, x, dev_z(zm))
+        res[c, zh, x, r] = total
+
+        def pass_on(at, column, device):
+            return send(res.at[c, at, column, r], res.at[c, at, column, r], device)
+
+        up = pass_on(zh, x, z_ahead)
+        down = pass_on(zh, x, z_back)
         first, second = [pass_on(zh, x, ahead)], [pass_on(zh, x, back)]
         third = []
-        yield 2.5
+        yield 3.0
         up.wait_recv()
-        up = pass_on(zm, x, dev_z(z_at(e)))
+        up = pass_on(zm, x, z_ahead)
         first.append(pass_on(zm, x, ahead))
         second.append(pass_on(zm, x, back))
         yield 0.2
         down.wait_recv()
-        first.append(pass_on(z_at(e), x, ahead))
-        second.append(pass_on(z_at(e), x, back))
+        first.append(pass_on(q[1], x, ahead))
+        second.append(pass_on(q[1], x, back))
         yield 0.3
         first[0].wait_recv()
         third.append(pass_on(zh, xm, ahead))
-        yield 2.0
+        yield 2.5
         up.wait_recv()
-        first.append(pass_on(z_at(2), x, ahead))
-        second.append(pass_on(z_at(2), x, back))
-        for at, q in ((1, zm), (2, z_at(e)), (3, z_at(2))):
-            yield 0.7
-            first[at].wait_recv()
-            third.append(pass_on(q, xm, ahead))
+        first.append(pass_on(q[0], x, ahead))
+        second.append(pass_on(q[0], x, back))
+        for i, at in ((1, zm), (2, q[1]), (3, q[0])):
+            yield 1.0
+            first[i].wait_recv()
+            third.append(pass_on(at, xm, ahead))
+        yield 3.0
+        for copy in second + third:
+            copy.wait_recv()
+        store(res.at[c, :, :, r], dwqkv_out.at[:, :, r, pl.ds(c * 128, 128)])
+
+    def weight_sum_z(c):
+        r = pl.ds(CUT, 128 - CUT)
+        zp_, zm = z_at(e), z_at(-e)
+        ahead, back = dev_z(zp_), dev_z(zm)
+        far = send(wg.at[c, z_at(2), :, r], tzz.at[c], ahead)
+        plain = send(wg.at[c, zm, :, r], pzz.at[c], back)
+        yield 5.0
+        far.wait_recv()
+        tzz[c] = (tzz[c].astype(F32) + wg[c, zp_, :, r].astype(F32)).astype(BF)
+        near = send(tzz.at[c], mzz.at[c], ahead)
+        yield 5.0
+        plain.wait_recv()
+        near.wait_recv()
+        szz[c] = (
+            wg[c, zh, :, r].astype(F32) + pzz[c].astype(F32) + mzz[c].astype(F32)
+        ).astype(BF)
+        across = [send(szz.at[c, x_at(s)], rxx.at[c, s - 1], dev_x(x_at(s))) for s in (1, 3, 2)]
         yield 2.5
-        for copy in second + third:
-            copy.wait_recv()
-        store(res.at[c], dwqkv_hbm.at[:, :, :, pl.ds(c * 128, 128)])
+        for copy in across:
+            copy.wait_recv()
+        total = wg[c, zh, x, r].astype(F32) + pzz[c, x].astype(F32) + mzz[c, x].astype(F32)
+        for s in range(3):
+            total += rxx[c, s].astype(F32)
+        res[c, zh, x, r] = total.astype(BF)
+        own = res.at[c, zh, x, r]
+        across = [send(own, own, dev_x(x_at(s))) for s in (1, 3, 2)]
+        yield 2.5
+        for copy in across:
+            copy.wait_recv()
+        own = res.at[c, zh, :, r]
+        up, down = send(own, own, ahead), send(own, own, back)
+        yield 5.0
+        up.wait_recv()
+        other = res.at[c, zm, :, r]
+        up = send(other, other, ahead)
+        yield 5.0
+        down.wait_recv()
+        up.wait_recv()
+        store(res.at[c, :, :, r], dwqkv_out.at[:, :, r, pl.ds(c * 128, 128)])
 
     flows = []
     clock = [0.0]
@@ -309,6 +353,10 @@
     def finish(flow):
         while any(item[1] is flow for item in flows):
             step(min(flows, key=lambda item: item[0]))
+
+    def advance(flow, waits):
+        for _ in range(waits):
+            step(next(item for item in flows if item[1] is flow))
 
     def passed(time):
         target = clock[0] + time
@@ -325,6 +373,7 @@
     finish(flow_x)
     gather_x = start(gather(xb))
     finish(flow_g)
+    advance(gather_x, 7)
     gather_g = start(gather(gb))
     finish(gather_x)
 
@@ -377,7 +426,7 @@
         )
         yield 0.1
         yield from patches_to_frames(los, b1l, lod)
-        store(lod, lo_hbm)
+        store(lod, lo_out)
 
     start(layer_flow())
     att_t[...] = jnp.transpose(attended).astype(BF)
@@ -395,17 +444,20 @@
     def pair_of(i):
         return jnp.concatenate([flat(gb[2 * i]), flat(gb[2 * i + 1])], axis=1)
 
-    total = jnp.zeros((256, HEAD), F32)
-    for i in range(8):
-        total += mm_nt(pair_of(i), wout[:, pl.ds(i * 256, 256)])
-    gheads[...] = total.astype(BF)
-
     def out_weight(i, carry):
         wide = mm(att_t[...], pair_of(i)).astype(BF)
         wg[3, lax.div(i, 2), 2 * lax.rem(i, 2)] = wide[:, :128]
         wg[3, lax.div(i, 2), 2 * lax.rem(i, 2) + 1] = wide[:, 128:]
         return carry
 
+    lax.fori_loop(0, 8, out_weight, 0, unroll=4)
+    start(weight_sum(3, 128, False))
+    passed(1.0)
+    total = jnp.zeros((256, HEAD), F32)
+    for i in range(8):
+        total += mm_nt(pair_of(i), wout[:, pl.ds(i * 256, 256)])
+    gheads[...] = total.astype(BF)
+
     def in_weight(c):
         grad = dqkv[:, pl.ds(c * 128, 128)]
 
@@ -416,7 +468,8 @@
             return carry
 
         lax.fori_loop(0, 8, body, 0, unroll=4)
-        start(weight_sum(c, True))
+        start(weight_sum(c, CUT, True))
+        start(weight_sum_z(c))
         passed(1.5)
 
     dqkv[:, pl.ds(256, 128)] = mm(probs_t[...], gheads[...]).astype(BF)
@@ -429,16 +482,11 @@
     low = (dscores - high.astype(F32)).astype(BF)
     keys = qkv[:, pl.ds(128, 128)]
     dqkv[:, pl.ds(0, 128)] = (mm(high, keys) + mm(low, keys)).astype(BF)
-    in_weight(0)
     turned = jnp.transpose(dscores)
     high = turned.astype(BF)
     low = (turned - high.astype(F32)).astype(BF)
     queries = qkv[:, pl.ds(0, 128)]
     dqkv[:, pl.ds(128, 128)] = (mm(high, queries) + mm(low, queries)).astype(BF)
-    in_weight(1)
-    lax.fori_loop(0, 8, out_weight, 0, unroll=4)
-    start(weight_sum(3, False))
-    passed(1.5)
 
     def norm_term(i, total):
         tall = wqkv[pl.ds(pl.multiple_of(i * 256, 256), 256), :]
@@ -470,9 +518,12 @@
         igs[...] = out.astype(BF).reshape(4, 4, 16, HEAD)
         yield 0.1
         yield from patches_to_frames(igs, b1i, igd)
-        store(igd, ig_hbm)
+        store(igd, ig_out)
 
     start(input_flow())
+    passed(2.0)
+    in_weight(0)
+    in_weight(1)
     while flows:
         step(min(flows, key=lambda item: item[0]))
 
@@ -507,14 +558,17 @@
         f32(16, 8, 256),
         bf(4, 4, 4, HEAD, HEAD),
         bf(4, 4, HEAD, HEAD), bf(4, 4, HEAD, HEAD),
-        bf(4, 4, HEAD, HEAD), bf(4, 4, HEAD, HEAD),
-        bf(4, 3, HEAD, HEAD),
+        bf(4, 4, HEAD, HEAD), bf(4, 2, HEAD, HEAD),
+        bf(4, HEAD, HEAD), bf(4, HEAD, HEAD), bf(4, HEAD, HEAD),
+        bf(3, 4, 128 - CUT, HEAD), bf(3, 4, 128 - CUT, HEAD),
+        bf(3, 4, 128 - CUT, HEAD), bf(3, 4, 128 - CUT, HEAD),
+        bf(3, 3, 128 - CUT, HEAD),
         bf(3, 4, 4, HEAD, HEAD), bf(HEAD, HEAD),
         bf(4, 4, 16, HEAD), bf(4, 4, 16, HEAD), bf(4, 4, 16, HEAD),
         bf(4, 4, 16, HEAD), bf(4, 4, 16, HEAD), bf(4, 4, 16, HEAD),
         pltpu.SemaphoreType.DMA((COPIES,)),
         pltpu.SemaphoreType.DMA((COPIES,)),
-        pltpu.SemaphoreType.DMA((11,)),
+        pltpu.SemaphoreType.DMA((14,)),
     ]
     layer_out, input_grad, qkv_weight_grad, out_weight_grad = pl.pallas_call(
         kernel,
@@ -528,7 +582,7 @@
         out_specs=(hbm, hbm, hbm, hbm),
         scratch_shapes=scratch,
         compiler_params=pltpu.CompilerParams(
-            collective_id=0, has_side_effects=True, vmem_limit_bytes=60 * 1024 * 1024
+            collective_id=0, has_side_effects=True, vmem_limit_bytes=54656 * 1024
         ),
         name="sublayer",
     )(

time: 120 us -> 123 us (1.025)
  the two profiles are of different devices: /device:TPU:8 before, /device:TPU:4 now
where the time goes in v2:
time: 123 us
  Pallas kernels  115 us (93%)
  local copies, waits for them, and re-layouts  6.94 us (6%)
    pallas_call x1, Pallas kernels, shards(): pl.pallas_call(kernel, out_shape=(jax.ShapeDtypeStruct((4, 4, 16, HEAD),...  115 us
    unnamed x10, local copies, waits for them, and re-layouts  6.94 us

profile of v2, /device:TPU:4, one launch (start us, length us, event | category | flops | bytes accessed | tf_op | source)
XLA Modules:
  0.0 122.7 jit_solution(989339665254147818)
XLA Ops:
  0.6 0.0 copy-start
  0.6 0.8 copy-done
  1.5 0.0 copy-start.1
  1.5 0.8 copy-done.1
  2.3 0.0 copy-start.2
  2.3 0.7 copy-done.2
  3.0 115.1 %sublayer.1 = (bf16[4,4,16,128]{3,2,1,0:T(8,128)(2,1)S(1)}, bf16[4,4,16,128]{3,2,1,0:T(8,128)(2,1)S(1)}, bf16[4,4,128,384]{3,2,1,0:T(8,128)(2,1)}, bf16[128,128]{1,0:T(8,128)(2,1)S(1)}) custom-call(bf16[4,4,16,128]{3,2,1,0:T(8,128)(2,1)S(1)} %bitcast.6, bf16[16,128]{1,0:T(8,128)(2,1)S(1)} %bitcast.10, bf16[2048,384]{1,0:T(8,128)(2,1)} %wqkv_hbm.1, ...), custom_call_target="tpu_custom_call" | custom-call | tf_op jit(solution)/shard_map/sublayer/pallas_call | solution.py:573
  118.1 0.6 copy.13
  118.8 0.6 copy.14
  119.4 2.7 %copy.15 = bf16[2048,384]{1,0:T(8,128)(2,1)} copy(bf16[2048,384]{1,0:T(8,128)(2,1)} %bitcast.11) | data formatting | bytes 3145728
  122.1 0.6 copy.16
Async XLA Ops:
  0.6 0.8 copy-start
  1.5 0.8 copy-start.1
  2.3 0.7 copy-start.2

commit v3 on v1

v3 whole, which is shorter than its diff:
```python
import jax
import jax.numpy as jnp
from jax import lax
from jax.experimental import pallas as pl
from jax.experimental.pallas import tpu as pltpu
from jax.sharding import PartitionSpec as P

HEAD = 128
EPS = 1e-05
BF = jnp.bfloat16
F32 = jnp.float32
MESH = pl.DeviceIdType.MESH
COPIES = 232
NT = (((1,), (1,)), ((), ()))


def mm(a, b):
    return jnp.dot(a, b, preferred_element_type=F32)


def mm_nt(a, b):
    return lax.dot_general(a, b, NT, preferred_element_type=F32)


def flat(block):
    return block.reshape(256, HEAD)


def kernel(
    x_hbm, gain_hbm, wqkv_hbm, wout_hbm, g_hbm,
    lo_out, ig_out, dwqkv_out, dwo_out,
    x_ref, g_ref, gain_ref, xb, gb, wqkv, wout, gain, inv, norm, norm_t, qkv, att, att_t,
    probs, probs_t, gheads, dqkv, term1, term2, rb1, rb2, zs1, zb1, zs2, zb2, rowb,
    wg, tx, px, mx, sx, rz, res, dwo, los, igs, lod, igd,
    ssem, rsem, lsem,
):
    clip, seq, mp = lax.axis_index("clip"), lax.axis_index("seq"), lax.axis_index("mp")
    zh, x = seq // 4, seq & 3
    zl, y = mp // 8, mp & 7
    e = 1 - 2 * clip
    zp = 1 - zl

    def x_at(step):
        return (x + step) & 3

    def z_at(step):
        return (zh + step) & 3

    def y_at(step):
        return (y + step) & 7

    def dev_x(to):
        return (clip, zh * 4 + to, mp)

    def dev_z(to):
        return (clip, to * 4 + x, mp)

    def dev_y(to):
        return (clip, seq, zl * 8 + to)

    dev_pair = (clip, seq, zp * 8 + y)

    loads = [
        pltpu.make_async_copy(src, dst, lsem.at[at])
        for at, (src, dst) in enumerate(
            [(x_hbm, x_ref), (g_hbm, g_ref), (gain_hbm, gain_ref), (wqkv_hbm, wqkv), (wout_hbm, wout)]
        )
    ]
    for load in loads:
        load.start()

    barrier = pltpu.get_barrier_semaphore()
    peers = [(clip, (seq + s) & 15, mp) for s in range(1, 16)]
    peers += [dev_y(y_at(s)) for s in (1, -1, 2, -2)] + [dev_pair]
    for peer in peers:
        pl.semaphore_signal(barrier, inc=1, device_id=peer, device_id_type=MESH)
    pl.semaphore_wait(barrier, len(peers))

    started = []

    def send(src, dst, device):
        at = len(started)
        copy = pltpu.make_async_remote_copy(
            src_ref=src,
            dst_ref=dst,
            send_sem=ssem.at[at],
            recv_sem=rsem.at[at],
            device_id=device,
            device_id_type=MESH,
        )
        copy.start()
        started.append(copy)
        return copy

    stores = []

    def store(src, dst):
        stores.append(pltpu.make_async_copy(src, dst, lsem.at[len(loads) + len(stores)]))
        stores[-1].start()

    def frames_to_patches(src, dst):
        sent = []
        for s in range(1, 16):
            to = (seq + s) & 15
            sent.append(send(src.at[to], dst.at[mp, seq], (clip, to, mp)))
        dst[mp, seq] = src[seq]
        yield 4.0
        for copy in sent:
            copy.wait_recv()

    def patches_to_frames(src, dst):
        sent = []
        for s in range(1, 16):
            to = (seq + s) & 15
            sent.append(send(src.at[to], dst.at[seq], (clip, to, mp)))
        dst[seq] = src[seq]
        yield 4.0
        for copy in sent:
            copy.wait_recv()

    def gather(buf):
        def pass_on(block, device):
            return send(buf.at[block], buf.at[block], device)

        def own(step):
            return zl * 8 + y_at(step)

        def other(step):
            return zp * 8 + y_at(step)

        ahead, back, ahead_2, back_2 = (dev_y(y_at(s)) for s in (e, -e, 2 * e, -2 * e))
        a2 = pass_on(mp, ahead_2)
        b2 = pass_on(mp, back_2)
        pair = [pass_on(mp, dev_pair)]
        a1 = pass_on(mp, ahead)
        b1 = pass_on(mp, back)
        yield 4.0
        a2.wait_recv()
        a4 = pass_on(own(-2 * e), ahead_2)
        a3 = pass_on(own(-2 * e), ahead)
        pair.append(pass_on(own(-2 * e), dev_pair))
        yield 0.1
        b2.wait_recv()
        b3 = pass_on(own(2 * e), back)
        pair.append(pass_on(own(2 * e), dev_pair))
        yield 0.5
        pair[0].wait_recv()
        c1 = pass_on(other(0), ahead)
        d1 = pass_on(other(0), back)
        yield 0.5
        a1.wait_recv()
        b1.wait_recv()
        yield 3.0
        a3.wait_recv()
        pair.append(pass_on(own(-3 * e), dev_pair))
        yield 0.1
        b3.wait_recv()
        pair.append(pass_on(own(3 * e), dev_pair))
        yield 1.0
        a4.wait_recv()
        pair.append(pass_on(own(-4 * e), dev_pair))
        yield 0.2
        c1.wait_recv()
        d1.wait_recv()
        for copy in pair[1:]:
            yield 1.0
            copy.wait_recv()

    def scatter_sum(term, rb, zs, zb):
        planes = (zp, zl)

        def share(i, step):
            return term[planes[i] * 8 + y_at(step)].astype(F32)

        def push(i, step, slot, hop):
            return send(term.at[planes[i] * 8 + y_at(step)], rb.at[7 * i + slot], dev_y(y_at(hop)))

        a1, b1, a2, b2, a3, b3, a4 = ({} for _ in range(7))
        for i in (0, 1):
            a4[i] = push(i, 4, 0, 2 * e)
            a3[i] = push(i, 3 * e, 3, e)
            b3[i] = push(i, -3 * e, 6, -e)
        for i in (0, 1):
            a1[i] = push(i, e, 1, e)
            b1[i] = push(i, -e, 4, -e)
        for i in (0, 1):
            yield 4.0 if i == 0 else 1.0
            b3[i].wait_recv()
            far = rb.at[7 * i + 6]
            far[...] = (far[...].astype(F32) + share(i, -2 * e)).astype(BF)
            b2[i] = send(far, rb.at[7 * i + 5], dev_y(y_at(-2 * e)))
            yield 0.2
            a3[i].wait_recv()
            a4[i].wait_recv()
            far = rb.at[7 * i + 3]
            far[...] = (
                far[...].astype(F32) + rb[7 * i].astype(F32) + share(i, 2 * e)
            ).astype(BF)
            a2[i] = send(far, rb.at[7 * i + 2], dev_y(y_at(2 * e)))
        last = None
        for i in (0, 1):
            yield 4.0 if i == 0 else 1.5
            for copy in (a1[i], b1[i], a2[i], b2[i]):
                copy.wait_recv()
            if i == 0:
                zs[...] = received(term, rb, 0, zp).astype(BF)
                last = send(zs, zb, dev_pair)
        yield 2.5
        last.wait_recv()

    def received(term, rb, i, plane):
        total = term[plane * 8 + y].astype(F32)
        for slot in (1, 2, 4, 5):
            total += rb[7 * i + slot].astype(F32)
        return total

    def summed(term, rb, zb):
        return received(term, rb, 1, zl) + zb[...].astype(F32)

    def weight_sum(c, gathered):
        xp, xm = x_at(e), x_at(-e)
        ahead, back = dev_x(xp), dev_x(xm)
        q = (z_at(2), z_at(1), z_at(3), zh)
        far = [send(wg.at[c, q[i], x_at(2)], tx.at[c, i], ahead) for i in range(4)]
        plain = send(wg.at[c, :, xm], px.at[c], back)
        near = []

        def here(i):
            return wg[c, q[i], x].astype(F32) + px[c, q[i]].astype(F32) + mx[c, i].astype(F32)

        for i in range(4):
            yield 4.0 if i == 0 else 0.7
            far[i].wait_recv()
            tx[c, i] = (tx[c, i].astype(F32) + wg[c, q[i], xp].astype(F32)).astype(BF)
            near.append(send(tx.at[c, i], mx.at[c, i], ahead))
        across = []
        yield 1.0
        plain.wait_recv()
        for i in range(3):
            yield 0.7
            near[i].wait_recv()
            sx[c, i] = here(i).astype(BF)
            across.append(send(sx.at[c, i], rz.at[c, i], dev_z(q[i])))
        yield 0.7
        near[3].wait_recv()
        total = here(3)
        yield 3.0
        for i in range(3):
            across[i].wait_recv()
            total += rz[c, i].astype(F32)
        if not gathered:
            dwo[...] = total.astype(BF)
            store(dwo, dwo_out)
            return
        res[c, zh, x] = total.astype(BF)

        def pass_on(at, column, device):
            return send(res.at[c, at, column], res.at[c, at, column], device)

        across = [pass_on(zh, x, dev_z(q[i])) for i in range(3)]
        first, second = [pass_on(zh, x, ahead)], [pass_on(zh, x, back)]
        third = []
        at = (zh, z_at(3), z_at(1), z_at(2))
        for i, come in enumerate((1, 2, 0)):
            yield 3.5 if i == 0 else 0.3
            across[come].wait_recv()
            first.append(pass_on(at[i + 1], x, ahead))
            second.append(pass_on(at[i + 1], x, back))
        for i in range(4):
            yield 0.7
            first[i].wait_recv()
            third.append(pass_on(at[i], xm, ahead))
        yield 4.0
        for copy in second + third:
            copy.wait_recv()
        store(res.at[c], dwqkv_out.at[:, :, :, pl.ds(c * 128, 128)])

    flows = []
    clock = [0.0]

    def start(flow):
        flows.append([clock[0] + next(flow), flow])
        return flow

    def step(item):
        clock[0] = max(clock[0], item[0])
        wait = next(item[1], None)
        if wait is None:
            flows.remove(item)
        else:
            item[0] = clock[0] + wait

    def finish(flow):
        while any(item[1] is flow for item in flows):
            step(min(flows, key=lambda item: item[0]))

    def advance(flow, waits):
        for _ in range(waits):
            step(next(item for item in flows if item[1] is flow))

    def passed(time):
        target = clock[0] + time
        while flows and min(item[0] for item in flows) <= target:
            step(min(flows, key=lambda item: item[0]))
        clock[0] = target

    loads[0].wait()
    flow_x = start(frames_to_patches(x_ref, xb))
    loads[1].wait()
    flow_g = start(frames_to_patches(g_ref, gb))
    loads[2].wait()
    gain[...] = gain_ref[...].astype(F32)
    finish(flow_x)
    gather_x = start(gather(xb))
    finish(flow_g)
    advance(gather_x, 3)
    gather_g = start(gather(gb))
    finish(gather_x)

    def square(m, total):
        block = flat(xb[m]).astype(F32)
        return total + block * block

    squares = lax.fori_loop(0, 16, square, jnp.zeros((256, HEAD), F32))
    mean = jnp.sum(squares, axis=-1, keepdims=True) * (1.0 / 2048)
    inv[...] = jnp.broadcast_to(lax.rsqrt(mean + EPS), (256, HEAD))

    def normalise(m, carry):
        block = flat(xb[m]).astype(F32) * inv[...] * gain[pl.ds(m, 1), :]
        norm[:, pl.ds(pl.multiple_of(m * 128, 128), 128)] = block.astype(BF)
        return carry

    lax.fori_loop(0, 16, normalise, 0, unroll=2)
    passed(1.5)
    for load in loads[3:]:
        load.wait()
    qkv[...] = mm(norm[...], wqkv[...]).astype(BF)
    passed(1.0)

    scale = HEAD ** (-0.5)
    rows = lax.broadcasted_iota(jnp.int32, (256, 256), 0)
    cols = lax.broadcasted_iota(jnp.int32, (256, 256), 1)
    keep = (((rows - cols) & 15) == 0) & (cols <= rows)
    queries, keys, values = (qkv[:, pl.ds(i * 128, 128)] for i in range(3))
    scores = jnp.where(keep, mm_nt(queries, keys) * scale, -1e30)
    expo = jnp.exp(scores - jnp.max(scores, axis=-1, keepdims=True))
    soft = expo / jnp.sum(expo, axis=-1, keepdims=True)
    probs[...] = soft
    attended = mm(soft.astype(BF), values)
    att[...] = attended.astype(BF)
    passed(1.5)

    def out_term(i, carry):
        wide = mm(att[...], wout[:, pl.ds(pl.multiple_of(i * 256, 256), 256)]).astype(BF)
        term1[2 * i] = wide[:, :128]
        term1[2 * i + 1] = wide[:, 128:]
        return carry

    lax.fori_loop(0, 8, out_term, 0, unroll=4)
    passed(1.0)

    def layer_flow():
        yield from scatter_sum(term1, rb1, zs1, zb1)
        los[...] = (flat(xb[mp]).astype(F32) + summed(term1, rb1, zb1)).astype(BF).reshape(
            16, 16, HEAD
        )
        yield 0.1
        yield from patches_to_frames(los, lod)
        store(lod, lo_out)

    start(layer_flow())
    att_t[...] = jnp.transpose(attended).astype(BF)
    probs_t[...] = jnp.transpose(soft).astype(BF)

    def turn(m, carry):
        at = pl.multiple_of(m * 128, 128)
        block = norm[:, pl.ds(at, 128)].astype(F32)
        norm_t[pl.ds(at, 128), :] = jnp.transpose(block).astype(BF)
        return carry

    lax.fori_loop(0, 16, turn, 0, unroll=2)
    finish(gather_g)

    def pair_of(i):
        return jnp.concatenate([flat(gb[2 * i]), flat(gb[2 * i + 1])], axis=1)

    def out_weight(i, carry):
        wide = mm(att_t[...], pair_of(i)).astype(BF)
        wg[3, lax.div(i, 2), 2 * lax.rem(i, 2)] = wide[:, :128]
        wg[3, lax.div(i, 2), 2 * lax.rem(i, 2) + 1] = wide[:, 128:]
        return carry

    lax.fori_loop(0, 8, out_weight, 0, unroll=4)
    start(weight_sum(3, False))
    passed(1.0)
    total = jnp.zeros((256, HEAD), F32)
    for i in range(8):
        total += mm_nt(pair_of(i), wout[:, pl.ds(i * 256, 256)])
    gheads[...] = total.astype(BF)

    def in_weight(c):
        grad = dqkv[:, pl.ds(c * 128, 128)]

        def body(i, carry):
            tall = mm(norm_t[pl.ds(pl.multiple_of(i * 256, 256), 256), :], grad).astype(BF)
            wg[c, lax.div(i, 2), 2 * lax.rem(i, 2)] = tall[:128]
            wg[c, lax.div(i, 2), 2 * lax.rem(i, 2) + 1] = tall[128:]
            return carry

        lax.fori_loop(0, 8, body, 0, unroll=4)
        start(weight_sum(c, True))
        passed(1.5)

    dqkv[:, pl.ds(256, 128)] = mm(probs_t[...], gheads[...]).astype(BF)
    in_weight(2)
    dprobs = mm_nt(gheads[...], qkv[:, pl.ds(256, 128)]).astype(BF).astype(F32)
    soft = probs[...]
    delta = jnp.sum(soft * dprobs, axis=-1, keepdims=True)
    dscores = soft * (dprobs - delta) * scale
    high = dscores.astype(BF)
    low = (dscores - high.astype(F32)).astype(BF)
    keys = qkv[:, pl.ds(128, 128)]
    dqkv[:, pl.ds(0, 128)] = (mm(high, keys) + mm(low, keys)).astype(BF)
    turned = jnp.transpose(dscores)
    high = turned.astype(BF)
    low = (turned - high.astype(F32)).astype(BF)
    queries = qkv[:, pl.ds(0, 128)]
    dqkv[:, pl.ds(128, 128)] = (mm(high, queries) + mm(low, queries)).astype(BF)

    def norm_term(i, total):
        tall = wqkv[pl.ds(pl.multiple_of(i * 256, 256), 256), :]
        wide = mm_nt(dqkv[...], tall).astype(BF)
        for half in (0, 1):
            part = wide[:, half * 128 : half * 128 + 128]
            term2[2 * i + half] = part
            total += gain[pl.ds(2 * i + half, 1), :] * part.astype(F32) * flat(
                xb[2 * i + half]
            ).astype(F32)
        return total

    inner = lax.fori_loop(0, 8, norm_term, jnp.zeros((256, HEAD), F32), unroll=2)
    rowb[mp] = jnp.broadcast_to(jnp.sum(jnp.transpose(inner), axis=0, keepdims=True), (8, 256))
    rows_flow = gather(rowb)

    def input_flow():
        yield from scatter_sum(term2, rb2, zs2, zb2)
        yield from rows_flow
        row = jnp.sum(rowb[...].reshape(16, 8, 256), axis=0)[:1]
        row = jnp.transpose(jnp.broadcast_to(row, (HEAD, 256)))
        grad = summed(term2, rb2, zb2)
        scale_own = inv[...]
        out = (
            flat(gb[mp]).astype(F32)
            + scale_own * gain[pl.ds(mp, 1), :] * grad
            - flat(xb[mp]).astype(F32) * (scale_own * scale_own * scale_own) * row * (1.0 / 2048)
        )
        igs[...] = out.astype(BF).reshape(16, 16, HEAD)
        yield 0.1
        yield from patches_to_frames(igs, igd)
        store(igd, ig_out)

    start(input_flow())
    passed(2.0)
    in_weight(0)
    in_weight(1)
    while flows:
        step(min(flows, key=lambda item: item[0]))

    for copy in started:
        copy.wait_send()
    for copy in stores:
        copy.wait()


def shards(frames_in, norm_gain, w_qkv, w_out, cotangent):
    hbm = pl.BlockSpec(memory_space=pltpu.HBM)

    def bf(*shape):
        return pltpu.VMEM(shape, BF)

    def f32(*shape):
        return pltpu.VMEM(shape, F32)

    scratch = [
        bf(16, 16, HEAD), bf(16, 16, HEAD), bf(16, HEAD),
        bf(16, 16, 16, HEAD), bf(16, 16, 16, HEAD),
        bf(2048, 384), bf(HEAD, 2048),
        f32(16, HEAD), f32(256, HEAD),
        bf(256, 2048), bf(2048, 256),
        bf(256, 384), bf(256, HEAD), bf(HEAD, 256),
        f32(256, 256), bf(256, 256),
        bf(256, HEAD), bf(256, 384),
        bf(16, 256, HEAD), bf(16, 256, HEAD),
        bf(14, 256, HEAD), bf(14, 256, HEAD),
        bf(256, HEAD), bf(256, HEAD), bf(256, HEAD), bf(256, HEAD),
        f32(16, 8, 256),
        bf(4, 4, 4, HEAD, HEAD),
        bf(4, 4, HEAD, HEAD), bf(4, 4, HEAD, HEAD),
        bf(4, 4, HEAD, HEAD), bf(4, 3, HEAD, HEAD), bf(4, 3, HEAD, HEAD),
        bf(3, 4, 4, HEAD, HEAD), bf(HEAD, HEAD),
        bf(16, 16, HEAD), bf(16, 16, HEAD), bf(16, 16, HEAD), bf(16, 16, HEAD),
        pltpu.SemaphoreType.DMA((COPIES,)),
        pltpu.SemaphoreType.DMA((COPIES,)),
        pltpu.SemaphoreType.DMA((14,)),
    ]
    layer_out, input_grad, qkv_weight_grad, out_weight_grad = pl.pallas_call(
        kernel,
        out_shape=(
            jax.ShapeDtypeStruct((16, 16, HEAD), BF),
            jax.ShapeDtypeStruct((16, 16, HEAD), BF),
            jax.ShapeDtypeStruct((4, 4, HEAD, 384), BF),
            jax.ShapeDtypeStruct((HEAD, HEAD), BF),
        ),
        in_specs=[hbm] * 5,
        out_specs=(hbm, hbm, hbm, hbm),
        scratch_shapes=scratch,
        compiler_params=pltpu.CompilerParams(
            collective_id=0, has_side_effects=True, vmem_limit_bytes=56 * 1024 * 1024
        ),
        name="sublayer",
    )(
        frames_in.reshape(16, 16, HEAD),
        norm_gain.reshape(16, HEAD),
        w_qkv,
        w_out,
        cotangent.reshape(16, 16, HEAD),
    )
    return (
        layer_out.reshape(1, 256, HEAD),
        input_grad.reshape(1, 256, HEAD),
        qkv_weight_grad.reshape(2048, 384),
        out_weight_grad,
    )


def solution(mesh):
    return jax.shard_map(
        shards,
        mesh=mesh,
        in_specs=(
            P(("clip", "seq"), None, "mp"),
            P(),
            P(None, "mp"),
            P("mp", None),
            P(("clip", "seq"), None, "mp"),
        ),
        out_specs=(
            P(("clip", "seq"), None, "mp"),
            P(("clip", "seq"), None, "mp"),
            P("clip", "mp"),
            P(("clip", "mp"), "seq"),
        ),
        check_vma=False,
    )
```

time: 120 us -> 119 us (level)
  the two profiles are of different devices: /device:TPU:8 before, /device:TPU:6 now
where the time goes in v3:
time: 119 us
  Pallas kernels  112 us (94%)
  local copies, waits for them, and re-layouts  6.28 us (5%)
    pallas_call x1, Pallas kernels, shards(): pl.pallas_call(kernel, out_shape=(jax.ShapeDtypeStruct((16, 16, HEAD), BF...  112 us
    unnamed x6, local copies, waits for them, and re-layouts  6.28 us

profile of v3, /device:TPU:6, one launch (start us, length us, event | category | flops | bytes accessed | tf_op | source)
XLA Modules:
  0.0 118.7 jit_solution(17377061891732341693)
XLA Ops:
  0.6 111.8 %sublayer.1 = (bf16[16,16,128]{2,1,0:T(8,128)(2,1)}, bf16[16,16,128]{2,1,0:T(8,128)(2,1)}, bf16[4,4,128,384]{3,2,1,0:T(8,128)(2,1)}, bf16[128,128]{1,0:T(8,128)(2,1)}) custom-call(bf16[16,16,128]{2,1,0:T(8,128)(2,1)} %bitcast.7, bf16[16,128]{1,0:T(8,128)(2,1)} %bitcast.11, bf16[2048,384]{1,0:T(8,128)(2,1)} %wqkv_hbm.1, bf16[128,2048]{1,0:T(8,128)(2,1)} %wout_hbm.1, ...), custom_call_target="tpu_custom_call" | custom-call | tf_op jit(solution)/shard_map/sublayer/pallas_call | solution.py:506
  112.4 1.5 %copy.13 = bf16[1,256,128]{2,1,0:T(8,128)(2,1)} copy(bf16[1,256,128]{2,1,0:T(8,128)(2,1)} %bitcast.10) | data formatting | bytes 131072
  113.9 1.5 %copy.14 = bf16[1,256,128]{2,1,0:T(8,128)(2,1)} copy(bf16[1,256,128]{2,1,0:T(8,128)(2,1)} %bitcast.9) | data formatting | bytes 131072
  115.4 0.0 copy-start
  115.4 2.7 %copy.15 = bf16[2048,384]{1,0:T(8,128)(2,1)} copy(bf16[2048,384]{1,0:T(8,128)(2,1)} %bitcast.6) | data formatting | bytes 3145728
  118.1 0.0 copy-done
  118.1 0.6 copy.16
Async XLA Ops:
  115.4 2.7 %copy-start = (bf16[128,128]{1,0:T(8,128)(2,1)S(1)}, bf16[128,128]{1,0:T(8,128)(2,1)}, u32[]{:S(2)}) copy-start(bf16[128,128]{1,0:T(8,128)(2,1)} %get-tuple-element.19) | copy-start | bytes 98308

commit v4 on v0

v4 whole, which is shorter than its diff:
```python
import jax
import jax.numpy as jnp
from jax import lax
from jax.experimental import pallas as pl
from jax.experimental.pallas import tpu as pltpu
from jax.sharding import PartitionSpec as P

HEAD = 128
EPS = 1e-05
BF = jnp.bfloat16
F32 = jnp.float32
MESH = pl.DeviceIdType.MESH
COPIES = 92
ROWS = 544
SCALE = HEAD ** (-0.5)
NT = (((1,), (1,)), ((), ()))


def mm(a, b):
    return jnp.dot(a, b, preferred_element_type=F32)


def mm_nt(a, b):
    return lax.dot_general(a, b, NT, preferred_element_type=F32)


def mm_tn(a, b):
    return lax.dot_general(a, b, (((0,), (0,)), ((), ())), preferred_element_type=F32)


class Net:
    def __init__(self, ssem, rsem):
        self.ssem, self.rsem, self.started, self.flows, self.clock = ssem, rsem, [], [], 0.0
        clip, seq, mp = lax.axis_index("clip"), lax.axis_index("seq"), lax.axis_index("mp")
        self.clip, self.seq, self.mp = clip, seq, mp
        self.zh, self.x = seq // 4, seq & 3
        self.zl, self.y = mp // 8, mp & 7
        self.e = 1 - 2 * clip
        self.zp = 1 - self.zl
        self.dev_pair = (clip, seq, self.zp * 8 + self.y)
        barrier = pltpu.get_barrier_semaphore()
        peers = [self.dev_x(self.x_at(s)) for s in (1, 2, 3)]
        peers += [self.dev_z(self.z_at(s)) for s in (1, 2, 3)]
        peers += [self.dev_y(self.y_at(s)) for s in (1, -1, 2, -2)] + [self.dev_pair]
        for peer in peers:
            pl.semaphore_signal(barrier, inc=1, device_id=peer, device_id_type=MESH)
        pl.semaphore_wait(barrier, len(peers))

    def x_at(self, step):
        return (self.x + step) & 3

    def z_at(self, step):
        return (self.zh + step) & 3

    def y_at(self, step):
        return (self.y + step) & 7

    def dev_x(self, to):
        return (self.clip, self.zh * 4 + to, self.mp)

    def dev_z(self, to):
        return (self.clip, to * 4 + self.x, self.mp)

    def dev_y(self, to):
        return (self.clip, self.seq, self.zl * 8 + to)

    def send(self, src, dst, device):
        at = len(self.started)
        copy = pltpu.make_async_remote_copy(
            src_ref=src,
            dst_ref=dst,
            send_sem=self.ssem.at[at],
            recv_sem=self.rsem.at[at],
            device_id=device,
            device_id_type=MESH,
        )
        copy.start()
        self.started.append(copy)
        return copy

    def start(self, flow):
        self.flows.append([self.clock + next(flow), flow])
        return flow

    def step(self):
        item = min(self.flows, key=lambda entry: entry[0])
        self.clock = max(self.clock, item[0])
        wait = next(item[1], None)
        if wait is None:
            self.flows.remove(item)
        else:
            item[0] = self.clock + wait

    def only(self, flow):
        item = next(entry for entry in self.flows if entry[1] is flow)
        self.clock = max(self.clock, item[0])
        item[0] = self.clock + next(flow)

    def finish(self, flow=None):
        while any(flow is None or item[1] is flow for item in self.flows):
            self.step()

    def passed(self, time):
        target = self.clock + time
        while self.flows and min(item[0] for item in self.flows) <= target:
            self.step()
        self.clock = target

    def close(self):
        for copy in self.started:
            copy.wait_send()

    def frames_to_patches(self, src, mid, xb, gb):
        zh, x, mp = self.zh, self.x, self.mp
        sent = []
        for s in (1, 3, 2):
            to = self.x_at(s)
            sent.append(self.send(src.at[:, to], mid.at[x], self.dev_x(to)))
        mid[x] = src[:, x]
        yield 3.0
        for copy in sent:
            copy.wait_recv()
        sent = []
        for half, dst in ((0, xb), (1, gb)):
            for s in (1, 3, 2):
                to = self.z_at(s)
                sent.append(self.send(mid.at[:, to, half], dst.at[mp, zh], self.dev_z(to)))
            dst[mp, zh] = mid[:, zh, half]
        for some in (sent[:3], sent[3:]):
            yield 3.0
            for copy in some:
                copy.wait_recv()

    def patches_to_frames(self, src, mid, dst):
        zh, x = self.zh, self.x
        sent = []
        for s in (1, 3, 2):
            to = self.z_at(s)
            sent.append(self.send(src.at[to], mid.at[zh], self.dev_z(to)))
        mid[zh] = src[zh]
        yield 3.0
        for copy in sent:
            copy.wait_recv()
        sent = []
        for s in (1, 3, 2):
            to = self.x_at(s)
            sent.append(self.send(mid.at[:, to], dst.at[:, x], self.dev_x(to)))
        dst[:, x] = mid[:, x]
        yield 3.0
        for copy in sent:
            copy.wait_recv()

    def gather(self, buf):
        def pass_on(block, device):
            return self.send(buf.at[block], buf.at[block], device)

        def own(step):
            return self.zl * 8 + self.y_at(step)

        def other(step):
            return self.zp * 8 + self.y_at(step)

        ahead, back, ahead_2, back_2 = (self.dev_y(self.y_at(s)) for s in (self.e, -self.e, 2 * self.e, -2 * self.e))
        a2 = pass_on(self.mp, ahead_2)
        b2 = pass_on(self.mp, back_2)
        pair = [pass_on(self.mp, self.dev_pair)]
        a1 = pass_on(self.mp, ahead)
        b1 = pass_on(self.mp, back)
        yield 4.0
        a2.wait_recv()
        a4 = pass_on(own(-2 * self.e), ahead_2)
        a3 = pass_on(own(-2 * self.e), ahead)
        pair.append(pass_on(own(-2 * self.e), self.dev_pair))
        yield 0.1
        b2.wait_recv()
        b3 = pass_on(own(2 * self.e), back)
        pair.append(pass_on(own(2 * self.e), self.dev_pair))
        yield 0.5
        pair[0].wait_recv()
        c1 = pass_on(other(0), ahead)
        d1 = pass_on(other(0), back)
        yield 0.5
        a1.wait_recv()
        b1.wait_recv()
        yield 3.0
        a3.wait_recv()
        pair.append(pass_on(own(-3 * self.e), self.dev_pair))
        yield 0.1
        b3.wait_recv()
        pair.append(pass_on(own(3 * self.e), self.dev_pair))
        yield 1.0
        a4.wait_recv()
        pair.append(pass_on(own(-4 * self.e), self.dev_pair))
        yield 0.2
        c1.wait_recv()
        d1.wait_recv()
        for copy in pair[1:]:
            yield 1.0
            copy.wait_recv()

    def scatter_sum(self, term, rb, zs, zb):
        planes = (self.zp, self.zl)
        ways = ((self.e, 4), (-self.e, 3))
        order = [(i, j) for i in (0, 1) for j in (0, 1)]

        def slot(i, j, k):
            return i * 7 + j * 4 + k - 1

        sent = {}
        for i, j in order:
            way, steps = ways[j]
            dest = planes[i] * 8 + self.y_at(steps * way)
            sent[i, j] = self.send(term.at[dest], rb.at[slot(i, j, 1)], self.dev_y(self.y_at(way)))
        last = None
        for k in (1, 2, 3, 4):
            for i, j in order:
                way, steps = ways[j]
                if k > steps:
                    continue
                yield 5.0 if (i, j) == (0, 0) else 0.6
                sent[i, j].wait_recv()
                here = rb.at[slot(i, j, k)]
                if k < steps:
                    dest = planes[i] * 8 + self.y_at((steps - k) * way)
                    fold(here, here[...].astype(F32) + term[dest].astype(F32))
                    after = rb.at[slot(i, j, k + 1)]
                    sent[i, j] = self.send(here, after, self.dev_y(self.y_at(way)))
                elif k == 4 and i == 0:
                    fold(zs, self.received(term, rb, 0, self.zp))
                    last = self.send(zs, zb, self.dev_pair)
        yield 3.0
        last.wait_recv()

    def received(self, term, rb, i, plane):
        return (
            term[plane * 8 + self.y].astype(F32)
            + rb[7 * i + 3].astype(F32)
            + rb[7 * i + 6].astype(F32)
        )

    def weight_sum(self, piece, wg, tx, px, mx, sx, tz, pz, mz, res, dwo, done):
        zh, x, e = self.zh, self.x, self.e
        xp, xm, zm = self.x_at(e), self.x_at(-e), self.z_at(-e)
        ahead, back = self.dev_x(xp), self.dev_x(xm)
        z_ahead, z_back = self.dev_z(self.z_at(e)), self.dev_z(zm)
        q = (self.z_at(2), self.z_at(e), zm, zh)
        far, plain, near = [], [], []

        def here(i):
            return wg[q[i], x].astype(F32) + px[i].astype(F32) + mx[i].astype(F32)

        for i in range(4):
            piece(q[i])
            far.append(self.send(wg.at[q[i], self.x_at(2)], tx.at[i], ahead))
            plain.append(self.send(wg.at[q[i], xm], px.at[i], back))
            if i < 3:
                yield 0.8
        for i in range(4):
            yield 3.0
            far[i].wait_recv()
            tx[i] = (tx[i].astype(F32) + wg[q[i], xp].astype(F32)).astype(BF)
            near.append(self.send(tx.at[i], mx.at[i], ahead))
        yield 2.0
        plain[0].wait_recv()
        near[0].wait_recv()
        sx[0] = here(0).astype(BF)
        z_far = self.send(sx.at[0], tz, z_ahead)
        for i in (1, 2):
            yield 1.5
            plain[i].wait_recv()
            near[i].wait_recv()
        sx[1] = here(2).astype(BF)
        z_plain = self.send(sx.at[1], pz, z_back)
        yield 1.0
        z_far.wait_recv()
        tz[...] = (tz[...].astype(F32) + here(1)).astype(BF)
        z_near = self.send(tz, mz, z_ahead)
        yield 2.0
        plain[3].wait_recv()
        near[3].wait_recv()
        yield 3.0
        z_plain.wait_recv()
        z_near.wait_recv()
        total = (here(3) + pz[...].astype(F32) + mz[...].astype(F32)).astype(BF)
        res[zh, x] = total[:3]

        def pass_on(at, column, device):
            return self.send(res.at[at, column], res.at[at, column], device)

        up, down = pass_on(zh, x, z_ahead), pass_on(zh, x, z_back)
        first, second, third = [pass_on(zh, x, ahead)], [pass_on(zh, x, back)], []
        dwo[...] = total[3]
        yield 4.0
        up.wait_recv()
        up = pass_on(zm, x, z_ahead)
        first.append(pass_on(zm, x, ahead))
        second.append(pass_on(zm, x, back))
        yield 0.2
        down.wait_recv()
        first.append(pass_on(q[1], x, ahead))
        second.append(pass_on(q[1], x, back))
        yield 0.5
        first[0].wait_recv()
        third.append(pass_on(zh, xm, ahead))
        yield 2.0
        up.wait_recv()
        first.append(pass_on(q[0], x, ahead))
        second.append(pass_on(q[0], x, back))
        for i, at in ((1, zm), (2, q[1]), (3, q[0])):
            yield 2.0
            first[i].wait_recv()
            third.append(pass_on(at, xm, ahead))
        for copy in second + third:
            yield 1.0
            copy.wait_recv()
        done()


def flat(block):
    return block.reshape(256, HEAD)


def fold(ref, total):
    inner = total[512:528] + total[528:544]
    high = inner.astype(BF)
    ref[pl.ds(0, 512)] = total[:512].astype(BF)
    ref[pl.ds(512, 16)] = high
    ref[pl.ds(528, 16)] = (inner - high.astype(F32)).astype(BF)


def kernel(
    x_hbm, gain_hbm, wqkv_hbm, wout_hbm, g_hbm,
    lo_out, ig_out, dwqkv_out, dwo_out,
    both, mid, gain_ref, xb, gb, wqkv, wout, gain, inv, norm, norm_t, qkv, att, att_t,
    probs, probs_t, gheads, dqkv, term, rb, zs, zb,
    wg, tx, px, mx, sx, tz, pz, mz, res, dwo, done_both, back_mid, back_both,
    ssem, rsem, lsem,
):
    loads = [
        pltpu.make_async_copy(src, dst, lsem.at[at])
        for at, (src, dst) in enumerate(
            [
                (x_hbm, both.at[:, :, 0]),
                (g_hbm, both.at[:, :, 1]),
                (gain_hbm, gain_ref),
                (wqkv_hbm, wqkv),
                (wout_hbm, wout),
            ]
        )
    ]
    for load in loads:
        load.start()
    stores = []

    def store(src, dst):
        stores.append(pltpu.make_async_copy(src, dst, lsem.at[len(loads) + len(stores)]))
        stores[-1].start()

    net = Net(ssem, rsem)
    mp = net.mp

    for load in loads[:3]:
        load.wait()
    bring = net.start(net.frames_to_patches(both, mid, xb, gb))
    gain[...] = gain_ref[...].astype(F32)
    net.step()
    net.step()
    gather_x = net.start(net.gather(xb))
    net.finish(bring)
    for _ in range(3):
        net.only(gather_x)
    gather_g = net.start(net.gather(gb))
    net.finish(gather_x)

    def square(m, total):
        block = flat(xb[m]).astype(F32)
        return total + block * block

    squares = lax.fori_loop(0, 16, square, jnp.zeros((256, HEAD), F32))
    mean = jnp.sum(squares, axis=-1, keepdims=True) * (1.0 / 2048)
    inv[...] = jnp.broadcast_to(lax.rsqrt(mean + EPS), (256, HEAD))

    def normalise(m, carry):
        block = flat(xb[m]).astype(F32) * inv[...] * gain[pl.ds(m, 1), :]
        norm[:, pl.ds(pl.multiple_of(m * 128, 128), 128)] = block.astype(BF)
        return carry

    lax.fori_loop(0, 16, normalise, 0, unroll=2)
    net.passed(1.5)
    for load in loads[3:]:
        load.wait()
    qkv[...] = mm(norm[...], wqkv[...]).astype(BF)
    net.passed(1.0)

    scale = HEAD ** (-0.5)
    rows = lax.broadcasted_iota(jnp.int32, (256, 256), 0)
    cols = lax.broadcasted_iota(jnp.int32, (256, 256), 1)
    keep = (((rows - cols) & 15) == 0) & (cols <= rows)
    queries, keys, values = (qkv[:, pl.ds(i * 128, 128)] for i in range(3))
    scores = jnp.where(keep, mm_nt(queries, keys) * scale, -1e30)
    expo = jnp.exp(scores - jnp.max(scores, axis=-1, keepdims=True))
    soft = expo / jnp.sum(expo, axis=-1, keepdims=True)
    probs[...] = soft
    attended = mm(soft.astype(BF), values)
    att[...] = attended.astype(BF)
    net.passed(1.5)

    def out_term(i, carry):
        wide = mm(att[...], wout[:, pl.ds(pl.multiple_of(i * 256, 256), 256)]).astype(BF)
        term[2 * i, pl.ds(0, 256)] = wide[:, :128]
        term[2 * i + 1, pl.ds(0, 256)] = wide[:, 128:]
        return carry

    lax.fori_loop(0, 8, out_term, 0, unroll=4)
    net.passed(1.0)

    att_t[...] = jnp.transpose(attended).astype(BF)
    probs_t[...] = jnp.transpose(soft).astype(BF)

    def turn(m, carry):
        at = pl.multiple_of(m * 128, 128)
        block = norm[:, pl.ds(at, 128)].astype(F32)
        norm_t[pl.ds(at, 128), :] = jnp.transpose(block).astype(BF)
        return carry

    lax.fori_loop(0, 16, turn, 0, unroll=2)
    net.finish(gather_g)

    def pair_of(i):
        return jnp.concatenate([flat(gb[2 * i]), flat(gb[2 * i + 1])], axis=1)

    total = jnp.zeros((256, HEAD), F32)
    for i in range(8):
        total += mm_nt(pair_of(i), wout[:, pl.ds(i * 256, 256)])
    gheads[...] = total.astype(BF)

    dqkv[:, pl.ds(256, 128)] = mm(probs_t[...], gheads[...]).astype(BF)
    dprobs = mm_nt(gheads[...], qkv[:, pl.ds(256, 128)]).astype(BF).astype(F32)
    soft = probs[...]
    delta = jnp.sum(soft * dprobs, axis=-1, keepdims=True)
    dscores = soft * (dprobs - delta) * scale
    high = dscores.astype(BF)
    low = (dscores - high.astype(F32)).astype(BF)
    keys = qkv[:, pl.ds(128, 128)]
    dqkv[:, pl.ds(0, 128)] = (mm(high, keys) + mm(low, keys)).astype(BF)
    turned = jnp.transpose(dscores)
    high = turned.astype(BF)
    low = (turned - high.astype(F32)).astype(BF)
    queries = qkv[:, pl.ds(0, 128)]
    dqkv[:, pl.ds(128, 128)] = (mm(high, queries) + mm(low, queries)).astype(BF)

    def piece(q):
        for half in range(2):
            at = q * 4 + half * 2
            rows = norm_t[pl.ds(pl.multiple_of(at * 128, 256), 256), :]
            tall = mm(rows, dqkv[...]).astype(BF)
            wide = mm(att_t[...], jnp.concatenate([flat(gb[at]), flat(gb[at + 1])], axis=1)).astype(BF)
            for k in range(2):
                for c in range(3):
                    wg[q, 2 * half + k, c] = tall[k * 128 : k * 128 + 128, c * 128 : c * 128 + 128]
                wg[q, 2 * half + k, 3] = wide[:, k * 128 : k * 128 + 128]

    def stored():
        for c in range(3):
            store(res.at[:, :, c], dwqkv_out.at[:, :, :, pl.ds(c * 128, 128)])
        store(dwo, dwo_out)

    net.start(net.weight_sum(piece, wg, tx, px, mx, sx, tz, pz, mz, res, dwo, stored))
    net.passed(1.0)

    def norm_term(i, total):
        tall = wqkv[pl.ds(pl.multiple_of(i * 256, 256), 256), :]
        wide = mm_nt(dqkv[...], tall).astype(BF)
        for half in (0, 1):
            part = wide[:, half * 128 : half * 128 + 128]
            term[2 * i + half, pl.ds(256, 256)] = part
            total += gain[pl.ds(2 * i + half, 1), :] * part.astype(F32) * flat(
                xb[2 * i + half]
            ).astype(F32)
        return total

    inner = lax.fori_loop(0, 8, norm_term, jnp.zeros((256, HEAD), F32), unroll=2)
    inner = jnp.sum(jnp.transpose(inner), axis=0, keepdims=True)
    at_row = lax.broadcasted_iota(jnp.int32, (16, HEAD), 0)
    inner = jnp.where(at_row == 0, inner[:, :128], jnp.where(at_row == 1, inner[:, 128:], 0.0))
    high = inner.astype(BF)
    low = (inner - high.astype(F32)).astype(BF)
    for m in range(16):
        term[m, pl.ds(512, 16)] = high
        term[m, pl.ds(528, 16)] = low

    def token_flow():
        yield from net.scatter_sum(term, rb, zs, zb)
        total = net.received(term, rb, 1, net.zl) + zb[...].astype(F32)
        local = flat(xb[mp]).astype(F32)
        done_both[:, :, 0] = (local + total[:256]).astype(BF).reshape(4, 4, 16, HEAD)
        rows = total[512:528] + total[528:544]
        rows = jnp.concatenate(
            [jnp.transpose(jnp.broadcast_to(rows[k : k + 1], (HEAD, HEAD))) for k in (0, 1)], axis=0
        )
        scale_own = inv[...]
        grad = (
            flat(gb[mp]).astype(F32)
            + scale_own * gain[pl.ds(mp, 1), :] * total[256:512]
            - local * (scale_own * scale_own * scale_own) * rows * (1.0 / 2048)
        )
        done_both[:, :, 1] = grad.astype(BF).reshape(4, 4, 16, HEAD)
        yield 0.1
        yield from net.patches_to_frames(done_both, back_mid, back_both)
        store(back_both.at[:, :, 0], lo_out)
        store(back_both.at[:, :, 1], ig_out)

    net.start(token_flow())
    net.finish()
    net.close()
    for copy in stores:
        copy.wait()


def bf(*shape):
    return pltpu.VMEM(shape, BF)


def f32(*shape):
    return pltpu.VMEM(shape, F32)


def shards(frames_in, norm_gain, w_qkv, w_out, cotangent):
    hbm = pl.BlockSpec(memory_space=pltpu.HBM)
    block = (4, 4, 16, HEAD)
    scratch = [
        bf(4, 4, 2, 16, HEAD), bf(4, 4, 2, 16, HEAD), bf(16, HEAD),
        bf(16, *block), bf(16, *block),
        bf(2048, 384), bf(HEAD, 2048),
        f32(16, HEAD), f32(256, HEAD),
        bf(256, 2048), bf(2048, 256),
        bf(256, 384), bf(256, HEAD), bf(HEAD, 256),
        f32(256, 256), bf(256, 256),
        bf(256, HEAD), bf(256, 384),
        bf(16, ROWS, HEAD), bf(14, ROWS, HEAD), bf(ROWS, HEAD), bf(ROWS, HEAD),
        bf(4, 4, 4, HEAD, HEAD),
        bf(4, 4, HEAD, HEAD), bf(4, 4, HEAD, HEAD), bf(4, 4, HEAD, HEAD),
        bf(2, 4, HEAD, HEAD),
        bf(4, HEAD, HEAD), bf(4, HEAD, HEAD), bf(4, HEAD, HEAD),
        bf(4, 4, 3, HEAD, HEAD), bf(HEAD, HEAD),
        bf(4, 4, 2, 16, HEAD), bf(4, 4, 2, 16, HEAD), bf(4, 4, 2, 16, HEAD),
        pltpu.SemaphoreType.DMA((COPIES,)),
        pltpu.SemaphoreType.DMA((COPIES,)),
        pltpu.SemaphoreType.DMA((11,)),
    ]
    layer_out, input_grad, qkv_weight_grad, out_weight_grad = pl.pallas_call(
        kernel,
        out_shape=(
            jax.ShapeDtypeStruct(block, BF),
            jax.ShapeDtypeStruct(block, BF),
            jax.ShapeDtypeStruct((4, 4, HEAD, 384), BF),
            jax.ShapeDtypeStruct((HEAD, HEAD), BF),
        ),
        in_specs=[hbm] * 5,
        out_specs=(hbm,) * 4,
        scratch_shapes=scratch,
        compiler_params=pltpu.CompilerParams(
            collective_id=0, has_side_effects=True, vmem_limit_bytes=56 * 1024 * 1024
        ),
        name="sublayer",
    )(frames_in.reshape(block), norm_gain.reshape(16, HEAD), w_qkv, w_out, cotangent.reshape(block))
    return (
        layer_out.reshape(1, 256, HEAD),
        input_grad.reshape(1, 256, HEAD),
        qkv_weight_grad.reshape(2048, 384),
        out_weight_grad,
    )


def solution(mesh):
    return jax.shard_map(
        shards,
        mesh=mesh,
        in_specs=(
            P(("clip", "seq"), None, "mp"),
            P(),
            P(None, "mp"),
            P("mp", None),
            P(("clip", "seq"), None, "mp"),
        ),
        out_specs=(
            P(("clip", "seq"), None, "mp"),
            P(("clip", "seq"), None, "mp"),
            P("clip", "mp"),
            P(("clip", "mp"), "seq"),
        ),
        check_vma=False,
    )
```

time: 586 us -> 113 us (0.19)
  waiting for transfers between devices: 453 us -> 0 us
  Pallas kernels: 0 us -> 106 us
  blocking collectives: 50.7 us -> 0 us
  starting transfers between devices: 23.8 us -> 0 us
  local copies, waits for them, and re-layouts: 27.6 us -> 6.28 us
  between operations: 14.5 us -> 0.64 us
  matrix products: 9.21 us -> 0 us
  other arithmetic: 6.47 us -> 0 us
    unnamed x9 -> x0, waiting for transfers between devices: 185 us -> none
    psum x1 -> x0, waiting for transfers between devices: 147 us -> none  [shards(): qkv_weight_grad = lax.psum(qkv_weight_part.astype(jnp.bfloat16), 'seq')]
    all_gather x2 -> x0, waiting for transfers between devices: 107 us -> none  [the longest x1 72.5 us: shards(): gathered = lax.all_gather(frames_in, 'mp', axis=2, tiled=True)]
    pallas_call x0 -> x1, Pallas kernels: none -> 106 us  [shards(): pl.pallas_call(kernel, out_shape=(jax.ShapeDtypeStruct(block, BF), jax.Sh...]
    psum x1 -> x0, blocking collectives: 33.4 us -> none  [shards(): lax.psum(jnp.sum(gain_local * normed_grad * local_f32, axis=-1, keepdims=...]
    all_to_all x3 -> x0, starting transfers between devices: 23.5 us -> none  [the longest x1 9.88 us: shards(): lax.all_to_all(grad_heads, 'seq', split_axis=1, concat_axis=0, tiled=True)]
    unnamed x51 -> x6, local copies, waits for them, and re-layouts: 24 us -> 6.28 us
    all_to_all x1 -> x0, blocking collectives: 17.3 us -> none  [shards(): lax.all_to_all(grad_proj, 'seq', split_axis=0, concat_axis=1, tiled=True)]
  transfers between devices with their start and end apart: 9 -> 0, of which waited for: 8 -> 0; matrix products, arithmetic and copies ran while one was open for 6% -> 0% of each run, Pallas kernels for 0% -> 0%
where the time goes in v4:
time: 113 us
  Pallas kernels  106 us (94%)
  local copies, waits for them, and re-layouts  6.28 us (6%)
    pallas_call x1, Pallas kernels, shards(): pl.pallas_call(kernel, out_shape=(jax.ShapeDtypeStruct(block, BF), jax.Sh...  106 us
    unnamed x6, local copies, waits for them, and re-layouts  6.28 us

profile of v4, /device:TPU:8, one launch (start us, length us, event | category | flops | bytes accessed | tf_op | source)
XLA Modules:
  0.0 113.1 jit_solution(10777516332810994887)
XLA Ops:
  0.6 106.2 %sublayer.1 = (bf16[4,4,16,128]{3,2,1,0:T(8,128)(2,1)}, bf16[4,4,16,128]{3,2,1,0:T(8,128)(2,1)}, bf16[4,4,128,384]{3,2,1,0:T(8,128)(2,1)}, bf16[128,128]{1,0:T(8,128)(2,1)}) custom-call(bf16[4,4,16,128]{3,2,1,0:T(8,128)(2,1)} %bitcast.7, bf16[16,128]{1,0:T(8,128)(2,1)} %bitcast.11, bf16[2048,384]{1,0:T(8,128)(2,1)} %wqkv_hbm.1, bf16[128,2048]{1,0:T(8,128)(2,1)} %wout_hbm.1, ...), custom_call_target="tpu_custom_call" | custom-call | tf_op jit(solution)/shard_map/sublayer/pallas_call | solution.py:551
  106.8 1.5 %copy.13 = bf16[1,256,128]{2,1,0:T(8,128)(2,1)} copy(bf16[1,256,128]{2,1,0:T(8,128)(2,1)} %bitcast.10) | data formatting | bytes 131072
  108.3 1.5 %copy.14 = bf16[1,256,128]{2,1,0:T(8,128)(2,1)} copy(bf16[1,256,128]{2,1,0:T(8,128)(2,1)} %bitcast.9) | data formatting | bytes 131072
  109.7 0.0 copy-start
  109.7 2.7 %copy.15 = bf16[2048,384]{1,0:T(8,128)(2,1)} copy(bf16[2048,384]{1,0:T(8,128)(2,1)} %bitcast.6) | data formatting | bytes 3145728
  112.5 0.0 copy-done
  112.5 0.6 copy.16
Async XLA Ops:
  109.7 2.7 %copy-start = (bf16[128,128]{1,0:T(8,128)(2,1)S(1)}, bf16[128,128]{1,0:T(8,128)(2,1)}, u32[]{:S(2)}) copy-start(bf16[128,128]{1,0:T(8,128)(2,1)} %get-tuple-element.19) | copy-start | bytes 98308

commit v5 on v4

--- a/solution.py
+++ b/solution.py
@@ -10,8 +10,8 @@
 BF = jnp.bfloat16
 F32 = jnp.float32
 MESH = pl.DeviceIdType.MESH
-COPIES = 92
-ROWS = 544
+COPIES = 106
+ROWS = 288
 SCALE = HEAD ** (-0.5)
 NT = (((1,), (1,)), ((), ()))
 
@@ -30,7 +30,7 @@
 
 class Net:
     def __init__(self, ssem, rsem):
-        self.ssem, self.rsem, self.started, self.flows, self.clock = ssem, rsem, [], [], 0.0
+        self.ssem, self.rsem, self.started, self.flows, self.clock, self.steps = ssem, rsem, [], [], 0.0, {}
         clip, seq, mp = lax.axis_index("clip"), lax.axis_index("seq"), lax.axis_index("mp")
         self.clip, self.seq, self.mp = clip, seq, mp
         self.zh, self.x = seq // 4, seq & 3
@@ -82,19 +82,19 @@
         self.flows.append([self.clock + next(flow), flow])
         return flow
 
-    def step(self):
-        item = min(self.flows, key=lambda entry: entry[0])
+    def step(self, item=None):
+        item = item or min(self.flows, key=lambda entry: entry[0])
         self.clock = max(self.clock, item[0])
         wait = next(item[1], None)
+        self.steps[id(item[1])] = self.steps.get(id(item[1]), 0) + 1
         if wait is None:
             self.flows.remove(item)
         else:
             item[0] = self.clock + wait
 
-    def only(self, flow):
-        item = next(entry for entry in self.flows if entry[1] is flow)
-        self.clock = max(self.clock, item[0])
-        item[0] = self.clock + next(flow)
+    def until(self, flow, steps):
+        while self.steps.get(id(flow), 0) < steps:
+            self.step(next(entry for entry in self.flows if entry[1] is flow))
 
     def finish(self, flow=None):
         while any(flow is None or item[1] is flow for item in self.flows):
@@ -200,43 +200,49 @@
 
     def scatter_sum(self, term, rb, zs, zb):
         planes = (self.zp, self.zl)
-        ways = ((self.e, 4), (-self.e, 3))
-        order = [(i, j) for i in (0, 1) for j in (0, 1)]
-
-        def slot(i, j, k):
-            return i * 7 + j * 4 + k - 1
-
-        sent = {}
-        for i, j in order:
-            way, steps = ways[j]
-            dest = planes[i] * 8 + self.y_at(steps * way)
-            sent[i, j] = self.send(term.at[dest], rb.at[slot(i, j, 1)], self.dev_y(self.y_at(way)))
+
+        def share(i, step):
+            return term[planes[i] * 8 + self.y_at(step)].astype(F32)
+
+        def push(i, step, slot, hop):
+            return self.send(term.at[planes[i] * 8 + self.y_at(step)], rb.at[7 * i + slot], self.dev_y(self.y_at(hop)))
+
+        a1, b1, a2, b2, a3, b3, a4 = ({} for _ in range(7))
+        for i in (0, 1):
+            a4[i] = push(i, 4, 0, 2 * self.e)
+            a3[i] = push(i, 3 * self.e, 3, self.e)
+            b3[i] = push(i, -3 * self.e, 6, -self.e)
+        for i in (0, 1):
+            a1[i] = push(i, self.e, 1, self.e)
+            b1[i] = push(i, -self.e, 4, -self.e)
+        for i in (0, 1):
+            yield 4.0 if i == 0 else 1.0
+            b3[i].wait_recv()
+            far = rb.at[7 * i + 6]
+            fold(far, far[...].astype(F32) + share(i, -2 * self.e))
+            b2[i] = self.send(far, rb.at[7 * i + 5], self.dev_y(self.y_at(-2 * self.e)))
+            yield 0.2
+            a3[i].wait_recv()
+            a4[i].wait_recv()
+            far = rb.at[7 * i + 3]
+            fold(far, far[...].astype(F32) + rb[7 * i].astype(F32) + share(i, 2 * self.e))
+            a2[i] = self.send(far, rb.at[7 * i + 2], self.dev_y(self.y_at(2 * self.e)))
         last = None
-        for k in (1, 2, 3, 4):
-            for i, j in order:
-                way, steps = ways[j]
-                if k > steps:
-                    continue
-                yield 5.0 if (i, j) == (0, 0) else 0.6
-                sent[i, j].wait_recv()
-                here = rb.at[slot(i, j, k)]
-                if k < steps:
-                    dest = planes[i] * 8 + self.y_at((steps - k) * way)
-                    fold(here, here[...].astype(F32) + term[dest].astype(F32))
-                    after = rb.at[slot(i, j, k + 1)]
-                    sent[i, j] = self.send(here, after, self.dev_y(self.y_at(way)))
-                elif k == 4 and i == 0:
-                    fold(zs, self.received(term, rb, 0, self.zp))
-                    last = self.send(zs, zb, self.dev_pair)
-        yield 3.0
+        for i in (0, 1):
+            yield 4.0 if i == 0 else 1.5
+            for copy in (a1[i], b1[i], a2[i], b2[i]):
+                copy.wait_recv()
+            if i == 0:
+                fold(zs, self.received(term, rb, 0, self.zp))
+                last = self.send(zs, zb, self.dev_pair)
+        yield 2.5
         last.wait_recv()
 
     def received(self, term, rb, i, plane):
-        return (
-            term[plane * 8 + self.y].astype(F32)
-            + rb[7 * i + 3].astype(F32)
-            + rb[7 * i + 6].astype(F32)
-        )
+        total = term[plane * 8 + self.y].astype(F32)
+        for slot in (1, 2, 4, 5):
+            total += rb[7 * i + slot].astype(F32)
+        return total
 
     def weight_sum(self, piece, wg, tx, px, mx, sx, tz, pz, mz, res, dwo, done):
         zh, x, e = self.zh, self.x, self.e
@@ -287,29 +293,19 @@
         def pass_on(at, column, device):
             return self.send(res.at[at, column], res.at[at, column], device)
 
-        up, down = pass_on(zh, x, z_ahead), pass_on(zh, x, z_back)
+        across = [pass_on(zh, x, self.dev_z(self.z_at(s))) for s in (2, 1, 3)]
+        at = (zh, self.z_at(3), self.z_at(1), self.z_at(2))
         first, second, third = [pass_on(zh, x, ahead)], [pass_on(zh, x, back)], []
         dwo[...] = total[3]
-        yield 4.0
-        up.wait_recv()
-        up = pass_on(zm, x, z_ahead)
-        first.append(pass_on(zm, x, ahead))
-        second.append(pass_on(zm, x, back))
-        yield 0.2
-        down.wait_recv()
-        first.append(pass_on(q[1], x, ahead))
-        second.append(pass_on(q[1], x, back))
-        yield 0.5
-        first[0].wait_recv()
-        third.append(pass_on(zh, xm, ahead))
-        yield 2.0
-        up.wait_recv()
-        first.append(pass_on(q[0], x, ahead))
-        second.append(pass_on(q[0], x, back))
-        for i, at in ((1, zm), (2, q[1]), (3, q[0])):
-            yield 2.0
+        for i, come in enumerate((1, 2, 0)):
+            yield 4.0 if i == 0 else 0.5
+            across[come].wait_recv()
+            first.append(pass_on(at[i + 1], x, ahead))
+            second.append(pass_on(at[i + 1], x, back))
+        for i in range(4):
+            yield 0.5 if i == 0 else 2.0
             first[i].wait_recv()
-            third.append(pass_on(at, xm, ahead))
+            third.append(pass_on(at[i], xm, ahead))
         for copy in second + third:
             yield 1.0
             copy.wait_recv()
@@ -321,18 +317,19 @@
 
 
 def fold(ref, total):
-    inner = total[512:528] + total[528:544]
-    high = inner.astype(BF)
-    ref[pl.ds(0, 512)] = total[:512].astype(BF)
-    ref[pl.ds(512, 16)] = high
-    ref[pl.ds(528, 16)] = (inner - high.astype(F32)).astype(BF)
+    ref[pl.ds(0, 256)] = total[:256].astype(BF)
+    if total.shape[0] == ROWS:
+        inner = total[256:272] + total[272:288]
+        high = inner.astype(BF)
+        ref[pl.ds(256, 16)] = high
+        ref[pl.ds(272, 16)] = (inner - high.astype(F32)).astype(BF)
 
 
 def kernel(
     x_hbm, gain_hbm, wqkv_hbm, wout_hbm, g_hbm,
     lo_out, ig_out, dwqkv_out, dwo_out,
     both, mid, gain_ref, xb, gb, wqkv, wout, gain, inv, norm, norm_t, qkv, att, att_t,
-    probs, probs_t, gheads, dqkv, term, rb, zs, zb,
+    probs, probs_t, gheads, dqkv, term1, rb1, zs1, zb1, term2, rb2, zs2, zb2,
     wg, tx, px, mx, sx, tz, pz, mz, res, dwo, done_both, back_mid, back_both,
     ssem, rsem, lsem,
 ):
@@ -367,8 +364,7 @@
     net.step()
     gather_x = net.start(net.gather(xb))
     net.finish(bring)
-    for _ in range(3):
-        net.only(gather_x)
+    net.until(gather_x, 3)
     gather_g = net.start(net.gather(gb))
     net.finish(gather_x)
 
@@ -407,12 +403,13 @@
 
     def out_term(i, carry):
         wide = mm(att[...], wout[:, pl.ds(pl.multiple_of(i * 256, 256), 256)]).astype(BF)
-        term[2 * i, pl.ds(0, 256)] = wide[:, :128]
-        term[2 * i + 1, pl.ds(0, 256)] = wide[:, 128:]
+        term1[2 * i] = wide[:, :128]
+        term1[2 * i + 1] = wide[:, 128:]
         return carry
 
     lax.fori_loop(0, 8, out_term, 0, unroll=4)
-    net.passed(1.0)
+    net.until(gather_g, 4)
+    sum_1 = net.start(net.scatter_sum(term1, rb1, zs1, zb1))
 
     att_t[...] = jnp.transpose(attended).astype(BF)
     probs_t[...] = jnp.transpose(soft).astype(BF)
@@ -473,7 +470,7 @@
         wide = mm_nt(dqkv[...], tall).astype(BF)
         for half in (0, 1):
             part = wide[:, half * 128 : half * 128 + 128]
-            term[2 * i + half, pl.ds(256, 256)] = part
+            term2[2 * i + half, pl.ds(0, 256)] = part
             total += gain[pl.ds(2 * i + half, 1), :] * part.astype(F32) * flat(
                 xb[2 * i + half]
             ).astype(F32)
@@ -486,22 +483,25 @@
     high = inner.astype(BF)
     low = (inner - high.astype(F32)).astype(BF)
     for m in range(16):
-        term[m, pl.ds(512, 16)] = high
-        term[m, pl.ds(528, 16)] = low
+        term2[m, pl.ds(256, 16)] = high
+        term2[m, pl.ds(272, 16)] = low
 
     def token_flow():
-        yield from net.scatter_sum(term, rb, zs, zb)
-        total = net.received(term, rb, 1, net.zl) + zb[...].astype(F32)
+        yield from net.scatter_sum(term2, rb2, zs2, zb2)
+        total = net.received(term2, rb2, 1, net.zl) + zb2[...].astype(F32)
+        while any(item[1] is sum_1 for item in net.flows):
+            yield 0.5
+        summed = net.received(term1, rb1, 1, net.zl) + zb1[...].astype(F32)
         local = flat(xb[mp]).astype(F32)
-        done_both[:, :, 0] = (local + total[:256]).astype(BF).reshape(4, 4, 16, HEAD)
-        rows = total[512:528] + total[528:544]
+        done_both[:, :, 0] = (local + summed).astype(BF).reshape(4, 4, 16, HEAD)
+        rows = total[256:272] + total[272:288]
         rows = jnp.concatenate(
             [jnp.transpose(jnp.broadcast_to(rows[k : k + 1], (HEAD, HEAD))) for k in (0, 1)], axis=0
         )
         scale_own = inv[...]
         grad = (
             flat(gb[mp]).astype(F32)
-            + scale_own * gain[pl.ds(mp, 1), :] * total[256:512]
+            + scale_own * gain[pl.ds(mp, 1), :] * total[:256]
             - local * (scale_own * scale_own * scale_own) * rows * (1.0 / 2048)
         )
         done_both[:, :, 1] = grad.astype(BF).reshape(4, 4, 16, HEAD)
@@ -537,6 +537,7 @@
         bf(256, 384), bf(256, HEAD), bf(HEAD, 256),
         f32(256, 256), bf(256, 256),
         bf(256, HEAD), bf(256, 384),
+        bf(16, 256, HEAD), bf(14, 256, HEAD), bf(256, HEAD), bf(256, HEAD),
         bf(16, ROWS, HEAD), bf(14, ROWS, HEAD), bf(ROWS, HEAD), bf(ROWS, HEAD),
         bf(4, 4, 4, HEAD, HEAD),
         bf(4, 4, HEAD, HEAD), bf(4, 4, HEAD, HEAD), bf(4, 4, HEAD, HEAD),
@@ -560,7 +561,7 @@
         out_specs=(hbm,) * 4,
         scratch_shapes=scratch,
         compiler_params=pltpu.CompilerParams(
-            collective_id=0, has_side_effects=True, vmem_limit_bytes=56 * 1024 * 1024
+            collective_id=0, has_side_effects=True, vmem_limit_bytes=55040 * 1024
         ),
         name="sublayer",
     )(frames_in.reshape(block), norm_gain.reshape(16, HEAD), w_qkv, w_out, cotangent.reshape(block))

time: 113 us -> 126 us (1.12)
  the two profiles are of different devices: /device:TPU:8 before, /device:TPU:16 now
where the time goes in v5:
time: 126 us
  Pallas kernels  120 us (95%)
  local copies, waits for them, and re-layouts  5.26 us (4%)
    pallas_call x1, Pallas kernels, shards(): pl.pallas_call(kernel, out_shape=(jax.ShapeDtypeStruct(block, BF), jax.Sh...  120 us
    unnamed x6, local copies, waits for them, and re-layouts  5.26 us

profile of v5, /device:TPU:16, one launch (start us, length us, event | category | flops | bytes accessed | tf_op | source)
XLA Modules:
  0.0 125.6 jit_solution(16789184349670783001)
XLA Ops:
  0.6 0.0 copy-start
  0.6 0.7 copy-done
  1.3 119.7 %sublayer.1 = (bf16[4,4,16,128]{3,2,1,0:T(8,128)(2,1)S(1)}, bf16[4,4,16,128]{3,2,1,0:T(8,128)(2,1)S(1)}, bf16[4,4,128,384]{3,2,1,0:T(8,128)(2,1)}, bf16[128,128]{1,0:T(8,128)(2,1)S(1)}) custom-call(bf16[4,4,16,128]{3,2,1,0:T(8,128)(2,1)} %bitcast.10, bf16[16,128]{1,0:T(8,128)(2,1)S(1)} %bitcast.8, bf16[2048,384]{1,0:T(8,128)(2,1)} %wqkv_hbm.1, ...), custom_call_target="tpu_custom_call" | custom-call | tf_op jit(solution)/shard_map/sublayer/pallas_call | solution.py:552
  121.0 0.6 copy.13
  121.7 0.6 copy.14
  122.3 2.7 %copy.15 = bf16[2048,384]{1,0:T(8,128)(2,1)} copy(bf16[2048,384]{1,0:T(8,128)(2,1)} %bitcast.9) | data formatting | bytes 3145728
  125.0 0.6 copy.16
Async XLA Ops:
  0.6 0.7 copy-start

commit v6 on v4

--- a/solution.py
+++ b/solution.py
@@ -10,8 +10,8 @@
 BF = jnp.bfloat16
 F32 = jnp.float32
 MESH = pl.DeviceIdType.MESH
-COPIES = 92
-ROWS = 544
+COPIES = 112
+ROWS = 288
 SCALE = HEAD ** (-0.5)
 NT = (((1,), (1,)), ((), ()))
 
@@ -30,7 +30,7 @@
 
 class Net:
     def __init__(self, ssem, rsem):
-        self.ssem, self.rsem, self.started, self.flows, self.clock = ssem, rsem, [], [], 0.0
+        self.ssem, self.rsem, self.started, self.flows, self.clock, self.steps = ssem, rsem, [], [], 0.0, {}
         clip, seq, mp = lax.axis_index("clip"), lax.axis_index("seq"), lax.axis_index("mp")
         self.clip, self.seq, self.mp = clip, seq, mp
         self.zh, self.x = seq // 4, seq & 3
@@ -82,19 +82,19 @@
         self.flows.append([self.clock + next(flow), flow])
         return flow
 
-    def step(self):
-        item = min(self.flows, key=lambda entry: entry[0])
+    def step(self, item=None):
+        item = item or min(self.flows, key=lambda entry: entry[0])
         self.clock = max(self.clock, item[0])
         wait = next(item[1], None)
+        self.steps[id(item[1])] = self.steps.get(id(item[1]), 0) + 1
         if wait is None:
             self.flows.remove(item)
         else:
             item[0] = self.clock + wait
 
-    def only(self, flow):
-        item = next(entry for entry in self.flows if entry[1] is flow)
-        self.clock = max(self.clock, item[0])
-        item[0] = self.clock + next(flow)
+    def until(self, flow, steps):
+        while self.steps.get(id(flow), 0) < steps:
+            self.step(next(entry for entry in self.flows if entry[1] is flow))
 
     def finish(self, flow=None):
         while any(flow is None or item[1] is flow for item in self.flows):
@@ -154,48 +154,53 @@
         def pass_on(block, device):
             return self.send(buf.at[block], buf.at[block], device)
 
+        ahead, back = self.dev_y(self.y_at(self.e)), self.dev_y(self.y_at(-self.e))
+
         def own(step):
             return self.zl * 8 + self.y_at(step)
 
         def other(step):
             return self.zp * 8 + self.y_at(step)
 
-        ahead, back, ahead_2, back_2 = (self.dev_y(self.y_at(s)) for s in (self.e, -self.e, 2 * self.e, -2 * self.e))
-        a2 = pass_on(self.mp, ahead_2)
-        b2 = pass_on(self.mp, back_2)
+        a = pass_on(self.mp, ahead)
+        b = pass_on(self.mp, back)
         pair = [pass_on(self.mp, self.dev_pair)]
-        a1 = pass_on(self.mp, ahead)
-        b1 = pass_on(self.mp, back)
         yield 4.0
-        a2.wait_recv()
-        a4 = pass_on(own(-2 * self.e), ahead_2)
-        a3 = pass_on(own(-2 * self.e), ahead)
-        pair.append(pass_on(own(-2 * self.e), self.dev_pair))
+        a.wait_recv()
+        a = pass_on(own(-self.e), ahead)
         yield 0.1
-        b2.wait_recv()
-        b3 = pass_on(own(2 * self.e), back)
-        pair.append(pass_on(own(2 * self.e), self.dev_pair))
+        b.wait_recv()
+        b = pass_on(own(self.e), back)
         yield 0.5
         pair[0].wait_recv()
-        c1 = pass_on(other(0), ahead)
-        d1 = pass_on(other(0), back)
-        yield 0.5
-        a1.wait_recv()
-        b1.wait_recv()
-        yield 3.0
-        a3.wait_recv()
+        c = pass_on(other(0), ahead)
+        d = pass_on(other(0), back)
+        yield 2.5
+        a.wait_recv()
+        a = pass_on(own(-2 * self.e), ahead)
+        yield 0.1
+        b.wait_recv()
+        b = pass_on(own(2 * self.e), back)
+        pair.append(pass_on(own(2 * self.e), self.dev_pair))
+        yield 1.0
+        c.wait_recv()
+        c = pass_on(other(-self.e), ahead)
+        yield 0.1
+        d.wait_recv()
+        yield 2.5
+        a.wait_recv()
+        a = pass_on(own(-3 * self.e), ahead)
         pair.append(pass_on(own(-3 * self.e), self.dev_pair))
         yield 0.1
-        b3.wait_recv()
+        b.wait_recv()
         pair.append(pass_on(own(3 * self.e), self.dev_pair))
-        yield 1.0
-        a4.wait_recv()
+        yield 0.5
+        c.wait_recv()
+        yield 2.5
+        a.wait_recv()
         pair.append(pass_on(own(-4 * self.e), self.dev_pair))
-        yield 0.2
-        c1.wait_recv()
-        d1.wait_recv()
         for copy in pair[1:]:
-            yield 1.0
+            yield 0.5
             copy.wait_recv()
 
     def scatter_sum(self, term, rb, zs, zb):
@@ -217,7 +222,7 @@
                 way, steps = ways[j]
                 if k > steps:
                     continue
-                yield 5.0 if (i, j) == (0, 0) else 0.6
+                yield 4.0 if (i, j) == (0, 0) else 0.6
                 sent[i, j].wait_recv()
                 here = rb.at[slot(i, j, k)]
                 if k < steps:
@@ -238,7 +243,7 @@
             + rb[7 * i + 6].astype(F32)
         )
 
-    def weight_sum(self, piece, wg, tx, px, mx, sx, tz, pz, mz, res, dwo, done):
+    def weight_sum(self, piece, wg, tx, px, mx, sx, tz, pz, mz, res, done):
         zh, x, e = self.zh, self.x, self.e
         xp, xm, zm = self.x_at(e), self.x_at(-e), self.z_at(-e)
         ahead, back = self.dev_x(xp), self.dev_x(xm)
@@ -282,14 +287,13 @@
         z_plain.wait_recv()
         z_near.wait_recv()
         total = (here(3) + pz[...].astype(F32) + mz[...].astype(F32)).astype(BF)
-        res[zh, x] = total[:3]
+        res[zh, x] = total
 
         def pass_on(at, column, device):
             return self.send(res.at[at, column], res.at[at, column], device)
 
         up, down = pass_on(zh, x, z_ahead), pass_on(zh, x, z_back)
         first, second, third = [pass_on(zh, x, ahead)], [pass_on(zh, x, back)], []
-        dwo[...] = total[3]
         yield 4.0
         up.wait_recv()
         up = pass_on(zm, x, z_ahead)
@@ -315,25 +319,53 @@
             copy.wait_recv()
         done()
 
+    def out_sum(self, wo, tx, px, mx, sx, tz, pz, mz, done):
+        zh, x, e = self.zh, self.x, self.e
+        xp, xm, zm = self.x_at(e), self.x_at(-e), self.z_at(-e)
+        ahead, back = self.dev_x(xp), self.dev_x(xm)
+        z_ahead, z_back = self.dev_z(self.z_at(e)), self.dev_z(zm)
+        far = self.send(wo.at[:, self.x_at(2)], tx, ahead)
+        plain = self.send(wo.at[:, xm], px, back)
+        yield 7.0
+        far.wait_recv()
+        tx[...] = (tx[...].astype(F32) + wo[:, xp].astype(F32)).astype(BF)
+        near = self.send(tx, mx, ahead)
+        yield 6.0
+        plain.wait_recv()
+        near.wait_recv()
+        sx[...] = (wo[:, x].astype(F32) + px[...].astype(F32) + mx[...].astype(F32)).astype(BF)
+        z_far = self.send(sx.at[self.z_at(2)], tz, z_ahead)
+        z_plain = self.send(sx.at[zm], pz, z_back)
+        yield 5.0
+        z_far.wait_recv()
+        tz[...] = (tz[...].astype(F32) + sx[self.z_at(e)].astype(F32)).astype(BF)
+        z_near = self.send(tz, mz, z_ahead)
+        yield 5.0
+        z_plain.wait_recv()
+        z_near.wait_recv()
+        total = wo[zh, x].astype(F32) + px[zh].astype(F32) + mx[zh].astype(F32)
+        done((total + pz[...].astype(F32) + mz[...].astype(F32)).astype(BF))
+
 
 def flat(block):
     return block.reshape(256, HEAD)
 
 
 def fold(ref, total):
-    inner = total[512:528] + total[528:544]
-    high = inner.astype(BF)
-    ref[pl.ds(0, 512)] = total[:512].astype(BF)
-    ref[pl.ds(512, 16)] = high
-    ref[pl.ds(528, 16)] = (inner - high.astype(F32)).astype(BF)
+    ref[pl.ds(0, 256)] = total[:256].astype(BF)
+    if total.shape[0] == ROWS:
+        inner = total[256:272] + total[272:288]
+        high = inner.astype(BF)
+        ref[pl.ds(256, 16)] = high
+        ref[pl.ds(272, 16)] = (inner - high.astype(F32)).astype(BF)
 
 
 def kernel(
     x_hbm, gain_hbm, wqkv_hbm, wout_hbm, g_hbm,
     lo_out, ig_out, dwqkv_out, dwo_out,
     both, mid, gain_ref, xb, gb, wqkv, wout, gain, inv, norm, norm_t, qkv, att, att_t,
-    probs, probs_t, gheads, dqkv, term, rb, zs, zb,
-    wg, tx, px, mx, sx, tz, pz, mz, res, dwo, done_both, back_mid, back_both,
+    probs, probs_t, gheads, dqkv, term1, rb1, zs1, zb1, term2, rb2, zs2, zb2,
+    wg, tx, px, mx, sx, tz, pz, mz, wo, txo, pxo, mxo, sxo, tzo, pzo, mzo, res, dwo, done_both, back_mid, back_both,
     ssem, rsem, lsem,
 ):
     loads = [
@@ -367,8 +399,7 @@
     net.step()
     gather_x = net.start(net.gather(xb))
     net.finish(bring)
-    for _ in range(3):
-        net.only(gather_x)
+    net.until(gather_x, 7)
     gather_g = net.start(net.gather(gb))
     net.finish(gather_x)
 
@@ -386,11 +417,11 @@
         return carry
 
     lax.fori_loop(0, 16, normalise, 0, unroll=2)
-    net.passed(1.5)
+    net.passed(2.2)
     for load in loads[3:]:
         load.wait()
     qkv[...] = mm(norm[...], wqkv[...]).astype(BF)
-    net.passed(1.0)
+    net.passed(1.2)
 
     scale = HEAD ** (-0.5)
     rows = lax.broadcasted_iota(jnp.int32, (256, 256), 0)
@@ -403,12 +434,12 @@
     probs[...] = soft
     attended = mm(soft.astype(BF), values)
     att[...] = attended.astype(BF)
-    net.passed(1.5)
+    net.passed(1.8)
 
     def out_term(i, carry):
         wide = mm(att[...], wout[:, pl.ds(pl.multiple_of(i * 256, 256), 256)]).astype(BF)
-        term[2 * i, pl.ds(0, 256)] = wide[:, :128]
-        term[2 * i + 1, pl.ds(0, 256)] = wide[:, 128:]
+        term1[2 * i] = wide[:, :128]
+        term1[2 * i + 1] = wide[:, 128:]
         return carry
 
     lax.fori_loop(0, 8, out_term, 0, unroll=4)
@@ -429,10 +460,22 @@
     def pair_of(i):
         return jnp.concatenate([flat(gb[2 * i]), flat(gb[2 * i + 1])], axis=1)
 
+    sum_1 = net.start(net.scatter_sum(term1, rb1, zs1, zb1))
+    for i in range(8):
+        wide = mm(att_t[...], pair_of(i)).astype(BF)
+        wo[i // 2, 2 * (i % 2)] = wide[:, :128]
+        wo[i // 2, 2 * (i % 2) + 1] = wide[:, 128:]
+
+    def out_stored(total):
+        dwo[...] = total
+        store(dwo, dwo_out)
+
+    net.start(net.out_sum(wo, txo, pxo, mxo, sxo, tzo, pzo, mzo, out_stored))
     total = jnp.zeros((256, HEAD), F32)
     for i in range(8):
         total += mm_nt(pair_of(i), wout[:, pl.ds(i * 256, 256)])
     gheads[...] = total.astype(BF)
+    net.passed(2.5)
 
     dqkv[:, pl.ds(256, 128)] = mm(probs_t[...], gheads[...]).astype(BF)
     dprobs = mm_nt(gheads[...], qkv[:, pl.ds(256, 128)]).astype(BF).astype(F32)
@@ -454,18 +497,15 @@
             at = q * 4 + half * 2
             rows = norm_t[pl.ds(pl.multiple_of(at * 128, 256), 256), :]
             tall = mm(rows, dqkv[...]).astype(BF)
-            wide = mm(att_t[...], jnp.concatenate([flat(gb[at]), flat(gb[at + 1])], axis=1)).astype(BF)
             for k in range(2):
                 for c in range(3):
                     wg[q, 2 * half + k, c] = tall[k * 128 : k * 128 + 128, c * 128 : c * 128 + 128]
-                wg[q, 2 * half + k, 3] = wide[:, k * 128 : k * 128 + 128]
 
     def stored():
         for c in range(3):
             store(res.at[:, :, c], dwqkv_out.at[:, :, :, pl.ds(c * 128, 128)])
-        store(dwo, dwo_out)
-
-    net.start(net.weight_sum(piece, wg, tx, px, mx, sx, tz, pz, mz, res, dwo, stored))
+
+    net.start(net.weight_sum(piece, wg, tx, px, mx, sx, tz, pz, mz, res, stored))
     net.passed(1.0)
 
     def norm_term(i, total):
@@ -473,7 +513,7 @@
         wide = mm_nt(dqkv[...], tall).astype(BF)
         for half in (0, 1):
             part = wide[:, half * 128 : half * 128 + 128]
-            term[2 * i + half, pl.ds(256, 256)] = part
+            term2[2 * i + half, pl.ds(0, 256)] = part
             total += gain[pl.ds(2 * i + half, 1), :] * part.astype(F32) * flat(
                 xb[2 * i + half]
             ).astype(F32)
@@ -486,22 +526,25 @@
     high = inner.astype(BF)
     low = (inner - high.astype(F32)).astype(BF)
     for m in range(16):
-        term[m, pl.ds(512, 16)] = high
-        term[m, pl.ds(528, 16)] = low
+        term2[m, pl.ds(256, 16)] = high
+        term2[m, pl.ds(272, 16)] = low
 
     def token_flow():
-        yield from net.scatter_sum(term, rb, zs, zb)
-        total = net.received(term, rb, 1, net.zl) + zb[...].astype(F32)
+        yield from net.scatter_sum(term2, rb2, zs2, zb2)
+        total = net.received(term2, rb2, 1, net.zl) + zb2[...].astype(F32)
+        while any(item[1] is sum_1 for item in net.flows):
+            yield 0.5
+        summed = net.received(term1, rb1, 1, net.zl) + zb1[...].astype(F32)
         local = flat(xb[mp]).astype(F32)
-        done_both[:, :, 0] = (local + total[:256]).astype(BF).reshape(4, 4, 16, HEAD)
-        rows = total[512:528] + total[528:544]
+        done_both[:, :, 0] = (local + summed).astype(BF).reshape(4, 4, 16, HEAD)
+        rows = total[256:272] + total[272:288]
         rows = jnp.concatenate(
             [jnp.transpose(jnp.broadcast_to(rows[k : k + 1], (HEAD, HEAD))) for k in (0, 1)], axis=0
         )
         scale_own = inv[...]
         grad = (
             flat(gb[mp]).astype(F32)
-            + scale_own * gain[pl.ds(mp, 1), :] * total[256:512]
+            + scale_own * gain[pl.ds(mp, 1), :] * total[:256]
             - local * (scale_own * scale_own * scale_own) * rows * (1.0 / 2048)
         )
         done_both[:, :, 1] = grad.astype(BF).reshape(4, 4, 16, HEAD)
@@ -537,11 +580,15 @@
         bf(256, 384), bf(256, HEAD), bf(HEAD, 256),
         f32(256, 256), bf(256, 256),
         bf(256, HEAD), bf(256, 384),
+        bf(16, 256, HEAD), bf(14, 256, HEAD), bf(256, HEAD), bf(256, HEAD),
         bf(16, ROWS, HEAD), bf(14, ROWS, HEAD), bf(ROWS, HEAD), bf(ROWS, HEAD),
-        bf(4, 4, 4, HEAD, HEAD),
-        bf(4, 4, HEAD, HEAD), bf(4, 4, HEAD, HEAD), bf(4, 4, HEAD, HEAD),
-        bf(2, 4, HEAD, HEAD),
-        bf(4, HEAD, HEAD), bf(4, HEAD, HEAD), bf(4, HEAD, HEAD),
+        bf(4, 4, 3, HEAD, HEAD),
+        bf(4, 3, HEAD, HEAD), bf(4, 3, HEAD, HEAD), bf(4, 3, HEAD, HEAD),
+        bf(2, 3, HEAD, HEAD),
+        bf(3, HEAD, HEAD), bf(3, HEAD, HEAD), bf(3, HEAD, HEAD),
+        bf(4, 4, HEAD, HEAD), bf(4, HEAD, HEAD), bf(4, HEAD, HEAD),
+        bf(4, HEAD, HEAD), bf(4, HEAD, HEAD),
+        bf(HEAD, HEAD), bf(HEAD, HEAD), bf(HEAD, HEAD),
         bf(4, 4, 3, HEAD, HEAD), bf(HEAD, HEAD),
         bf(4, 4, 2, 16, HEAD), bf(4, 4, 2, 16, HEAD), bf(4, 4, 2, 16, HEAD),
         pltpu.SemaphoreType.DMA((COPIES,)),
@@ -560,7 +607,7 @@
         out_specs=(hbm,) * 4,
         scratch_shapes=scratch,
         compiler_params=pltpu.CompilerParams(
-            collective_id=0, has_side_effects=True, vmem_limit_bytes=56 * 1024 * 1024
+            collective_id=0, has_side_effects=True, vmem_limit_bytes=55040 * 1024
         ),
         name="sublayer",
     )(frames_in.reshape(block), norm_gain.reshape(16, HEAD), w_qkv, w_out, cotangent.reshape(block))

time: 113 us -> 115 us (1.018)
  the two profiles are of different devices: /device:TPU:8 before, /device:TPU:2 now
where the time goes in v6:
time: 115 us
  Pallas kernels  109 us (95%)
  local copies, waits for them, and re-layouts  5.26 us (5%)
    pallas_call x1, Pallas kernels, shards(): pl.pallas_call(kernel, out_shape=(jax.ShapeDtypeStruct(block, BF), jax.Sh...  109 us
    unnamed x6, local copies, waits for them, and re-layouts  5.26 us

profile of v6, /device:TPU:2, one launch (start us, length us, event | category | flops | bytes accessed | tf_op | source)
XLA Modules:
  0.0 114.7 jit_solution(13839460809676025432)
XLA Ops:
  0.6 0.0 copy-start
  0.6 0.7 copy-done
  1.3 108.8 %sublayer.1 = (bf16[4,4,16,128]{3,2,1,0:T(8,128)(2,1)S(1)}, bf16[4,4,16,128]{3,2,1,0:T(8,128)(2,1)S(1)}, bf16[4,4,128,384]{3,2,1,0:T(8,128)(2,1)}, bf16[128,128]{1,0:T(8,128)(2,1)S(1)}) custom-call(bf16[4,4,16,128]{3,2,1,0:T(8,128)(2,1)} %bitcast.10, bf16[16,128]{1,0:T(8,128)(2,1)S(1)} %bitcast.8, bf16[2048,384]{1,0:T(8,128)(2,1)} %wqkv_hbm.1, ...), custom_call_target="tpu_custom_call" | custom-call | tf_op jit(solution)/shard_map/sublayer/pallas_call | solution.py:598
  110.1 0.6 copy.13
  110.8 0.6 copy.14
  111.4 2.7 %copy.15 = bf16[2048,384]{1,0:T(8,128)(2,1)} copy(bf16[2048,384]{1,0:T(8,128)(2,1)} %bitcast.9) | data formatting | bytes 3145728
  114.1 0.6 copy.16
Async XLA Ops:
  0.6 0.7 copy-start

commit v7 on v6

--- a/solution.py
+++ b/solution.py
@@ -117,7 +117,7 @@
             to = self.x_at(s)
             sent.append(self.send(src.at[:, to], mid.at[x], self.dev_x(to)))
         mid[x] = src[:, x]
-        yield 3.0
+        yield 9.96
         for copy in sent:
             copy.wait_recv()
         sent = []
@@ -127,7 +127,7 @@
                 sent.append(self.send(mid.at[:, to, half], dst.at[mp, zh], self.dev_z(to)))
             dst[mp, zh] = mid[:, zh, half]
         for some in (sent[:3], sent[3:]):
-            yield 3.0
+            yield 2.2
             for copy in some:
                 copy.wait_recv()
 
@@ -138,7 +138,7 @@
             to = self.z_at(s)
             sent.append(self.send(src.at[to], mid.at[zh], self.dev_z(to)))
         mid[zh] = src[zh]
-        yield 3.0
+        yield 2.41
         for copy in sent:
             copy.wait_recv()
         sent = []
@@ -146,7 +146,7 @@
             to = self.x_at(s)
             sent.append(self.send(mid.at[:, to], dst.at[:, x], self.dev_x(to)))
         dst[:, x] = mid[:, x]
-        yield 3.0
+        yield 36.64
         for copy in sent:
             copy.wait_recv()
 
@@ -168,39 +168,39 @@
         yield 4.0
         a.wait_recv()
         a = pass_on(own(-self.e), ahead)
-        yield 0.1
+        yield 0.3
         b.wait_recv()
         b = pass_on(own(self.e), back)
-        yield 0.5
+        yield 0.42
         pair[0].wait_recv()
         c = pass_on(other(0), ahead)
         d = pass_on(other(0), back)
-        yield 2.5
+        yield 2.25
         a.wait_recv()
         a = pass_on(own(-2 * self.e), ahead)
-        yield 0.1
+        yield 0.62
         b.wait_recv()
         b = pass_on(own(2 * self.e), back)
         pair.append(pass_on(own(2 * self.e), self.dev_pair))
-        yield 1.0
+        yield 0.31
         c.wait_recv()
         c = pass_on(other(-self.e), ahead)
-        yield 0.1
+        yield 0.92
         d.wait_recv()
-        yield 2.5
+        yield 1.75
         a.wait_recv()
         a = pass_on(own(-3 * self.e), ahead)
         pair.append(pass_on(own(-3 * self.e), self.dev_pair))
-        yield 0.1
+        yield 0.89
         b.wait_recv()
         pair.append(pass_on(own(3 * self.e), self.dev_pair))
-        yield 0.5
+        yield 0.4
         c.wait_recv()
         yield 2.5
         a.wait_recv()
         pair.append(pass_on(own(-4 * self.e), self.dev_pair))
         for copy in pair[1:]:
-            yield 0.5
+            yield 1.05
             copy.wait_recv()
 
     def scatter_sum(self, term, rb, zs, zb):
@@ -222,7 +222,7 @@
                 way, steps = ways[j]
                 if k > steps:
                     continue
-                yield 4.0 if (i, j) == (0, 0) else 0.6
+                yield 5.6 if (i, j) == (0, 0) else 0.6
                 sent[i, j].wait_recv()
                 here = rb.at[slot(i, j, k)]
                 if k < steps:
@@ -233,7 +233,7 @@
                 elif k == 4 and i == 0:
                     fold(zs, self.received(term, rb, 0, self.zp))
                     last = self.send(zs, zb, self.dev_pair)
-        yield 3.0
+        yield 2.2
         last.wait_recv()
 
     def received(self, term, rb, i, plane):
@@ -259,9 +259,9 @@
             far.append(self.send(wg.at[q[i], self.x_at(2)], tx.at[i], ahead))
             plain.append(self.send(wg.at[q[i], xm], px.at[i], back))
             if i < 3:
-                yield 0.8
+                yield 0.78
         for i in range(4):
-            yield 3.0
+            yield 2.1
             far[i].wait_recv()
             tx[i] = (tx[i].astype(F32) + wg[q[i], xp].astype(F32)).astype(BF)
             near.append(self.send(tx.at[i], mx.at[i], ahead))
@@ -271,16 +271,16 @@
         sx[0] = here(0).astype(BF)
         z_far = self.send(sx.at[0], tz, z_ahead)
         for i in (1, 2):
-            yield 1.5
+            yield 1.26
             plain[i].wait_recv()
             near[i].wait_recv()
         sx[1] = here(2).astype(BF)
         z_plain = self.send(sx.at[1], pz, z_back)
-        yield 1.0
+        yield 1.2
         z_far.wait_recv()
         tz[...] = (tz[...].astype(F32) + here(1)).astype(BF)
         z_near = self.send(tz, mz, z_ahead)
-        yield 2.0
+        yield 3.56
         plain[3].wait_recv()
         near[3].wait_recv()
         yield 3.0
@@ -294,28 +294,28 @@
 
         up, down = pass_on(zh, x, z_ahead), pass_on(zh, x, z_back)
         first, second, third = [pass_on(zh, x, ahead)], [pass_on(zh, x, back)], []
-        yield 4.0
+        yield 6.1
         up.wait_recv()
         up = pass_on(zm, x, z_ahead)
         first.append(pass_on(zm, x, ahead))
         second.append(pass_on(zm, x, back))
-        yield 0.2
+        yield 1.45
         down.wait_recv()
         first.append(pass_on(q[1], x, ahead))
         second.append(pass_on(q[1], x, back))
-        yield 0.5
+        yield 0.8
         first[0].wait_recv()
         third.append(pass_on(zh, xm, ahead))
-        yield 2.0
+        yield 0.98
         up.wait_recv()
         first.append(pass_on(q[0], x, ahead))
         second.append(pass_on(q[0], x, back))
         for i, at in ((1, zm), (2, q[1]), (3, q[0])):
-            yield 2.0
+            yield 0.15
             first[i].wait_recv()
             third.append(pass_on(at, xm, ahead))
         for copy in second + third:
-            yield 1.0
+            yield 2.59
             copy.wait_recv()
         done()
 
@@ -326,21 +326,21 @@
         z_ahead, z_back = self.dev_z(self.z_at(e)), self.dev_z(zm)
         far = self.send(wo.at[:, self.x_at(2)], tx, ahead)
         plain = self.send(wo.at[:, xm], px, back)
-        yield 7.0
+        yield 14.5
         far.wait_recv()
         tx[...] = (tx[...].astype(F32) + wo[:, xp].astype(F32)).astype(BF)
         near = self.send(tx, mx, ahead)
-        yield 6.0
+        yield 8.23
         plain.wait_recv()
         near.wait_recv()
         sx[...] = (wo[:, x].astype(F32) + px[...].astype(F32) + mx[...].astype(F32)).astype(BF)
         z_far = self.send(sx.at[self.z_at(2)], tz, z_ahead)
         z_plain = self.send(sx.at[zm], pz, z_back)
-        yield 5.0
+        yield 13.72
         z_far.wait_recv()
         tz[...] = (tz[...].astype(F32) + sx[self.z_at(e)].astype(F32)).astype(BF)
         z_near = self.send(tz, mz, z_ahead)
-        yield 5.0
+        yield 0.88
         z_plain.wait_recv()
         z_near.wait_recv()
         total = wo[zh, x].astype(F32) + px[zh].astype(F32) + mx[zh].astype(F32)
@@ -399,7 +399,7 @@
     net.step()
     gather_x = net.start(net.gather(xb))
     net.finish(bring)
-    net.until(gather_x, 7)
+    net.until(gather_x, 4)
     gather_g = net.start(net.gather(gb))
     net.finish(gather_x)
 
@@ -417,11 +417,11 @@
         return carry
 
     lax.fori_loop(0, 16, normalise, 0, unroll=2)
-    net.passed(2.2)
+    net.passed(0.14)
     for load in loads[3:]:
         load.wait()
     qkv[...] = mm(norm[...], wqkv[...]).astype(BF)
-    net.passed(1.2)
+    net.passed(1.7)
 
     scale = HEAD ** (-0.5)
     rows = lax.broadcasted_iota(jnp.int32, (256, 256), 0)
@@ -434,7 +434,7 @@
     probs[...] = soft
     attended = mm(soft.astype(BF), values)
     att[...] = attended.astype(BF)
-    net.passed(1.8)
+    net.passed(2.17)
 
     def out_term(i, carry):
         wide = mm(att[...], wout[:, pl.ds(pl.multiple_of(i * 256, 256), 256)]).astype(BF)
@@ -443,7 +443,7 @@
         return carry
 
     lax.fori_loop(0, 8, out_term, 0, unroll=4)
-    net.passed(1.0)
+    net.passed(0.19)
 
     att_t[...] = jnp.transpose(attended).astype(BF)
     probs_t[...] = jnp.transpose(soft).astype(BF)
@@ -475,7 +475,7 @@
     for i in range(8):
         total += mm_nt(pair_of(i), wout[:, pl.ds(i * 256, 256)])
     gheads[...] = total.astype(BF)
-    net.passed(2.5)
+    net.passed(0.82)
 
     dqkv[:, pl.ds(256, 128)] = mm(probs_t[...], gheads[...]).astype(BF)
     dprobs = mm_nt(gheads[...], qkv[:, pl.ds(256, 128)]).astype(BF).astype(F32)
@@ -533,7 +533,7 @@
         yield from net.scatter_sum(term2, rb2, zs2, zb2)
         total = net.received(term2, rb2, 1, net.zl) + zb2[...].astype(F32)
         while any(item[1] is sum_1 for item in net.flows):
-            yield 0.5
+            yield 6.43
         summed = net.received(term1, rb1, 1, net.zl) + zb1[...].astype(F32)
         local = flat(xb[mp]).astype(F32)
         done_both[:, :, 0] = (local + summed).astype(BF).reshape(4, 4, 16, HEAD)
@@ -548,7 +548,7 @@
             - local * (scale_own * scale_own * scale_own) * rows * (1.0 / 2048)
         )
         done_both[:, :, 1] = grad.astype(BF).reshape(4, 4, 16, HEAD)
-        yield 0.1
+        yield 0.14
         yield from net.patches_to_frames(done_both, back_mid, back_both)
         store(back_both.at[:, :, 0], lo_out)
         store(back_both.at[:, :, 1], ig_out)

time: 115 us -> 101 us (0.88)
  the two profiles are of different devices: /device:TPU:2 before, /device:TPU:8 now
where the time goes in v7:
time: 101 us
  Pallas kernels  94.7 us (94%)
  local copies, waits for them, and re-layouts  5.26 us (5%)
    pallas_call x1, Pallas kernels, shards(): pl.pallas_call(kernel, out_shape=(jax.ShapeDtypeStruct(block, BF), jax.Sh...  94.7 us
    unnamed x6, local copies, waits for them, and re-layouts  5.26 us

profile of v7, /device:TPU:8, one launch (start us, length us, event | category | flops | bytes accessed | tf_op | source)
XLA Modules:
  0.0 100.6 jit_solution(11306320826793018643)
XLA Ops:
  0.6 0.0 copy-start
  0.6 0.7 copy-done
  1.3 94.7 %sublayer.1 = (bf16[4,4,16,128]{3,2,1,0:T(8,128)(2,1)S(1)}, bf16[4,4,16,128]{3,2,1,0:T(8,128)(2,1)S(1)}, bf16[4,4,128,384]{3,2,1,0:T(8,128)(2,1)}, bf16[128,128]{1,0:T(8,128)(2,1)S(1)}) custom-call(bf16[4,4,16,128]{3,2,1,0:T(8,128)(2,1)} %bitcast.10, bf16[16,128]{1,0:T(8,128)(2,1)S(1)} %bitcast.8, bf16[2048,384]{1,0:T(8,128)(2,1)} %wqkv_hbm.1, ...), custom_call_target="tpu_custom_call" | custom-call | tf_op jit(solution)/shard_map/sublayer/pallas_call | solution.py:598
  96.0 0.6 copy.13
  96.6 0.6 copy.14
  97.3 2.7 %copy.15 = bf16[2048,384]{1,0:T(8,128)(2,1)} copy(bf16[2048,384]{1,0:T(8,128)(2,1)} %bitcast.9) | data formatting | bytes 3145728
  100.0 0.6 copy.16
Async XLA Ops:
  0.6 0.7 copy-start

commit v8 on v7

--- a/solution.py
+++ b/solution.py
@@ -31,6 +31,7 @@
 class Net:
     def __init__(self, ssem, rsem):
         self.ssem, self.rsem, self.started, self.flows, self.clock, self.steps = ssem, rsem, [], [], 0.0, {}
+        self.drained = 0
         clip, seq, mp = lax.axis_index("clip"), lax.axis_index("seq"), lax.axis_index("mp")
         self.clip, self.seq, self.mp = clip, seq, mp
         self.zh, self.x = seq // 4, seq & 3
@@ -84,6 +85,10 @@
 
     def step(self, item=None):
         item = item or min(self.flows, key=lambda entry: entry[0])
+        for _ in range(2):
+            if self.drained < len(self.started) - 24:
+                self.started[self.drained].wait_send()
+                self.drained += 1
         self.clock = max(self.clock, item[0])
         wait = next(item[1], None)
         self.steps[id(item[1])] = self.steps.get(id(item[1]), 0) + 1
@@ -107,7 +112,7 @@
         self.clock = target
 
     def close(self):
-        for copy in self.started:
+        for copy in self.started[self.drained :]:
             copy.wait_send()
 
     def frames_to_patches(self, src, mid, xb, gb):
@@ -117,7 +122,7 @@
             to = self.x_at(s)
             sent.append(self.send(src.at[:, to], mid.at[x], self.dev_x(to)))
         mid[x] = src[:, x]
-        yield 9.96
+        yield 7.15
         for copy in sent:
             copy.wait_recv()
         sent = []
@@ -127,7 +132,7 @@
                 sent.append(self.send(mid.at[:, to, half], dst.at[mp, zh], self.dev_z(to)))
             dst[mp, zh] = mid[:, zh, half]
         for some in (sent[:3], sent[3:]):
-            yield 2.2
+            yield 6.52
             for copy in some:
                 copy.wait_recv()
 
@@ -138,7 +143,7 @@
             to = self.z_at(s)
             sent.append(self.send(src.at[to], mid.at[zh], self.dev_z(to)))
         mid[zh] = src[zh]
-        yield 2.41
+        yield 27.35
         for copy in sent:
             copy.wait_recv()
         sent = []
@@ -146,7 +151,7 @@
             to = self.x_at(s)
             sent.append(self.send(mid.at[:, to], dst.at[:, x], self.dev_x(to)))
         dst[:, x] = mid[:, x]
-        yield 36.64
+        yield 1984.76
         for copy in sent:
             copy.wait_recv()
 
@@ -165,42 +170,42 @@
         a = pass_on(self.mp, ahead)
         b = pass_on(self.mp, back)
         pair = [pass_on(self.mp, self.dev_pair)]
-        yield 4.0
+        yield 3.68
         a.wait_recv()
         a = pass_on(own(-self.e), ahead)
-        yield 0.3
+        yield 0.51
         b.wait_recv()
         b = pass_on(own(self.e), back)
-        yield 0.42
+        yield 1.02
         pair[0].wait_recv()
         c = pass_on(other(0), ahead)
         d = pass_on(other(0), back)
-        yield 2.25
+        yield 2.08
         a.wait_recv()
         a = pass_on(own(-2 * self.e), ahead)
-        yield 0.62
+        yield 2.06
         b.wait_recv()
         b = pass_on(own(2 * self.e), back)
         pair.append(pass_on(own(2 * self.e), self.dev_pair))
-        yield 0.31
+        yield 0.71
         c.wait_recv()
         c = pass_on(other(-self.e), ahead)
-        yield 0.92
+        yield 0.45
         d.wait_recv()
-        yield 1.75
+        yield 0.94
         a.wait_recv()
         a = pass_on(own(-3 * self.e), ahead)
         pair.append(pass_on(own(-3 * self.e), self.dev_pair))
-        yield 0.89
+        yield 0.38
         b.wait_recv()
         pair.append(pass_on(own(3 * self.e), self.dev_pair))
-        yield 0.4
+        yield 2.71
         c.wait_recv()
-        yield 2.5
+        yield 0.3
         a.wait_recv()
         pair.append(pass_on(own(-4 * self.e), self.dev_pair))
         for copy in pair[1:]:
-            yield 1.05
+            yield 1.54
             copy.wait_recv()
 
     def scatter_sum(self, term, rb, zs, zb):
@@ -222,7 +227,7 @@
                 way, steps = ways[j]
                 if k > steps:
                     continue
-                yield 5.6 if (i, j) == (0, 0) else 0.6
+                yield 5.6 if (i, j) == (0, 0) else 0.7
                 sent[i, j].wait_recv()
                 here = rb.at[slot(i, j, k)]
                 if k < steps:
@@ -233,7 +238,7 @@
                 elif k == 4 and i == 0:
                     fold(zs, self.received(term, rb, 0, self.zp))
                     last = self.send(zs, zb, self.dev_pair)
-        yield 2.2
+        yield 60.63
         last.wait_recv()
 
     def received(self, term, rb, i, plane):
@@ -259,31 +264,31 @@
             far.append(self.send(wg.at[q[i], self.x_at(2)], tx.at[i], ahead))
             plain.append(self.send(wg.at[q[i], xm], px.at[i], back))
             if i < 3:
-                yield 0.78
+                yield 0.38
         for i in range(4):
             yield 2.1
             far[i].wait_recv()
             tx[i] = (tx[i].astype(F32) + wg[q[i], xp].astype(F32)).astype(BF)
             near.append(self.send(tx.at[i], mx.at[i], ahead))
-        yield 2.0
+        yield 1.77
         plain[0].wait_recv()
         near[0].wait_recv()
         sx[0] = here(0).astype(BF)
         z_far = self.send(sx.at[0], tz, z_ahead)
         for i in (1, 2):
-            yield 1.26
+            yield 0.55
             plain[i].wait_recv()
             near[i].wait_recv()
         sx[1] = here(2).astype(BF)
         z_plain = self.send(sx.at[1], pz, z_back)
-        yield 1.2
+        yield 1.95
         z_far.wait_recv()
         tz[...] = (tz[...].astype(F32) + here(1)).astype(BF)
         z_near = self.send(tz, mz, z_ahead)
-        yield 3.56
+        yield 2.93
         plain[3].wait_recv()
         near[3].wait_recv()
-        yield 3.0
+        yield 4.72
         z_plain.wait_recv()
         z_near.wait_recv()
         total = (here(3) + pz[...].astype(F32) + mz[...].astype(F32)).astype(BF)
@@ -294,28 +299,28 @@
 
         up, down = pass_on(zh, x, z_ahead), pass_on(zh, x, z_back)
         first, second, third = [pass_on(zh, x, ahead)], [pass_on(zh, x, back)], []
-        yield 6.1
+        yield 12.46
         up.wait_recv()
         up = pass_on(zm, x, z_ahead)
         first.append(pass_on(zm, x, ahead))
         second.append(pass_on(zm, x, back))
-        yield 1.45
+        yield 9.17
         down.wait_recv()
         first.append(pass_on(q[1], x, ahead))
         second.append(pass_on(q[1], x, back))
-        yield 0.8
+        yield 0.39
         first[0].wait_recv()
         third.append(pass_on(zh, xm, ahead))
-        yield 0.98
+        yield 61.54
         up.wait_recv()
         first.append(pass_on(q[0], x, ahead))
         second.append(pass_on(q[0], x, back))
         for i, at in ((1, zm), (2, q[1]), (3, q[0])):
-            yield 0.15
+            yield 1.41
             first[i].wait_recv()
             third.append(pass_on(at, xm, ahead))
         for copy in second + third:
-            yield 2.59
+            yield 3.28
             copy.wait_recv()
         done()
 
@@ -326,21 +331,21 @@
         z_ahead, z_back = self.dev_z(self.z_at(e)), self.dev_z(zm)
         far = self.send(wo.at[:, self.x_at(2)], tx, ahead)
         plain = self.send(wo.at[:, xm], px, back)
-        yield 14.5
+        yield 14.21
         far.wait_recv()
         tx[...] = (tx[...].astype(F32) + wo[:, xp].astype(F32)).astype(BF)
         near = self.send(tx, mx, ahead)
-        yield 8.23
+        yield 9.55
         plain.wait_recv()
         near.wait_recv()
         sx[...] = (wo[:, x].astype(F32) + px[...].astype(F32) + mx[...].astype(F32)).astype(BF)
         z_far = self.send(sx.at[self.z_at(2)], tz, z_ahead)
         z_plain = self.send(sx.at[zm], pz, z_back)
-        yield 13.72
+        yield 1.99
         z_far.wait_recv()
         tz[...] = (tz[...].astype(F32) + sx[self.z_at(e)].astype(F32)).astype(BF)
         z_near = self.send(tz, mz, z_ahead)
-        yield 0.88
+        yield 47.05
         z_plain.wait_recv()
         z_near.wait_recv()
         total = wo[zh, x].astype(F32) + px[zh].astype(F32) + mx[zh].astype(F32)
@@ -399,7 +404,7 @@
     net.step()
     gather_x = net.start(net.gather(xb))
     net.finish(bring)
-    net.until(gather_x, 4)
+    net.until(gather_x, 1)
     gather_g = net.start(net.gather(gb))
     net.finish(gather_x)
 
@@ -417,11 +422,11 @@
         return carry
 
     lax.fori_loop(0, 16, normalise, 0, unroll=2)
-    net.passed(0.14)
+    net.passed(0.85)
     for load in loads[3:]:
         load.wait()
     qkv[...] = mm(norm[...], wqkv[...]).astype(BF)
-    net.passed(1.7)
+    net.passed(0.07)
 
     scale = HEAD ** (-0.5)
     rows = lax.broadcasted_iota(jnp.int32, (256, 256), 0)
@@ -434,7 +439,7 @@
     probs[...] = soft
     attended = mm(soft.astype(BF), values)
     att[...] = attended.astype(BF)
-    net.passed(2.17)
+    net.passed(1.58)
 
     def out_term(i, carry):
         wide = mm(att[...], wout[:, pl.ds(pl.multiple_of(i * 256, 256), 256)]).astype(BF)
@@ -443,7 +448,7 @@
         return carry
 
     lax.fori_loop(0, 8, out_term, 0, unroll=4)
-    net.passed(0.19)
+    net.passed(0.2)
 
     att_t[...] = jnp.transpose(attended).astype(BF)
     probs_t[...] = jnp.transpose(soft).astype(BF)
@@ -475,7 +480,7 @@
     for i in range(8):
         total += mm_nt(pair_of(i), wout[:, pl.ds(i * 256, 256)])
     gheads[...] = total.astype(BF)
-    net.passed(0.82)
+    net.passed(2.96)
 
     dqkv[:, pl.ds(256, 128)] = mm(probs_t[...], gheads[...]).astype(BF)
     dprobs = mm_nt(gheads[...], qkv[:, pl.ds(256, 128)]).astype(BF).astype(F32)
@@ -506,7 +511,7 @@
             store(res.at[:, :, c], dwqkv_out.at[:, :, :, pl.ds(c * 128, 128)])
 
     net.start(net.weight_sum(piece, wg, tx, px, mx, sx, tz, pz, mz, res, stored))
-    net.passed(1.0)
+    net.passed(0.78)
 
     def norm_term(i, total):
         tall = wqkv[pl.ds(pl.multiple_of(i * 256, 256), 256), :]
@@ -533,7 +538,7 @@
         yield from net.scatter_sum(term2, rb2, zs2, zb2)
         total = net.received(term2, rb2, 1, net.zl) + zb2[...].astype(F32)
         while any(item[1] is sum_1 for item in net.flows):
-            yield 6.43
+            yield 6.73
         summed = net.received(term1, rb1, 1, net.zl) + zb1[...].astype(F32)
         local = flat(xb[mp]).astype(F32)
         done_both[:, :, 0] = (local + summed).astype(BF).reshape(4, 4, 16, HEAD)
@@ -548,7 +553,7 @@
             - local * (scale_own * scale_own * scale_own) * rows * (1.0 / 2048)
         )
         done_both[:, :, 1] = grad.astype(BF).reshape(4, 4, 16, HEAD)
-        yield 0.14
+        yield 1.41
         yield from net.patches_to_frames(done_both, back_mid, back_both)
         store(back_both.at[:, :, 0], lo_out)
         store(back_both.at[:, :, 1], ig_out)

time: 101 us -> 100 us (0.990)
  no operation moved by 1% of the time
where the time goes in v8:
time: 100 us
  Pallas kernels  94.3 us (94%)
  local copies, waits for them, and re-layouts  5.26 us (5%)
    pallas_call x1, Pallas kernels, shards(): pl.pallas_call(kernel, out_shape=(jax.ShapeDtypeStruct(block, BF), jax.Sh...  94.3 us
    unnamed x6, local copies, waits for them, and re-layouts  5.26 us

profile of v8, /device:TPU:8, one launch (start us, length us, event | category | flops | bytes accessed | tf_op | source)
XLA Modules:
  0.0 100.2 jit_solution(17941384058897356770)
XLA Ops:
  0.6 0.0 copy-start
  0.6 0.7 copy-done
  1.3 94.3 %sublayer.1 = (bf16[4,4,16,128]{3,2,1,0:T(8,128)(2,1)S(1)}, bf16[4,4,16,128]{3,2,1,0:T(8,128)(2,1)S(1)}, bf16[4,4,128,384]{3,2,1,0:T(8,128)(2,1)}, bf16[128,128]{1,0:T(8,128)(2,1)S(1)}) custom-call(bf16[4,4,16,128]{3,2,1,0:T(8,128)(2,1)} %bitcast.10, bf16[16,128]{1,0:T(8,128)(2,1)S(1)} %bitcast.8, bf16[2048,384]{1,0:T(8,128)(2,1)} %wqkv_hbm.1, ...), custom_call_target="tpu_custom_call" | custom-call | tf_op jit(solution)/shard_map/sublayer/pallas_call | solution.py:603
  95.6 0.6 copy.13
  96.3 0.6 copy.14
  96.9 2.7 %copy.15 = bf16[2048,384]{1,0:T(8,128)(2,1)} copy(bf16[2048,384]{1,0:T(8,128)(2,1)} %bitcast.9) | data formatting | bytes 3145728
  99.6 0.6 copy.16
Async XLA Ops:
  0.6 0.7 copy-start

commit v9 on v8

--- a/solution.py
+++ b/solution.py
@@ -10,7 +10,7 @@
 BF = jnp.bfloat16
 F32 = jnp.float32
 MESH = pl.DeviceIdType.MESH
-COPIES = 112
+COPIES = 159
 ROWS = 288
 SCALE = HEAD ** (-0.5)
 NT = (((1,), (1,)), ((), ()))
@@ -40,8 +40,7 @@
         self.zp = 1 - self.zl
         self.dev_pair = (clip, seq, self.zp * 8 + self.y)
         barrier = pltpu.get_barrier_semaphore()
-        peers = [self.dev_x(self.x_at(s)) for s in (1, 2, 3)]
-        peers += [self.dev_z(self.z_at(s)) for s in (1, 2, 3)]
+        peers = [(clip, (seq + s) & 15, mp) for s in range(1, 16)]
         peers += [self.dev_y(self.y_at(s)) for s in (1, -1, 2, -2)] + [self.dev_pair]
         for peer in peers:
             pl.semaphore_signal(barrier, inc=1, device_id=peer, device_id_type=MESH)
@@ -118,42 +117,30 @@
     def frames_to_patches(self, src, mid, xb, gb):
         zh, x, mp = self.zh, self.x, self.mp
         sent = []
-        for s in (1, 3, 2):
-            to = self.x_at(s)
-            sent.append(self.send(src.at[:, to], mid.at[x], self.dev_x(to)))
-        mid[x] = src[:, x]
-        yield 7.15
+        for s in range(1, 16):
+            to = (self.seq + s) & 15
+            there = (self.clip, to, mp)
+            sent.append(self.send(src.at[to // 4, to & 3], mid.at[zh, x], there))
+        mid[zh, x] = src[zh, x]
+        yield 2.99
         for copy in sent:
             copy.wait_recv()
+        xb[mp] = mid[:, :, 0]
+        gb[mp] = mid[:, :, 1]
+
+    def patches_to_frames(self, src, dst):
         sent = []
-        for half, dst in ((0, xb), (1, gb)):
-            for s in (1, 3, 2):
-                to = self.z_at(s)
-                sent.append(self.send(mid.at[:, to, half], dst.at[mp, zh], self.dev_z(to)))
-            dst[mp, zh] = mid[:, zh, half]
-        for some in (sent[:3], sent[3:]):
-            yield 6.52
-            for copy in some:
-                copy.wait_recv()
-
-    def patches_to_frames(self, src, mid, dst):
-        zh, x = self.zh, self.x
-        sent = []
-        for s in (1, 3, 2):
-            to = self.z_at(s)
-            sent.append(self.send(src.at[to], mid.at[zh], self.dev_z(to)))
-        mid[zh] = src[zh]
-        yield 27.35
+        for s in range(1, 16):
+            to = (self.seq + s) & 15
+            there = self.dev_far(to)
+            sent.append(self.send(src.at[to // 4, to & 3], dst.at[self.zh, self.x], there))
+        dst[self.zh, self.x] = src[self.zh, self.x]
+        yield 71.26
         for copy in sent:
             copy.wait_recv()
-        sent = []
-        for s in (1, 3, 2):
-            to = self.x_at(s)
-            sent.append(self.send(mid.at[:, to], dst.at[:, x], self.dev_x(to)))
-        dst[:, x] = mid[:, x]
-        yield 1984.76
-        for copy in sent:
-            copy.wait_recv()
+
+    def dev_far(self, seq):
+        return (self.clip, seq, self.mp)
 
     def gather(self, buf):
         def pass_on(block, device):
@@ -170,38 +157,38 @@
         a = pass_on(self.mp, ahead)
         b = pass_on(self.mp, back)
         pair = [pass_on(self.mp, self.dev_pair)]
-        yield 3.68
+        yield 3.61
         a.wait_recv()
         a = pass_on(own(-self.e), ahead)
-        yield 0.51
+        yield 2.72
         b.wait_recv()
         b = pass_on(own(self.e), back)
-        yield 1.02
+        yield 0.5
         pair[0].wait_recv()
         c = pass_on(other(0), ahead)
         d = pass_on(other(0), back)
-        yield 2.08
+        yield 1.77
         a.wait_recv()
         a = pass_on(own(-2 * self.e), ahead)
-        yield 2.06
+        yield 1.94
         b.wait_recv()
         b = pass_on(own(2 * self.e), back)
         pair.append(pass_on(own(2 * self.e), self.dev_pair))
-        yield 0.71
+        yield 0.06
         c.wait_recv()
         c = pass_on(other(-self.e), ahead)
-        yield 0.45
+        yield 1.11
         d.wait_recv()
-        yield 0.94
+        yield 1.01
         a.wait_recv()
         a = pass_on(own(-3 * self.e), ahead)
         pair.append(pass_on(own(-3 * self.e), self.dev_pair))
-        yield 0.38
+        yield 0.84
         b.wait_recv()
         pair.append(pass_on(own(3 * self.e), self.dev_pair))
-        yield 2.71
+        yield 2.24
         c.wait_recv()
-        yield 0.3
+        yield 0.05
         a.wait_recv()
         pair.append(pass_on(own(-4 * self.e), self.dev_pair))
         for copy in pair[1:]:
@@ -227,7 +214,7 @@
                 way, steps = ways[j]
                 if k > steps:
                     continue
-                yield 5.6 if (i, j) == (0, 0) else 0.7
+                yield 5.6 if (i, j) == (0, 0) else 0.99
                 sent[i, j].wait_recv()
                 here = rb.at[slot(i, j, k)]
                 if k < steps:
@@ -238,7 +225,7 @@
                 elif k == 4 and i == 0:
                     fold(zs, self.received(term, rb, 0, self.zp))
                     last = self.send(zs, zb, self.dev_pair)
-        yield 60.63
+        yield 30.06
         last.wait_recv()
 
     def received(self, term, rb, i, plane):
@@ -264,31 +251,31 @@
             far.append(self.send(wg.at[q[i], self.x_at(2)], tx.at[i], ahead))
             plain.append(self.send(wg.at[q[i], xm], px.at[i], back))
             if i < 3:
-                yield 0.38
+                yield 0.73
         for i in range(4):
-            yield 2.1
+            yield 1.97
             far[i].wait_recv()
             tx[i] = (tx[i].astype(F32) + wg[q[i], xp].astype(F32)).astype(BF)
             near.append(self.send(tx.at[i], mx.at[i], ahead))
-        yield 1.77
+        yield 1.86
         plain[0].wait_recv()
         near[0].wait_recv()
         sx[0] = here(0).astype(BF)
         z_far = self.send(sx.at[0], tz, z_ahead)
         for i in (1, 2):
-            yield 0.55
+            yield 1.82
             plain[i].wait_recv()
             near[i].wait_recv()
         sx[1] = here(2).astype(BF)
         z_plain = self.send(sx.at[1], pz, z_back)
-        yield 1.95
+        yield 1.67
         z_far.wait_recv()
         tz[...] = (tz[...].astype(F32) + here(1)).astype(BF)
         z_near = self.send(tz, mz, z_ahead)
         yield 2.93
         plain[3].wait_recv()
         near[3].wait_recv()
-        yield 4.72
+        yield 3.8
         z_plain.wait_recv()
         z_near.wait_recv()
         total = (here(3) + pz[...].astype(F32) + mz[...].astype(F32)).astype(BF)
@@ -299,16 +286,16 @@
 
         up, down = pass_on(zh, x, z_ahead), pass_on(zh, x, z_back)
         first, second, third = [pass_on(zh, x, ahead)], [pass_on(zh, x, back)], []
-        yield 12.46
+        yield 8.72
         up.wait_recv()
         up = pass_on(zm, x, z_ahead)
         first.append(pass_on(zm, x, ahead))
         second.append(pass_on(zm, x, back))
-        yield 9.17
+        yield 0.23
         down.wait_recv()
         first.append(pass_on(q[1], x, ahead))
         second.append(pass_on(q[1], x, back))
-        yield 0.39
+        yield 8.0
         first[0].wait_recv()
         third.append(pass_on(zh, xm, ahead))
         yield 61.54
@@ -316,11 +303,11 @@
         first.append(pass_on(q[0], x, ahead))
         second.append(pass_on(q[0], x, back))
         for i, at in ((1, zm), (2, q[1]), (3, q[0])):
-            yield 1.41
+            yield 3.2
             first[i].wait_recv()
             third.append(pass_on(at, xm, ahead))
         for copy in second + third:
-            yield 3.28
+            yield 47.18
             copy.wait_recv()
         done()
 
@@ -331,21 +318,21 @@
         z_ahead, z_back = self.dev_z(self.z_at(e)), self.dev_z(zm)
         far = self.send(wo.at[:, self.x_at(2)], tx, ahead)
         plain = self.send(wo.at[:, xm], px, back)
-        yield 14.21
+        yield 20.24
         far.wait_recv()
         tx[...] = (tx[...].astype(F32) + wo[:, xp].astype(F32)).astype(BF)
         near = self.send(tx, mx, ahead)
-        yield 9.55
+        yield 23.11
         plain.wait_recv()
         near.wait_recv()
         sx[...] = (wo[:, x].astype(F32) + px[...].astype(F32) + mx[...].astype(F32)).astype(BF)
         z_far = self.send(sx.at[self.z_at(2)], tz, z_ahead)
         z_plain = self.send(sx.at[zm], pz, z_back)
-        yield 1.99
+        yield 70.29
         z_far.wait_recv()
         tz[...] = (tz[...].astype(F32) + sx[self.z_at(e)].astype(F32)).astype(BF)
         z_near = self.send(tz, mz, z_ahead)
-        yield 47.05
+        yield 3.93
         z_plain.wait_recv()
         z_near.wait_recv()
         total = wo[zh, x].astype(F32) + px[zh].astype(F32) + mx[zh].astype(F32)
@@ -370,7 +357,8 @@
     lo_out, ig_out, dwqkv_out, dwo_out,
     both, mid, gain_ref, xb, gb, wqkv, wout, gain, inv, norm, norm_t, qkv, att, att_t,
     probs, probs_t, gheads, dqkv, term1, rb1, zs1, zb1, term2, rb2, zs2, zb2,
-    wg, tx, px, mx, sx, tz, pz, mz, wo, txo, pxo, mxo, sxo, tzo, pzo, mzo, res, dwo, done_both, back_mid, back_both,
+    wv, txv, pxv, mxv, sxv, tzv, pzv, mzv, resv,
+    wg, tx, px, mx, sx, tz, pz, mz, wo, txo, pxo, mxo, sxo, tzo, pzo, mzo, res, dwo, done_both, back_both,
     ssem, rsem, lsem,
 ):
     loads = [
@@ -400,11 +388,9 @@
         load.wait()
     bring = net.start(net.frames_to_patches(both, mid, xb, gb))
     gain[...] = gain_ref[...].astype(F32)
-    net.step()
-    net.step()
+    net.finish(bring)
     gather_x = net.start(net.gather(xb))
-    net.finish(bring)
-    net.until(gather_x, 1)
+    net.until(gather_x, 2)
     gather_g = net.start(net.gather(gb))
     net.finish(gather_x)
 
@@ -422,11 +408,11 @@
         return carry
 
     lax.fori_loop(0, 16, normalise, 0, unroll=2)
-    net.passed(0.85)
+    net.passed(0.25)
     for load in loads[3:]:
         load.wait()
     qkv[...] = mm(norm[...], wqkv[...]).astype(BF)
-    net.passed(0.07)
+    net.passed(0.46)
 
     scale = HEAD ** (-0.5)
     rows = lax.broadcasted_iota(jnp.int32, (256, 256), 0)
@@ -439,7 +425,7 @@
     probs[...] = soft
     attended = mm(soft.astype(BF), values)
     att[...] = attended.astype(BF)
-    net.passed(1.58)
+    net.passed(0.19)
 
     def out_term(i, carry):
         wide = mm(att[...], wout[:, pl.ds(pl.multiple_of(i * 256, 256), 256)]).astype(BF)
@@ -448,7 +434,7 @@
         return carry
 
     lax.fori_loop(0, 8, out_term, 0, unroll=4)
-    net.passed(0.2)
+    net.passed(0.05)
 
     att_t[...] = jnp.transpose(attended).astype(BF)
     probs_t[...] = jnp.transpose(soft).astype(BF)
@@ -480,9 +466,32 @@
     for i in range(8):
         total += mm_nt(pair_of(i), wout[:, pl.ds(i * 256, 256)])
     gheads[...] = total.astype(BF)
-    net.passed(2.96)
+    net.passed(2.87)
+
+    def pieces(wg, first, count):
+        def piece(q):
+            for half in range(2):
+                at = q * 4 + half * 2
+                rows = norm_t[pl.ds(pl.multiple_of(at * 128, 256), 256), :]
+                tall = mm(rows, dqkv[:, pl.ds(first * 128, count * 128)]).astype(BF)
+                for k in range(2):
+                    for c in range(count):
+                        wg[q, 2 * half + k, c] = tall[k * 128 : k * 128 + 128, c * 128 : c * 128 + 128]
+
+        return piece
+
+    def stored(res, first, count):
+        def store_all():
+            for c in range(count):
+                store(res.at[:, :, c], dwqkv_out.at[:, :, :, pl.ds((first + c) * 128, 128)])
+
+        return store_all
 
     dqkv[:, pl.ds(256, 128)] = mm(probs_t[...], gheads[...]).astype(BF)
+    net.start(
+        net.weight_sum(pieces(wv, 2, 1), wv, txv, pxv, mxv, sxv, tzv, pzv, mzv, resv, stored(resv, 2, 1))
+    )
+    net.passed(0.26)
     dprobs = mm_nt(gheads[...], qkv[:, pl.ds(256, 128)]).astype(BF).astype(F32)
     soft = probs[...]
     delta = jnp.sum(soft * dprobs, axis=-1, keepdims=True)
@@ -497,21 +506,8 @@
     queries = qkv[:, pl.ds(0, 128)]
     dqkv[:, pl.ds(128, 128)] = (mm(high, queries) + mm(low, queries)).astype(BF)
 
-    def piece(q):
-        for half in range(2):
-            at = q * 4 + half * 2
-            rows = norm_t[pl.ds(pl.multiple_of(at * 128, 256), 256), :]
-            tall = mm(rows, dqkv[...]).astype(BF)
-            for k in range(2):
-                for c in range(3):
-                    wg[q, 2 * half + k, c] = tall[k * 128 : k * 128 + 128, c * 128 : c * 128 + 128]
-
-    def stored():
-        for c in range(3):
-            store(res.at[:, :, c], dwqkv_out.at[:, :, :, pl.ds(c * 128, 128)])
-
-    net.start(net.weight_sum(piece, wg, tx, px, mx, sx, tz, pz, mz, res, stored))
-    net.passed(0.78)
+    net.start(net.weight_sum(pieces(wg, 0, 2), wg, tx, px, mx, sx, tz, pz, mz, res, stored(res, 0, 2)))
+    net.passed(1.18)
 
     def norm_term(i, total):
         tall = wqkv[pl.ds(pl.multiple_of(i * 256, 256), 256), :]
@@ -538,7 +534,7 @@
         yield from net.scatter_sum(term2, rb2, zs2, zb2)
         total = net.received(term2, rb2, 1, net.zl) + zb2[...].astype(F32)
         while any(item[1] is sum_1 for item in net.flows):
-            yield 6.73
+            yield 217.08
         summed = net.received(term1, rb1, 1, net.zl) + zb1[...].astype(F32)
         local = flat(xb[mp]).astype(F32)
         done_both[:, :, 0] = (local + summed).astype(BF).reshape(4, 4, 16, HEAD)
@@ -553,8 +549,8 @@
             - local * (scale_own * scale_own * scale_own) * rows * (1.0 / 2048)
         )
         done_both[:, :, 1] = grad.astype(BF).reshape(4, 4, 16, HEAD)
-        yield 1.41
-        yield from net.patches_to_frames(done_both, back_mid, back_both)
+        yield 0.82
+        yield from net.patches_to_frames(done_both, back_both)
         store(back_both.at[:, :, 0], lo_out)
         store(back_both.at[:, :, 1], ig_out)
 
@@ -587,15 +583,20 @@
         bf(256, HEAD), bf(256, 384),
         bf(16, 256, HEAD), bf(14, 256, HEAD), bf(256, HEAD), bf(256, HEAD),
         bf(16, ROWS, HEAD), bf(14, ROWS, HEAD), bf(ROWS, HEAD), bf(ROWS, HEAD),
-        bf(4, 4, 3, HEAD, HEAD),
-        bf(4, 3, HEAD, HEAD), bf(4, 3, HEAD, HEAD), bf(4, 3, HEAD, HEAD),
-        bf(2, 3, HEAD, HEAD),
-        bf(3, HEAD, HEAD), bf(3, HEAD, HEAD), bf(3, HEAD, HEAD),
+        bf(4, 4, 1, HEAD, HEAD),
+        bf(4, 1, HEAD, HEAD), bf(4, 1, HEAD, HEAD), bf(4, 1, HEAD, HEAD),
+        bf(2, 1, HEAD, HEAD),
+        bf(1, HEAD, HEAD), bf(1, HEAD, HEAD), bf(1, HEAD, HEAD),
+        bf(4, 4, 1, HEAD, HEAD),
+        bf(4, 4, 2, HEAD, HEAD),
+        bf(4, 2, HEAD, HEAD), bf(4, 2, HEAD, HEAD), bf(4, 2, HEAD, HEAD),
+        bf(2, 2, HEAD, HEAD),
+        bf(2, HEAD, HEAD), bf(2, HEAD, HEAD), bf(2, HEAD, HEAD),
         bf(4, 4, HEAD, HEAD), bf(4, HEAD, HEAD), bf(4, HEAD, HEAD),
         bf(4, HEAD, HEAD), bf(4, HEAD, HEAD),
         bf(HEAD, HEAD), bf(HEAD, HEAD), bf(HEAD, HEAD),
-        bf(4, 4, 3, HEAD, HEAD), bf(HEAD, HEAD),
-        bf(4, 4, 2, 16, HEAD), bf(4, 4, 2, 16, HEAD), bf(4, 4, 2, 16, HEAD),
+        bf(4, 4, 2, HEAD, HEAD), bf(HEAD, HEAD),
+        bf(4, 4, 2, 16, HEAD), bf(4, 4, 2, 16, HEAD),
         pltpu.SemaphoreType.DMA((COPIES,)),
         pltpu.SemaphoreType.DMA((COPIES,)),
         pltpu.SemaphoreType.DMA((11,)),

time: 100 us -> 96.2 us (0.962)
  Pallas kernels: 94.3 us -> 90.1 us
    pallas_call x1, Pallas kernels: 94.3 us -> 90.1 us  [shards(): pl.pallas_call(kernel, out_shape=(jax.ShapeDtypeStruct(block, BF), jax.Sh...]
where the time goes in v9:
time: 96.2 us; the launch traced here: 96 us
  Pallas kernels  90.1 us (94%)
  local copies, waits for them, and re-layouts  5.26 us (5%)
    pallas_call x1, Pallas kernels, shards(): pl.pallas_call(kernel, out_shape=(jax.ShapeDtypeStruct(block, BF), jax.Sh...  90.1 us
    unnamed x6, local copies, waits for them, and re-layouts  5.26 us

profile of v9, /device:TPU:8, one launch (start us, length us, event | category | flops | bytes accessed | tf_op | source)
XLA Modules:
  0.0 96.0 jit_solution(5216405077349373642)
XLA Ops:
  0.6 0.0 copy-start
  0.6 0.7 copy-done
  1.3 90.1 %sublayer.1 = (bf16[4,4,16,128]{3,2,1,0:T(8,128)(2,1)S(1)}, bf16[4,4,16,128]{3,2,1,0:T(8,128)(2,1)S(1)}, bf16[4,4,128,384]{3,2,1,0:T(8,128)(2,1)}, bf16[128,128]{1,0:T(8,128)(2,1)S(1)}) custom-call(bf16[4,4,16,128]{3,2,1,0:T(8,128)(2,1)} %bitcast.10, bf16[16,128]{1,0:T(8,128)(2,1)S(1)} %bitcast.8, bf16[2048,384]{1,0:T(8,128)(2,1)} %wqkv_hbm.1, ...), custom_call_target="tpu_custom_call" | custom-call | tf_op jit(solution)/shard_map/sublayer/pallas_call | solution.py:604
  91.4 0.6 copy.13
  92.1 0.6 copy.14
  92.7 2.7 %copy.15 = bf16[2048,384]{1,0:T(8,128)(2,1)} copy(bf16[2048,384]{1,0:T(8,128)(2,1)} %bitcast.9) | data formatting | bytes 3145728
  95.4 0.6 copy.16
Async XLA Ops:
  0.6 0.7 copy-start

commit v10 on v9

--- a/solution.py
+++ b/solution.py
@@ -122,7 +122,7 @@
             there = (self.clip, to, mp)
             sent.append(self.send(src.at[to // 4, to & 3], mid.at[zh, x], there))
         mid[zh, x] = src[zh, x]
-        yield 2.99
+        yield 17.64
         for copy in sent:
             copy.wait_recv()
         xb[mp] = mid[:, :, 0]
@@ -135,7 +135,7 @@
             there = self.dev_far(to)
             sent.append(self.send(src.at[to // 4, to & 3], dst.at[self.zh, self.x], there))
         dst[self.zh, self.x] = src[self.zh, self.x]
-        yield 71.26
+        yield 252.77
         for copy in sent:
             copy.wait_recv()
 
@@ -163,30 +163,30 @@
         yield 2.72
         b.wait_recv()
         b = pass_on(own(self.e), back)
-        yield 0.5
+        yield 1.5
         pair[0].wait_recv()
         c = pass_on(other(0), ahead)
         d = pass_on(other(0), back)
-        yield 1.77
+        yield 1.22
         a.wait_recv()
         a = pass_on(own(-2 * self.e), ahead)
         yield 1.94
         b.wait_recv()
         b = pass_on(own(2 * self.e), back)
         pair.append(pass_on(own(2 * self.e), self.dev_pair))
-        yield 0.06
+        yield 0.58
         c.wait_recv()
         c = pass_on(other(-self.e), ahead)
         yield 1.11
         d.wait_recv()
-        yield 1.01
+        yield 0.74
         a.wait_recv()
         a = pass_on(own(-3 * self.e), ahead)
         pair.append(pass_on(own(-3 * self.e), self.dev_pair))
-        yield 0.84
+        yield 1.18
         b.wait_recv()
         pair.append(pass_on(own(3 * self.e), self.dev_pair))
-        yield 2.24
+        yield 1.54
         c.wait_recv()
         yield 0.05
         a.wait_recv()
@@ -225,7 +225,7 @@
                 elif k == 4 and i == 0:
                     fold(zs, self.received(term, rb, 0, self.zp))
                     last = self.send(zs, zb, self.dev_pair)
-        yield 30.06
+        yield 25.36
         last.wait_recv()
 
     def received(self, term, rb, i, plane):
@@ -291,7 +291,7 @@
         up = pass_on(zm, x, z_ahead)
         first.append(pass_on(zm, x, ahead))
         second.append(pass_on(zm, x, back))
-        yield 0.23
+        yield 0.05
         down.wait_recv()
         first.append(pass_on(q[1], x, ahead))
         second.append(pass_on(q[1], x, back))
@@ -307,7 +307,7 @@
             first[i].wait_recv()
             third.append(pass_on(at, xm, ahead))
         for copy in second + third:
-            yield 47.18
+            yield 46.94
             copy.wait_recv()
         done()
 
@@ -332,7 +332,7 @@
         z_far.wait_recv()
         tz[...] = (tz[...].astype(F32) + sx[self.z_at(e)].astype(F32)).astype(BF)
         z_near = self.send(tz, mz, z_ahead)
-        yield 3.93
+        yield 3.59
         z_plain.wait_recv()
         z_near.wait_recv()
         total = wo[zh, x].astype(F32) + px[zh].astype(F32) + mx[zh].astype(F32)
@@ -408,11 +408,11 @@
         return carry
 
     lax.fori_loop(0, 16, normalise, 0, unroll=2)
-    net.passed(0.25)
+    net.passed(1.02)
     for load in loads[3:]:
         load.wait()
     qkv[...] = mm(norm[...], wqkv[...]).astype(BF)
-    net.passed(0.46)
+    net.passed(0.71)
 
     scale = HEAD ** (-0.5)
     rows = lax.broadcasted_iota(jnp.int32, (256, 256), 0)
@@ -425,7 +425,7 @@
     probs[...] = soft
     attended = mm(soft.astype(BF), values)
     att[...] = attended.astype(BF)
-    net.passed(0.19)
+    net.passed(1.4)
 
     def out_term(i, carry):
         wide = mm(att[...], wout[:, pl.ds(pl.multiple_of(i * 256, 256), 256)]).astype(BF)
@@ -434,7 +434,7 @@
         return carry
 
     lax.fori_loop(0, 8, out_term, 0, unroll=4)
-    net.passed(0.05)
+    net.passed(0.57)
 
     att_t[...] = jnp.transpose(attended).astype(BF)
     probs_t[...] = jnp.transpose(soft).astype(BF)
@@ -534,7 +534,7 @@
         yield from net.scatter_sum(term2, rb2, zs2, zb2)
         total = net.received(term2, rb2, 1, net.zl) + zb2[...].astype(F32)
         while any(item[1] is sum_1 for item in net.flows):
-            yield 217.08
+            yield 6.77
         summed = net.received(term1, rb1, 1, net.zl) + zb1[...].astype(F32)
         local = flat(xb[mp]).astype(F32)
         done_both[:, :, 0] = (local + summed).astype(BF).reshape(4, 4, 16, HEAD)
@@ -549,7 +549,7 @@
             - local * (scale_own * scale_own * scale_own) * rows * (1.0 / 2048)
         )
         done_both[:, :, 1] = grad.astype(BF).reshape(4, 4, 16, HEAD)
-        yield 0.82
+        yield 20.22
         yield from net.patches_to_frames(done_both, back_both)
         store(back_both.at[:, :, 0], lo_out)
         store(back_both.at[:, :, 1], ig_out)

time: 96.2 us -> 96.1 us (level)
  no operation moved by 1% of the time
where the time goes in v10:
time: 96.1 us; the launch traced here: 96 us
  Pallas kernels  90 us (94%)
  local copies, waits for them, and re-layouts  5.26 us (5%)
    pallas_call x1, Pallas kernels, shards(): pl.pallas_call(kernel, out_shape=(jax.ShapeDtypeStruct(block, BF), jax.Sh...  90 us
    unnamed x6, local copies, waits for them, and re-layouts  5.26 us

profile of v10, /device:TPU:8, one launch (start us, length us, event | category | flops | bytes accessed | tf_op | source)
XLA Modules:
  0.0 96.0 jit_solution(5308110094579332995)
XLA Ops:
  0.6 0.0 copy-start
  0.6 0.7 copy-done
  1.3 90.0 %sublayer.1 = (bf16[4,4,16,128]{3,2,1,0:T(8,128)(2,1)S(1)}, bf16[4,4,16,128]{3,2,1,0:T(8,128)(2,1)S(1)}, bf16[4,4,128,384]{3,2,1,0:T(8,128)(2,1)}, bf16[128,128]{1,0:T(8,128)(2,1)S(1)}) custom-call(bf16[4,4,16,128]{3,2,1,0:T(8,128)(2,1)} %bitcast.10, bf16[16,128]{1,0:T(8,128)(2,1)S(1)} %bitcast.8, bf16[2048,384]{1,0:T(8,128)(2,1)} %wqkv_hbm.1, ...), custom_call_target="tpu_custom_call" | custom-call | tf_op jit(solution)/shard_map/sublayer/pallas_call | solution.py:604
  91.4 0.6 copy.13
  92.0 0.6 copy.14
  92.6 2.7 %copy.15 = bf16[2048,384]{1,0:T(8,128)(2,1)} copy(bf16[2048,384]{1,0:T(8,128)(2,1)} %bitcast.9) | data formatting | bytes 3145728
  95.3 0.6 copy.16
Async XLA Ops:
  0.6 0.7 copy-start
